TPU v7x, 32 devices: a whole 2x2x4 slice. The times are simulated.
32 devices in a mesh: dp: 2 (over y), row: 4 (over x, core), col: 4 (over z).
Axes of the slice: x: 2, y: 2, z: 4, core: 2. Of those that a mesh axis runs over, the one named last changes fastest.
Arguments:
- hidden_in: bfloat16 [8192, 1536], P(('dp', 'row', 'col')), may hold values from -6 to 6
- norm_gain_attn: float32 [1536], replicated, may hold values from 0.1 to 1.9
- norm_gain_moe: float32 [1536], replicated, may hold values from 0.1 to 1.9
- w_qkv: bfloat16 [1536, 2560], P(('dp', 'row'), 'col'), may hold values from -0.15625 to 0.15625
- w_out: bfloat16 [1536, 1536], P(('dp', 'row'), 'col'), may hold values from -1.25 to 1.25
- router: float32 [1536, 32], replicated, may hold values from -0.078125 to 0.078125
- w_in: bfloat16 [32, 1536, 1024], P(('row', 'col')), may hold values from -0.15625 to 0.15625
- w_down: bfloat16 [32, 512, 1536], P(('row', 'col')), may hold values from -1 to 1
- lengths: int32 [8, 8], P(('dp', 'row')), may hold values from 1 to 512, 1024 in all within a row
- routes: int32 [8192, 8], P(('dp', 'row', 'col')), may hold values from 0 to 31, all different within a row; in each aligned block of 256 rows (0 to 255, 256 to 511, ...) at most 128 rows name the same one
- out_grad: bfloat16 [8192, 1536], P(('dp', 'row', 'col')), may hold values from -6 to 6
Outputs:
- result: float32 [8192, 1536], P(('dp', 'row', 'col'))
- grad_hidden: float32 [8192, 1536], P(('dp', 'row', 'col'))
- grad_norm_attn: float32 [1536], replicated
- grad_norm_moe: float32 [1536], replicated
- grad_w_qkv: float32 [1536, 2560], P(('dp', 'row'), 'col')
- grad_w_out: float32 [1536, 1536], P(('dp', 'row'), 'col')
- grad_router: float32 [1536, 32], replicated
- grad_w_in: float32 [32, 1536, 1024], P(('row', 'col'))
- grad_w_down: float32 [32, 512, 1536], P(('row', 'col'))
Inputs may be any that keep to these rules, and one draw needn't show every extreme that they name: Each row holds the lengths of 8 packed sequences in order, summing to 1024; the longest is exactly 512. `routes`: each row names 8 different experts; among the 256 rows of one device no expert is named by more than 128 rows, a bound that some block reaches.
All inputs are finite; a program needn't handle non-finite values.
Results may differ from a plain program's by a relative error of at most 0.019.
Values may be sent and summed in bfloat16 or wider, within the bound.
No kernel may reach another device: no remote copies, remote signals or barrier semaphores. Data moves between devices by JAX's collectives and lax.ppermute only.
A program may use at most 256 MiB of HBM per device.

v0:
```python
import functools
import math

import jax
import jax.numpy as jnp
from jax import lax
from jax.sharding import PartitionSpec as P

HD = 64
FFE = 512
TOP = 8
REP = 3


EPSILON = 1e-06
HIGHEST = lax.Precision.HIGHEST
MASKED_SCORE = -1e30


def rope_tables(positions, head_dim):
    freq_index = jnp.arange(head_dim // 2, dtype=jnp.float32)
    inverse = jnp.exp(freq_index * (-2.0 * math.log(10000.0) / head_dim))
    angles = positions.astype(jnp.float32)[:, None] * inverse[None, :]
    angles = jnp.concatenate([angles, angles], axis=1)
    return (jnp.cos(angles), jnp.sin(angles))


def rotate(values, cos_table, sin_table):
    middle_dim = values.shape[-1] // 2
    turned = jnp.concatenate([-values[..., middle_dim:], values[..., :middle_dim]], axis=-1)
    cos_shape = (cos_table.shape[0],) + (1,) * (values.ndim - 2) + (cos_table.shape[1],)
    return values * cos_table.reshape(cos_shape) + turned * sin_table.reshape(cos_shape)


def seq_layout(block_lengths, block_tok):
    seq_ends = jnp.cumsum(block_lengths)
    starts = seq_ends - block_lengths
    places = jnp.arange(block_tok, dtype=jnp.int32)
    segment = jnp.sum((places[:, None] >= seq_ends[None, :]).astype(jnp.int32), axis=1)
    owners = segment[:, None] == jnp.arange(block_lengths.shape[0], dtype=jnp.int32)[None, :]
    offset = jnp.sum(jnp.where(owners, starts[None, :], 0), axis=1)
    return (places - offset, segment)


def norm_apply(row_vals, gain_vec):
    scale_row = lax.rsqrt(jnp.mean(row_vals * row_vals, axis=1, keepdims=True) + EPSILON)
    return row_vals * scale_row * gain_vec


def block_sizes(block_tok):
    q_block = min(512, block_tok)
    return (q_block, min(2 * q_block, block_tok))


def block_view(queries, key_rows, segment, block_index, score_scale):
    block_tok = queries.shape[0]
    q_block, key_span = block_sizes(block_tok)
    q_start = block_index * q_block
    k_start = jnp.clip(q_start - q_block, 0, block_tok - key_span)
    q_part = lax.dynamic_slice_in_dim(queries, q_start, q_block, 0)
    scores = (
        jnp.einsum("qgrd,kgd->grqk", q_part, key_rows, preferred_element_type=jnp.float32)
        * score_scale
    )
    q_places = q_start + jnp.arange(q_block, dtype=jnp.int32)
    k_places = k_start + jnp.arange(key_span, dtype=jnp.int32)
    q_seg = lax.dynamic_slice_in_dim(segment, q_start, q_block, 0)
    allowed = (q_seg[:, None] == segment[None, :]) & (q_places[:, None] >= k_places[None, :])
    return (jnp.where(allowed, scores, MASKED_SCORE), q_part, key_rows, q_start, k_start)


def add_rows(accumulated, term_rows):
    return accumulated + term_rows


def attend_forward(queries, key_rows, value_rows, segment, score_scale):
    block_tok = queries.shape[0]
    q_block, key_span = block_sizes(block_tok)

    def one_block(block_index):
        masked, q_part, k_part, q_start, k_start = block_view(
            queries, key_rows, segment, block_index, score_scale
        )
        row_max = jnp.max(masked, axis=3, keepdims=True)
        exp_terms = jnp.exp(masked - row_max)
        row_total = jnp.sum(exp_terms, axis=3, keepdims=True)
        soft_low = (exp_terms / row_total).astype(jnp.bfloat16)
        mixed_heads = jnp.einsum(
            "grqk,kgd->qgrd", soft_low, value_rows, preferred_element_type=jnp.float32
        )
        return (mixed_heads.astype(jnp.bfloat16), row_max + jnp.log(row_total))

    heads_out, log_sums = lax.map(one_block, jnp.arange(block_tok // q_block, dtype=jnp.int32))
    return (heads_out.reshape(block_tok, -1), log_sums)


def attend_backward(queries, key_rows, value_rows, segment, score_scale, log_sums, grad_heads):
    block_tok = queries.shape[0]
    q_block, key_span = block_sizes(block_tok)

    def one_block(accumulated, block_index):
        grad_keys, grad_values = accumulated
        masked, q_part, k_part, q_start, k_start = block_view(
            queries, key_rows, segment, block_index, score_scale
        )
        soft_w = jnp.exp(masked - log_sums[block_index])
        g_part = lax.dynamic_slice_in_dim(grad_heads, q_start, q_block, 0)
        grad_soft = jnp.einsum(
            "qgrd,kgd->grqk", g_part, value_rows, preferred_element_type=jnp.float32
        )
        value_term = jnp.einsum(
            "grqk,qgrd->kgd",
            soft_w.astype(jnp.bfloat16),
            g_part,
            preferred_element_type=jnp.float32,
        )
        inner_sum = jnp.sum(grad_soft * soft_w, axis=3, keepdims=True)
        grad_scores = (soft_w * (grad_soft - inner_sum)).astype(jnp.bfloat16)
        query_term = (
            jnp.einsum("grqk,kgd->qgrd", grad_scores, k_part, preferred_element_type=jnp.float32)
            * score_scale
        )
        key_term = (
            jnp.einsum("grqk,qgrd->kgd", grad_scores, q_part, preferred_element_type=jnp.float32)
            * score_scale
        )
        grad_keys = add_rows(grad_keys, key_term)
        grad_values = add_rows(grad_values, value_term)
        return ((grad_keys, grad_values), query_term)

    zero_rows = jnp.zeros(key_rows.shape, jnp.float32)
    totals, query_terms = lax.scan(
        one_block, (zero_rows, zero_rows), jnp.arange(block_tok // q_block, dtype=jnp.int32)
    )
    return (query_terms.reshape(queries.shape), totals[0], totals[1])


def swiglu(gate_up):
    return jax.nn.silu(gate_up[..., :FFE]) * gate_up[..., FFE:]


def shards(
    hidden_in,
    norm_gain_attn,
    norm_gain_moe,
    w_qkv,
    w_out,
    router,
    w_in,
    w_down,
    lengths,
    routes,
    out_grad,
):
    tok_dev, features = hidden_in.shape
    col_count = lax.axis_size("col")
    block_tok = tok_dev * col_count
    experts = router.shape[1]
    ep_count = lax.axis_size(("row", "col"))
    expert_local = w_in.shape[0]
    capacity = tok_dev * TOP * 2 // experts
    kv_local = w_qkv.shape[1] // ((REP + 2) * HD)
    score_scale = HD ** (-0.5)
    rows_in = hidden_in.astype(jnp.float32)

    def fetch_weights():
        return (
            lax.all_gather(w_qkv, ("dp", "row"), axis=0, tiled=True),
            lax.all_gather(w_out, ("dp", "row"), axis=0, tiled=True),
        )

    qkv_full, out_full = fetch_weights()
    normed_attn = norm_apply(rows_in, norm_gain_attn).astype(jnp.bfloat16)
    block_rows = lax.all_gather(normed_attn, "col", axis=0, tiled=True)
    mixed_cols = jnp.dot(block_rows, qkv_full, preferred_element_type=jnp.float32).reshape(
        block_tok, kv_local, (REP + 2) * HD
    )
    query_cols = mixed_cols[:, :, : REP * HD].reshape(block_tok, kv_local, REP, HD)
    key_cols = mixed_cols[:, :, REP * HD : (REP + 1) * HD]
    value_rows = mixed_cols[:, :, (REP + 1) * HD :].astype(jnp.bfloat16)
    positions, segment = seq_layout(lengths[0], block_tok)
    cos_table, sin_table = rope_tables(positions, HD)
    rotate_fixed = functools.partial(rotate, cos_table=cos_table, sin_table=sin_table)
    query_rows = rotate_fixed(query_cols).astype(jnp.bfloat16)
    key_rows = rotate_fixed(key_cols).astype(jnp.bfloat16)
    heads_low, log_sums = attend_forward(query_rows, key_rows, value_rows, segment, score_scale)
    part_rows = heads_low
    attn_out = lax.psum_scatter(
        lax.dot_general(
            part_rows, out_full, (((1,), (1,)), ((), ())), preferred_element_type=jnp.float32
        ),
        "col",
        scatter_dimension=0,
        tiled=True,
    )
    middle = rows_in + attn_out
    normed_moe = norm_apply(middle, norm_gain_moe).astype(jnp.bfloat16)
    normed_wide = normed_moe.astype(jnp.float32)
    logits = jnp.dot(normed_wide, router, precision=HIGHEST, preferred_element_type=jnp.float32)
    expert_ids = jnp.arange(experts, dtype=jnp.int32)
    picked = routes[:, :, None] == expert_ids[None, None, :]
    chosen = jnp.sum(jnp.where(picked, logits[:, None, :], 0.0), axis=2)
    gate_probs, gate_back = jax.vjp(functools.partial(jax.nn.softmax, axis=1), chosen)
    flat_ids = routes.reshape(-1)
    onehot = (flat_ids[:, None] == expert_ids[None, :]).astype(jnp.int32)
    before = jnp.cumsum(onehot, axis=0) - onehot
    target = flat_ids * capacity + jnp.sum(before * onehot, axis=1)
    entries = jnp.arange(tok_dev * TOP, dtype=jnp.int32)
    source = jnp.full((experts * capacity,), -1, jnp.int32).at[target].set(entries)
    filled = (source >= 0)[:, None]
    source_pair = jnp.maximum(source, 0)
    buffer_shape = (ep_count, expert_local, capacity, features)

    def pack_rows():
        return jnp.where(
            filled, normed_moe[source_pair // TOP], jnp.zeros((), jnp.bfloat16)
        ).reshape(buffer_shape)

    def expert_front(row_buf):
        return jnp.einsum("secd,edf->secf", row_buf, w_in, preferred_element_type=jnp.float32)

    arrived = lax.all_to_all(pack_rows(), ("row", "col"), split_axis=0, concat_axis=0, tiled=True)
    gate_up = expert_front(arrived)
    activated = swiglu(gate_up).astype(jnp.bfloat16)
    expert_out = jnp.einsum(
        "secf,efd->secd", activated, w_down, preferred_element_type=jnp.float32
    ).astype(jnp.bfloat16)
    returned = lax.all_to_all(
        expert_out, ("row", "col"), split_axis=0, concat_axis=0, tiled=True
    ).reshape(experts * capacity, features)
    dest_slots = target.reshape(tok_dev, TOP)
    pair_out = returned[dest_slots].astype(jnp.float32)
    result = middle + jnp.sum(gate_probs[:, :, None] * pair_out, axis=1)
    grad_out = out_grad.astype(jnp.float32)
    grad_gates = jnp.sum(pair_out * grad_out[:, None, :], axis=2)
    pair_grads = (
        (gate_probs[:, :, None] * grad_out[:, None, :])
        .reshape(tok_dev * TOP, features)
        .astype(jnp.bfloat16)
    )
    grad_send = jnp.where(filled, pair_grads[source_pair], jnp.zeros((), jnp.bfloat16)).reshape(
        buffer_shape
    )
    grad_arrived, rows_back = (
        lax.all_to_all(grad_send, ("row", "col"), split_axis=0, concat_axis=0, tiled=True),
        lax.all_to_all(pack_rows(), ("row", "col"), split_axis=0, concat_axis=0, tiled=True),
    )
    gate_up_back = expert_front(rows_back)
    act_back = swiglu(gate_up_back).astype(jnp.bfloat16)
    grad_acts = jnp.einsum(
        "secd,efd->secf", grad_arrived, w_down, preferred_element_type=jnp.float32
    )
    grad_down = jnp.einsum(
        "secf,secd->efd", act_back, grad_arrived, preferred_element_type=jnp.float32
    )
    unused, swiglu_back = jax.vjp(swiglu, gate_up_back)
    grad_gate_up = swiglu_back(grad_acts)[0].astype(jnp.bfloat16)
    grad_in = jnp.einsum(
        "secd,secf->edf", rows_back, grad_gate_up, preferred_element_type=jnp.float32
    )
    grad_pairs = jnp.einsum(
        "secf,edf->secd", grad_gate_up, w_in, preferred_element_type=jnp.float32
    ).astype(jnp.bfloat16)
    came_back = lax.all_to_all(
        grad_pairs, ("row", "col"), split_axis=0, concat_axis=0, tiled=True
    ).reshape(experts * capacity, features)
    grad_from_experts = jnp.sum(came_back[dest_slots].astype(jnp.float32), axis=1)
    grad_chosen = gate_back(grad_gates)[0]
    grad_logits = jnp.sum(jnp.where(picked, grad_chosen[:, :, None], 0.0), axis=1)
    grad_router = lax.dot_general(
        normed_wide,
        grad_logits,
        (((0,), (0,)), ((), ())),
        precision=HIGHEST,
        preferred_element_type=jnp.float32,
    )
    grad_normed_moe = grad_from_experts + lax.dot_general(
        grad_logits,
        router,
        (((1,), (1,)), ((), ())),
        precision=HIGHEST,
        preferred_element_type=jnp.float32,
    )
    unused, norm_back_moe = jax.vjp(norm_apply, middle, norm_gain_moe)
    grad_middle_part, grad_gain_moe = norm_back_moe(grad_normed_moe)
    grad_middle = grad_out + grad_middle_part
    grad_attn = grad_middle.astype(jnp.bfloat16)
    grad_block = lax.all_gather(grad_attn, "col", axis=0, tiled=True)
    qkv_back, out_back = fetch_weights()
    grad_w_out_part = lax.dot_general(
        grad_block, heads_low, (((0,), (0,)), ((), ())), preferred_element_type=jnp.float32
    )
    grad_heads = (
        jnp.dot(grad_block, out_back, preferred_element_type=jnp.float32)
        .astype(jnp.bfloat16)
        .reshape(query_rows.shape)
    )
    grad_queries, grad_keys, grad_values = attend_backward(
        query_rows, key_rows, value_rows, segment, score_scale, log_sums, grad_heads
    )
    unused, query_back = jax.vjp(rotate_fixed, query_cols)
    unused, key_back = jax.vjp(rotate_fixed, key_cols)
    grad_mixed = (
        jnp.concatenate(
            [
                query_back(grad_queries)[0].reshape(block_tok, kv_local, REP * HD),
                key_back(grad_keys)[0],
                grad_values,
            ],
            axis=2,
        )
        .reshape(block_tok, -1)
        .astype(jnp.bfloat16)
    )
    grad_w_qkv_part = lax.dot_general(
        block_rows, grad_mixed, (((0,), (0,)), ((), ())), preferred_element_type=jnp.float32
    )
    part_rows = grad_mixed
    grad_normed_attn = lax.psum_scatter(
        lax.dot_general(
            part_rows, qkv_back, (((1,), (1,)), ((), ())), preferred_element_type=jnp.float32
        ),
        "col",
        scatter_dimension=0,
        tiled=True,
    )
    unused, norm_back_attn = jax.vjp(norm_apply, rows_in, norm_gain_attn)
    grad_rows_part, grad_gain_attn = norm_back_attn(grad_normed_attn)
    grad_hidden = grad_middle + grad_rows_part
    grad_w_qkv, grad_w_out = (
        lax.psum_scatter(
            grad_w_qkv_part.astype(jnp.bfloat16), ("dp", "row"), scatter_dimension=0, tiled=True
        ).astype(jnp.float32),
        lax.psum_scatter(
            grad_w_out_part.astype(jnp.bfloat16), ("dp", "row"), scatter_dimension=0, tiled=True
        ).astype(jnp.float32),
    )
    grad_w_in, grad_w_down = (
        lax.psum(grad_in.astype(jnp.bfloat16), "dp").astype(jnp.float32),
        lax.psum(grad_down.astype(jnp.bfloat16), "dp").astype(jnp.float32),
    )
    grad_norm_attn, grad_norm_moe, grad_router_all = lax.psum(
        (grad_gain_attn, grad_gain_moe, grad_router), ("dp", "row", "col")
    )
    return (
        result,
        grad_hidden,
        grad_norm_attn,
        grad_norm_moe,
        grad_w_qkv,
        grad_w_out,
        grad_router_all,
        grad_w_in,
        grad_w_down,
    )


def solution(mesh):
    in_specs = (
        P(("dp", "row", "col"), None),
        P(),
        P(),
        P(("dp", "row"), "col"),
        P(("dp", "row"), "col"),
        P(),
        P(("row", "col"), None, None),
        P(("row", "col"), None, None),
        P(("dp", "row"), None),
        P(("dp", "row", "col"), None),
        P(("dp", "row", "col"), None),
    )
    out_specs = (
        P(("dp", "row", "col"), None),
        P(("dp", "row", "col"), None),
        P(),
        P(),
        P(("dp", "row"), "col"),
        P(("dp", "row"), "col"),
        P(),
        P(("row", "col"), None, None),
        P(("row", "col"), None, None),
    )
    return jax.shard_map(shards, mesh=mesh, in_specs=in_specs, out_specs=out_specs, check_vma=False)
```

profile of v0, /device:TPU:0, one launch (start us, length us, event | category | flops | bytes accessed | tf_op | source)
XLA Modules:
  0.0 2142.9 jit_solution(11417975600080087430)
XLA Ops:
  17.1 22.9 %all-gather.7.cloned.1.call-done = bf16[1536,640]{1,0:T(8,128)(2,1)} async-done(((bf16[192,640]{1,0:T(8,128)(2,1)}), bf16[1536,640]{1,0:T(8,128)(2,1)}) %all-gather.7.cloned.1.call-update) | async-done | bytes 1966096 | tf_op jit(solution)/shard_map/all_gather | solution.py:168
  40.0 65.7 %all-gather.5.cloned.1.call-done = bf16[1024,1536]{1,0:T(8,128)(2,1)} async-done(((bf16[256,1536]{1,0:T(8,128)(2,1)}), bf16[1024,1536]{1,0:T(8,128)(2,1)}) %all-gather.5.cloned.1.call-update) | async-done | bytes 3145744 | tf_op jit(solution)/shard_map/all_gather | solution.py:174
  114.0 27.3 %while.31 = (s32[]{:T(128)}, bf16[2,512,2,3,64]{1,4,3,2,0:T(8,128)(2,1)}, f32[2,2,3,512,1]{3,2,1,4,0:T(4,128)S(1)}, s32[2]{0:T(128)S(1)}, s32[1024]{0:T(1024)S(1...) while((s32[]{:T(128)}, ...), condition=%wide.region_7.8_spmd, body=%wide.region_4.7_spmd.sunk | while | flops 844823040 | bytes 42339084 | solution.py:93
  154.7 16.4 reduce-window.11
  188.5 71.6 %reduce-scatter.5.cloned.1.call-done = f32[256,1536]{1,0:T(8,128)} async-done(((f32[1024,1536]{1,0:T(8,128)}), f32[256,1536]{1,0:T(8,128)}) %reduce-scatter.5.cloned.1.call-update) | async-done | bytes 1572880 | tf_op jit(solution)/shard_map/reduce_scatter | solution.py:188
  265.2 26.5 %gather_fusion = bf16[4096,1536]{1,0:T(8,128)(2,1)} fusion(bf16[256,1536]{1,0:T(8,128)(2,1)} %copy-done.2, s32[4096]{0:T(1024)S(1)} %get-tuple-element.363), kind=kCustom, calls=%fused_computation | custom fusion | bytes 25182208 | tf_op jit(solution)/shard_map/gather | solution.py:216
  296.6 28.8 %gather_fusion.2 = bf16[4096,1536]{1,0:T(8,128)(2,1)} fusion(bf16[2048,1536]{1,0:T(8,128)(2,1)} %fusion.48, s32[4096]{0:T(1024)S(1)} %get-tuple-element.362), kind=kCustom, calls=%fused_computation.2 | custom fusion | bytes 25182208 | tf_op jit(solution)/shard_map/gather | solution.py:241
  325.5 13.6 broadcast_select_fusion
  339.1 279.5 %all_to_all.21 = bf16[16,2,128,1536]{3,2,1,0:T(8,128)(2,1)} all-to-all(bf16[16,2,128,1536]{3,2,1,0:T(8,128)(2,1)S(1)} %get-tuple-element.365), channel_id=1, replica_groups=mesh['dp'=2,'row'=4,'col'=4] {'row','col'}, dimensions={0} | all-to-all | bytes 25165824 | tf_op jit(solution)/shard_map/all_to_all | solution.py:222
  623.8 21.2 fusion.60
  645.0 253.0 %all-to-all-done.2 = bf16[16,2,128,1536]{3,2,1,0:T(8,128)(2,1)} async-done(((bf16[16,2,128,1536]{3,2,1,0:T(8,128)(2,1)}), bf16[16,2,128,1536]{3,2,1,0:T(8,128)(2,1)}, u32[]{:S(2)}, u32[]{:S(2)}) %all-to-all-start.2) | async-done | bytes 12582944 | tf_op jit(solution)/shard_map/all_to_all | solution.py:245
  898.0 19.2 bitcast_multiply_fusion.3
  936.7 19.6 convert_bitcast_fusion
  956.3 10.7 copy.84
  967.1 243.8 %all-to-all-done.1 = bf16[16,2,128,1536]{3,2,1,0:T(8,128)(2,1)} async-done(((bf16[16,2,128,1536]{3,2,1,0:T(8,128)(2,1)}), bf16[16,2,128,1536]{3,2,1,0:T(8,128)(2,1)}, u32[]{:S(2)}, u32[]{:S(2)}) %all-to-all-start.1) | async-done | bytes 12582944 | tf_op jit(solution)/shard_map/all_to_all | solution.py:228
  1216.0 19.6 gather_fusion.1
  1245.3 244.6 %all-to-all-done.3 = bf16[16,2,128,1536]{3,2,1,0:T(8,128)(2,1)} async-done(((bf16[16,2,128,1536]{3,2,1,0:T(8,128)(2,1)}), bf16[16,2,128,1536]{3,2,1,0:T(8,128)(2,1)}, u32[]{:S(2)}, u32[]{:S(2)}) %all-to-all-start.3) | async-done | bytes 12582944 | tf_op jit(solution)/shard_map/all_to_all | solution.py:264
  1490.0 19.8 gather_fusion.3
  1521.7 13.5 bitcast_convert_fusion.1
  1535.2 22.1 %bitcast_convert_fusion = bf16[2,1536,1024]{2,1,0:T(8,128)(2,1)} fusion(bf16[16,2,128,1536]{3,2,1,0:T(8,128)(2,1)} %all_to_all.21, f32[16,2,128,512]{3,2,0,1:T(8,128)} %get-tuple-element.346, f32[16,2,128,512]{3,2,0,1:T(8,128)} %get-tuple-element.345), kind=kOutput, calls=%fused_computation.69 | convolution fusion | flops 12896436224 | bytes 35651584 | tf_op jit(solution)/shard_map/secd,secf->edf/dot_general | solution.py:258
  1557.4 26.5 %all-gather.11.cloned.1.call-done = bf16[1024,1536]{1,0:T(8,128)(2,1)} async-done(((bf16[256,1536]{1,0:T(8,128)(2,1)}), bf16[1024,1536]{1,0:T(8,128)(2,1)}) %all-gather.11.cloned.1.call-update) | async-done | bytes 3145744 | tf_op jit(solution)/shard_map/all_gather | solution.py:288
  1587.6 128.1 %while.32 = (s32[]{:T(128)}, f32[1024,2,64]{0,2,1:T(8,128)S(1)}, f32[1024,2,64]{0,2,1:T(8,128)}, f32[2,512,2,3,64]{1,0,4,3,2:T(2,128)}, s32[2]{0:T(128)S(1)}, /*...) while((s32[]{:T(128)}, f32[1024,2,64]{0,2,1:T(8,128)S(1)}, ...), condition=%wide.region_25.26_spmd.clone, body=%wide.region_23.25_spmd.clone.sunk | while | flops 2062875136 | bytes 178375184 | solution.py:132
  1599.4 11.2 fusion.159
  1625.0 15.1 dynamic_update_slice.29
  1663.5 11.2 fusion.159
  1688.5 15.1 dynamic_update_slice.29
  1739.4 67.2 %all-reduce.13.cloned.1.call-done = (bf16[2,1536,1024]{2,1,0:T(8,128)(2,1)}, bf16[2,512,1536]{2,1,0:T(8,128)(2,1)}) async-done(((bf16[2,1536,1024]{2,1,0:T(8,128)(2,1)}, bf16[2,512,1536]{2,1,0:T(8,128)(2,1)}), (bf16[2,1536,1024]{2,1,0:T(8,128)(2,1)}, bf16[2,512,1536]{2,1,0:T(8,128)(2,1)})) %all-reduce.13.cloned.1.call-update) | async-done | bytes 9437200 | tf_op jit(solution)/shard_map/psum | solution.py:339
  1820.7 26.5 %reduce-scatter.11.cloned.1.call-done = bf16[192,384]{1,0:T(8,128)(2,1)} async-done(((bf16[1536,384]{1,0:T(8,128)(2,1)}), bf16[192,384]{1,0:T(8,128)(2,1)}) %reduce-scatter.11.cloned.1.call-update) | async-done | bytes 147472 | tf_op jit(solution)/shard_map/reduce_scatter | solution.py:334
  1848.9 42.5 %reduce-scatter.9.cloned.1.call-done = bf16[192,640]{1,0:T(8,128)(2,1)} async-done(((bf16[1536,640]{1,0:T(8,128)(2,1)}), bf16[192,640]{1,0:T(8,128)(2,1)}) %reduce-scatter.9.cloned.1.call-update) | async-done | bytes 245776 | tf_op jit(solution)/shard_map/reduce_scatter | solution.py:331
  1893.1 111.3 %reduce-scatter.7.cloned.1.call-done = f32[256,1536]{1,0:T(8,128)} async-done(((f32[1024,1536]{1,0:T(8,128)}), f32[256,1536]{1,0:T(8,128)}) %reduce-scatter.7.cloned.1.call-update) | async-done | bytes 1572880 | tf_op jit(solution)/shard_map/reduce_scatter | solution.py:319
  2012.4 40.9 %all-reduce.6 = (f32[1536]{0:T(1024)}, f32[1536]{0:T(1024)}) all-reduce(f32[1536]{0:T(1024)S(1)} %get-tuple-element.295, f32[1536]{0:T(1024)S(1)} %copy-done.43), channel_id=1, replica_groups=mesh['dp'=2,'row'=4,'col'=4] {'dp','row','col'}, use_global_device_ids=true, to_apply=%region_29.30 | all-reduce | flops 3072 | bytes 24576 | tf_op jit(solution)/shard_map/psum | solution.py:342
  2053.3 80.6 %all-reduce.11.cloned.1.call-done = f32[1536,32]{0,1:T(8,128)} async-done(((f32[1536,32]{0,1:T(8,128)}), f32[1536,32]{0,1:T(8,128)}) %all-reduce.11.cloned.1.call-update) | async-done | bytes 196624 | tf_op jit(solution)/shard_map/psum | solution.py:342
  (307 shorter events, 259.8 us)
Async XLA Ops:
  7.2 890.8 %copy-start = (bf16[2,512,1536]{2,1,0:T(8,128)(2,1)S(1)}, bf16[2,512,1536]{2,1,0:T(8,128)(2,1)}, u32[]{:S(2)}) copy-start(bf16[2,512,1536]{2,1,0:T(8,128)(2,1)} %param.22) | copy-start | bytes 9437188
  7.2 32.8 %all-gather.7.cloned.1.call-start = ((), (), s32[]{:S(2)}) async-start(), calls=%async_computation.9 | async-start | bytes 2211840 | tf_op jit(solution)/shard_map/all_gather | solution.py:168
  7.9 97.7 %all-gather.5.cloned.1.call-start = ((), (), s32[]{:S(2)}) async-start(), calls=%async_computation.8 | async-start | bytes 3932160 | tf_op jit(solution)/shard_map/all_gather | solution.py:174
  12.9 131.6 %all-gather.9.cloned.1.call-start = ((), (), s32[]{:S(2)}) async-start(), calls=%async_computation.10 | async-start | bytes 1327104 | tf_op jit(solution)/shard_map/all_gather | solution.py:169
  13.6 246.5 %reduce-scatter.5.cloned.1.call-start = ((), (), s32[]{:S(2)}) async-start(), calls=%async_computation.11 | async-start | bytes 7864320 | tf_op jit(solution)/shard_map/reduce_scatter | solution.py:188
  17.1 94.5 %copy-start.14 = (f32[1024,64]{0,1:T(8,128)}, f32[1024,64]{0,1:T(8,128)S(1)}, u32[]{:S(2)}) copy-start(f32[1024,64]{0,1:T(8,128)S(1)} %get-tuple-element.360) | copy-start | bytes 786436
  150.6 111.5 %copy-start.37 = (f32[1536]{0:T(1024)S(1)}, f32[1536]{0:T(1024)}, u32[]{:S(2)}) copy-start(f32[1536]{0:T(1024)} %param.17) | copy-start | bytes 18436
  176.1 87.4 %copy-start.26 = (f32[1536,32]{0,1:T(8,128)S(1)}, f32[1536,32]{0,1:T(8,128)}, u32[]{:S(2)}) copy-start(f32[1536,32]{0,1:T(8,128)} %param.20) | copy-start | bytes 589828
  618.6 279.3 %all-to-all-start.2 = ((bf16[16,2,128,1536]{3,2,1,0:T(8,128)(2,1)}), bf16[16,2,128,1536]{3,2,1,0:T(8,128)(2,1)}, u32[]{:S(2)}, u32[]{:S(2)}) async-start(bf16[16,2,128,1536]{3,2,1,0:T(8,128)(2,1)} %get-tuple-element.364), calls=%async_computation.3 | async-start | bytes 25165824 | tf_op jit(solution)/shard_map/all_to_all | solution.py:245
  931.5 279.3 %all-to-all-start.1 = ((bf16[16,2,128,1536]{3,2,1,0:T(8,128)(2,1)}), bf16[16,2,128,1536]{3,2,1,0:T(8,128)(2,1)}, u32[]{:S(2)}, u32[]{:S(2)}) async-start(bf16[16,2,128,1536]{3,2,1,0:T(8,128)(2,1)} %copy.81), calls=%async_computation.2 | async-start | bytes 25165824 | tf_op jit(solution)/shard_map/all_to_all | solution.py:228
  967.0 248.8 %copy-start.30 = (s32[256,8]{1,0:T(8,128)S(1)}, s32[256,8]{1,0:T(8,128)}, u32[]{:S(2)}) copy-start(s32[256,8]{1,0:T(8,128)} %get-tuple-element.358) | copy-start | bytes 24580
  967.0 248.9 %copy-start.50 = (f32[256]{0:T(256)S(1)}, f32[256]{0:T(256)}, u32[]{:S(2)}) copy-start(f32[256]{0:T(256)} %copy-done.49) | copy-start | bytes 3076
  1210.9 279.1 %all-to-all-start.3 = ((bf16[16,2,128,1536]{3,2,1,0:T(8,128)(2,1)}), bf16[16,2,128,1536]{3,2,1,0:T(8,128)(2,1)}, u32[]{:S(2)}, u32[]{:S(2)}) async-start(bf16[16,2,128,1536]{3,2,1,0:T(8,128)(2,1)} %copy.84), calls=%async_computation.4 | async-start | bytes 25165824 | tf_op jit(solution)/shard_map/all_to_all | solution.py:264
  1215.8 368.0 %all-gather.11.cloned.1.call-start = ((), (), s32[]{:S(2)}) async-start(), calls=%async_computation.12 | async-start | bytes 3932160 | tf_op jit(solution)/shard_map/all_gather | solution.py:288
  1245.3 271.8 %copy-start.31 = (f32[256,32]{0,1:T(8,128)}, f32[256,32]{0,1:T(8,128)S(1)}, u32[]{:S(2)}) copy-start(f32[256,32]{0,1:T(8,128)S(1)} %select_reduce_fusion) | copy-start | bytes 98308
  1521.6 285.0 %all-reduce.13.cloned.1.call-start = ((), (), s32[]{:S(2)}) async-start(), calls=%async_computation.17 | async-start | bytes 18874368 | tf_op jit(solution)/shard_map/psum | solution.py:339
  1557.3 30.2 %copy-start.6 = (bf16[1024,2,64]{0,2,1:T(8,128)(2,1)S(1)}, bf16[1024,2,64]{0,2,1:T(8,128)(2,1)}, u32[]{:S(2)}) copy-start(bf16[1024,2,64]{0,2,1:T(8,128)(2,1)} %copy-done.5) | copy-start | bytes 786436
  1557.3 30.2 %copy-start.12 = (bf16[1024,2,64]{0,2,1:T(8,128)(2,1)S(1)}, bf16[1024,2,64]{0,2,1:T(8,128)(2,1)}, u32[]{:S(2)}) copy-start(bf16[1024,2,64]{0,2,1:T(8,128)(2,1)} %get-tuple-element.613) | copy-start | bytes 786436
  1557.3 30.2 %copy-start.22 = (s32[1024]{0:T(1024)S(1)}, s32[1024]{0:T(1024)}, u32[]{:S(2)}) copy-start(s32[1024]{0:T(1024)} %copy-done.21) | copy-start | bytes 12292
  1557.3 289.9 %reduce-scatter.11.cloned.1.call-start = ((), (), s32[]{:S(2)}) async-start(), calls=%async_computation.15 | async-start | bytes 1327104 | tf_op jit(solution)/shard_map/reduce_scatter | solution.py:334
  1587.6 132.8 %copy-start.17 = (f32[1024,64]{0,1:T(8,128)S(1)}, f32[1024,64]{0,1:T(8,128)}, u32[]{:S(2)}) copy-start(f32[1024,64]{0,1:T(8,128)} %get-tuple-element.361) | copy-start | bytes 786436
  1726.1 165.2 %reduce-scatter.9.cloned.1.call-start = ((), (), s32[]{:S(2)}) async-start(), calls=%async_computation.14 | async-start | bytes 2211840 | tf_op jit(solution)/shard_map/reduce_scatter | solution.py:331
  1733.1 271.3 %reduce-scatter.7.cloned.1.call-start = ((), (), s32[]{:S(2)}) async-start(), calls=%async_computation.13 | async-start | bytes 7864320 | tf_op jit(solution)/shard_map/reduce_scatter | solution.py:319
  1739.4 394.6 %all-reduce.11.cloned.1.call-start = ((), (), s32[]{:S(2)}) async-start(), calls=%async_computation.16 | async-start | bytes 393216 | tf_op jit(solution)/shard_map/psum | solution.py:342
  1815.9 188.5 %copy-start.40 = (f32[1536]{0:T(1024)S(1)}, f32[1536]{0:T(1024)}, u32[]{:S(2)}) copy-start(f32[1536]{0:T(1024)} %param.16) | copy-start | bytes 18436
  1815.9 188.5 %copy-start.52 = (f32[256]{0:T(256)S(1)}, f32[256]{0:T(256)}, u32[]{:S(2)}) copy-start(f32[256]{0:T(256)} %copy-done.51) | copy-start | bytes 3076
  1815.9 190.8 %copy-start.56 = (f32[256]{0:T(256)S(1)}, f32[256]{0:T(256)}, u32[]{:S(2)}) copy-start(f32[256]{0:T(256)} %copy-done.55) | copy-start | bytes 3076
  1815.9 190.8 %copy-start.39 = (f32[1536]{0:T(1024)S(1)}, f32[1536]{0:T(1024)}, u32[]{:S(2)}) copy-start(f32[1536]{0:T(1024)} %param.17) | copy-start | bytes 18436
  1815.9 190.8 %copy-start.46 = (f32[256]{0:T(256)S(1)}, f32[256]{0:T(256)}, u32[]{:S(2)}) copy-start(f32[256]{0:T(256)} %copy-done.44) | copy-start | bytes 3076
  1815.9 190.8 %copy-start.54 = (f32[256]{0:T(256)S(1)}, f32[256]{0:T(256)}, u32[]{:S(2)}) copy-start(f32[256]{0:T(256)} %copy-done.53) | copy-start | bytes 3076
  1893.1 119.3 %copy-start.43 = (f32[1536]{0:T(1024)S(1)}, f32[1536]{0:T(1024)}, u32[]{:S(2)}) copy-start(f32[1536]{0:T(1024)} %get-tuple-element.293) | copy-start | bytes 18436
  2004.4 131.2 %copy-start.1 = (bf16[2,512,1536]{2,1,0:T(8,128)(2,1)S(1)}, bf16[2,512,1536]{2,1,0:T(8,128)(2,1)}, u32[]{:S(2)}) copy-start(bf16[2,512,1536]{2,1,0:T(8,128)(2,1)} %param.22) | copy-start | bytes 9437188
  (53 other events, 485.4 us)
Sparse Core Ops, SparseCore 0:
  9.9 30.0 all-gather.6
  42.1 63.4 all-gather.4
  107.6 22.7 all-gather.8
  150.7 109.4 reduce-scatter.4
  1521.7 62.1 all-gather.10
  1586.8 219.7 all-reduce.12
  1810.4 36.7 reduce-scatter.10
  1851.0 40.2 reduce-scatter.8
  1893.6 110.7 reduce-scatter.6
  2010.4 123.5 all-reduce.10
where the time goes:
time: 2160 us; the launch traced here: 2140 us
  waiting for transfers between devices  1260 us (58%)
  blocking collectives  320 us (15%)
  matrix products  219 us (10%)
  local copies, waits for them, and re-layouts  183 us (8%)
  other arithmetic  125 us (6%)
    all_to_all x1, blocking collectives, shards(): lax.all_to_all(pack_rows(), ('row', 'col'), split_axis=0, concat_axis=0,...  280 us
    all_to_all x1, waiting for transfers between devices, shards(): lax.all_to_all(grad_send, ('row', 'col'), split_axis=0, concat_axis=0, ti...  253 us
    all_to_all x1, waiting for transfers between devices, shards(): lax.all_to_all(grad_pairs, ('row', 'col'), split_axis=0, concat_axis=0, t...  245 us
    all_to_all x1, waiting for transfers between devices, shards(): lax.all_to_all(expert_out, ('row', 'col'), split_axis=0, concat_axis=0, t...  244 us
    reduce_scatter x1, waiting for transfers between devices, shards(): lax.psum_scatter(lax.dot_general(part_rows, qkv_back, (((1,), (1,)), ((),...  111 us
    psum x1, waiting for transfers between devices, shards(): lax.psum((grad_gain_attn, grad_gain_moe, grad_router), ('dp', 'row', 'col'))  80.6 us
    reduce_scatter x1, waiting for transfers between devices, shards(): lax.psum_scatter(lax.dot_general(part_rows, out_full, (((1,), (1,)), ((),...  71.6 us
    psum x1, waiting for transfers between devices, shards(): lax.psum(grad_in.astype(jnp.bfloat16), 'dp').astype(jnp.float32)  67.2 us
  transfers between devices with their start and end apart: 13, of which 12 were waited for; matrix products, arithmetic and copies ran while one was open for 17% of the time, Pallas kernels for 0%

commit v1 on v0

v1 whole, which is shorter than its diff:
```python
import functools
import math

import jax
import jax.numpy as jnp
from jax import lax
from jax.experimental import pallas as pl
from jax.experimental.pallas import tpu as pltpu
from jax.sharding import PartitionSpec as P

HD = 64
FFE = 512
TOP = 8
REP = 3
SEQ_MAX = 512

EPSILON = 1e-06
HIGHEST = lax.Precision.HIGHEST
MASKED_SCORE = -1e30
F32 = jnp.float32
BF16 = jnp.bfloat16


def dot_nn(left, right):
    return lax.dot_general(left, right, (((1,), (0,)), ((), ())), preferred_element_type=F32)


def dot_nt(left, right):
    return lax.dot_general(left, right, (((1,), (1,)), ((), ())), preferred_element_type=F32)


def dot_tn(left, right):
    return lax.dot_general(left, right, (((0,), (0,)), ((), ())), preferred_element_type=F32)


def moe_body(
    cap, tile, tiles,
    first_ref, x_ref, dy_ref, rt_ref, rs_ref, win_ref, wdn_ref,
    res_ref, gn_ref, dg_ref, dwi_ref, dwd_ref,
    buf, gate, slot, run, offs, acc_i, acc_d,
):
    step = pl.program_id(0)
    sources = slot.shape[1]
    tok, feat = x_ref.shape
    experts = rs_ref.shape[0] // 3
    local = buf.shape[0]
    ff = wdn_ref.shape[1]

    def one_hot(srow):
        places = lax.broadcasted_iota(jnp.int32, (cap, tok), 0).astype(F32)
        return srow == places

    @pl.when(step < sources)
    def _gather():
        x = x_ref[...]
        dy = dy_ref[...]

        @pl.when(step == 0)
        def _():
            for e in range(local):
                run[e] = 0

        thirds = dot_nt(rs_ref[...], x)
        logits = (thirds[2 * experts :] + thirds[experts : 2 * experts]) + thirds[:experts]
        ids = lax.broadcasted_iota(jnp.int32, (experts, tok), 0)
        rt = rt_ref[0]
        used = ids == rt[0:1]
        for k in range(1, rt.shape[0]):
            used = used | (ids == rt[k : k + 1])
        top = jnp.max(jnp.where(used, logits, MASKED_SCORE), axis=0, keepdims=True)
        terms = jnp.where(used, jnp.exp(logits - top), 0.0)
        gates = terms / jnp.sum(terms, axis=0, keepdims=True)
        before = (
            lax.broadcasted_iota(jnp.int32, (tok, tok), 0)
            < lax.broadcasted_iota(jnp.int32, (tok, tok), 1)
        )
        used_f = jnp.where(used, 1.0, 0.0)
        rank = dot_nn(used_f.astype(BF16), jnp.where(before, 1.0, 0.0).astype(BF16))
        for e in range(local):
            mine = ids == first_ref[0] + e
            grow = jnp.sum(jnp.where(mine, gates, 0.0), axis=0, keepdims=True)
            srow = jnp.sum(jnp.where(mine & used, rank + 1.0, 0.0), axis=0, keepdims=True) - 1.0
            hot = one_hot(srow)
            hot_b = jnp.where(hot, 1.0, 0.0).astype(BF16)
            off = pl.multiple_of(run[e], 16)
            buf[e, pl.ds(off, cap), :feat] = dot_nn(hot_b, x).astype(BF16)
            buf[e, pl.ds(off, cap), feat:] = dot_nn(hot_b, dy).astype(BF16)
            gcol = jnp.sum(jnp.where(hot, grow, 0.0), axis=1, keepdims=True)
            gate[e, pl.ds(off, cap), :] = jnp.broadcast_to(gcol, (cap, 128))
            slot[e, pl.ds(step, 1), :] = srow
            offs[e, step] = off
            count = jnp.sum(jnp.where(mine, used_f, 0.0)).astype(jnp.int32)
            run[e] = off + ((count + 15) & -16)

        @pl.when(step == sources - 1)
        def _():
            for e in range(local):
                end = pl.multiple_of(run[e], 16)
                buf[e, pl.ds(end, tile), :] = jnp.zeros((tile, 2 * feat), BF16)
                gate[e, pl.ds(end, tile), :] = jnp.zeros((tile, 128), F32)

    work = step - sources
    e = work // tiles
    j = work % tiles

    @pl.when((work >= 0) & (work < local * tiles))
    def _experts():
        @pl.when(j == 0)
        def _():
            acc_i[...] = jnp.zeros_like(acc_i)
            acc_d[...] = jnp.zeros_like(acc_d)

        @pl.when(j * tile < run[e])
        def _():
            at = pl.ds(pl.multiple_of(j * tile, tile), tile)
            rows = buf[e, at, :feat]
            grads = buf[e, at, feat:]
            g = gate[e, at, 0:1]
            a = dot_nn(rows, win_ref[0, :, :ff])
            b = dot_nn(rows, win_ref[0, :, ff:])
            ga = dot_nt(grads, wdn_ref[0])
            sig = 1.0 / (1.0 + jnp.exp(-a))
            silu = a * sig
            act = silu * b
            gate[e, at, :] = jnp.broadcast_to(
                jnp.sum(act * ga, axis=1, keepdims=True), (tile, 128)
            )
            gag = g * ga
            da = (gag * b * (sig * (1.0 + a * (1.0 - sig)))).astype(BF16)
            db = (gag * silu).astype(BF16)
            act_g = (g * act).astype(BF16)
            acc_d[...] += dot_tn(act_g, grads)
            acc_i[:, :ff] += dot_tn(rows, da)
            acc_i[:, ff:] += dot_tn(rows, db)
            buf[e, at, :feat] = dot_nn(act_g, wdn_ref[0]).astype(BF16)
            buf[e, at, feat:] = (
                dot_nt(da, win_ref[0, :, :ff]) + dot_nt(db, win_ref[0, :, ff:])
            ).astype(BF16)

        @pl.when(j == tiles - 1)
        def _():
            dwi_ref[0] = acc_i[...].astype(BF16)
            dwd_ref[0] = acc_d[...].astype(BF16)

    back = work - local * tiles

    @pl.when(back >= 0)
    def _scatter():
        total = None
        for e in range(local):
            srow = slot[e, pl.ds(back, 1), :]
            hot = one_hot(srow)
            off = pl.multiple_of(offs[e, back], 16)
            hot_b = jnp.where(hot, 1.0, 0.0).astype(BF16)
            term = dot_tn(hot_b, buf[e, pl.ds(off, cap), :])
            total = term if total is None else total + term
            dcol = gate[e, pl.ds(off, cap), 0:1]
            dg_ref[0, e : e + 1, :] = jnp.sum(jnp.where(hot, dcol, 0.0), axis=0, keepdims=True)
        dg_ref[0, local:, :] = jnp.zeros((dg_ref.shape[1] - local, tok), F32)
        res_ref[...] = total[:, :feat].astype(BF16)
        gn_ref[...] = total[:, feat:].astype(BF16)


def moe_experts(first, x_all, dy_all, rt_all, router_parts, w_in, w_down, cap):
    sources, top, tok = rt_all.shape
    feat = x_all.shape[1]
    local, _, ff2 = w_in.shape
    ff = ff2 // 2
    tile = min(256, sources * cap)
    tiles = sources * cap // tile
    room = sources * cap + max(tile, cap)
    steps = 2 * sources + local * tiles

    def src(i, first_ref):
        return (jnp.minimum(i, sources - 1), 0)

    def src3(i, first_ref):
        return (jnp.minimum(i, sources - 1), 0, 0)

    def exp3(i, first_ref):
        return (jnp.clip((i - sources) // tiles, 0, local - 1), 0, 0)

    def dst(i, first_ref):
        return (jnp.maximum(i - sources - local * tiles, 0), 0)

    def dst3(i, first_ref):
        return (jnp.maximum(i - sources - local * tiles, 0), 0, 0)

    pairs = sources * tok * top * local // (experts_of(router_parts))
    flops = 2 * pairs * feat * ff * 9
    return pl.pallas_call(
        functools.partial(moe_body, cap, tile, tiles),
        grid_spec=pltpu.PrefetchScalarGridSpec(
            num_scalar_prefetch=1,
            grid=(steps,),
            in_specs=[
                pl.BlockSpec((tok, feat), src),
                pl.BlockSpec((tok, feat), src),
                pl.BlockSpec((1, top, tok), src3),
                pl.BlockSpec(router_parts.shape, lambda i, f: (0, 0)),
                pl.BlockSpec((1, feat, ff2), exp3, pipeline_mode=pl.Buffered(1)),
                pl.BlockSpec((1, ff, feat), exp3, pipeline_mode=pl.Buffered(1)),
            ],
            out_specs=[
                pl.BlockSpec((tok, feat), dst),
                pl.BlockSpec((tok, feat), dst),
                pl.BlockSpec((1, 8, tok), dst3),
                pl.BlockSpec((1, feat, ff2), exp3, pipeline_mode=pl.Buffered(1)),
                pl.BlockSpec((1, ff, feat), exp3, pipeline_mode=pl.Buffered(1)),
            ],
            scratch_shapes=[
                pltpu.VMEM((local, room, 2 * feat), BF16),
                pltpu.VMEM((local, room, 128), F32),
                pltpu.VMEM((local, sources, tok), F32),
                pltpu.SMEM((local,), jnp.int32),
                pltpu.SMEM((local, sources), jnp.int32),
                pltpu.VMEM((feat, ff2), F32),
                pltpu.VMEM((ff, feat), F32),
            ],
        ),
        out_shape=[
            jax.ShapeDtypeStruct(x_all.shape, BF16),
            jax.ShapeDtypeStruct(x_all.shape, BF16),
            jax.ShapeDtypeStruct((sources, 8, tok), F32),
            jax.ShapeDtypeStruct(w_in.shape, BF16),
            jax.ShapeDtypeStruct(w_down.shape, BF16),
        ],
        compiler_params=pltpu.CompilerParams(vmem_limit_bytes=60 * 1024 * 1024),
        cost_estimate=pl.CostEstimate(
            flops=flops, bytes_accessed=5 * x_all.size * 2, transcendentals=0
        ),
        name="moe_experts",
    )(first, x_all, dy_all, rt_all, router_parts, w_in, w_down)


def experts_of(router_parts):
    return router_parts.shape[0] // 3


def split_router(router):
    flat = router.T
    one = flat.astype(BF16)
    rest = flat - one.astype(F32)
    two = rest.astype(BF16)
    three = (rest - two.astype(F32)).astype(BF16)
    return jnp.concatenate([one, two, three], axis=0)


def lane_low(shape):
    return lax.broadcasted_iota(jnp.int32, shape, 1) < HD


def twist(tile_vals):
    width = tile_vals.shape[1]
    lane = lax.broadcasted_iota(jnp.int32, tile_vals.shape, 1)
    ahead = pltpu.roll(tile_vals, width - HD // 2, 1)
    behind = pltpu.roll(tile_vals, HD // 2, 1)
    return jnp.where(lane % HD < HD // 2, -ahead, behind)


def both_halves(tile_vals, low):
    kept = jnp.where(lane_low(tile_vals.shape) == low, tile_vals, 0.0)
    return kept + pltpu.roll(kept, HD, 1)


def head_places():
    per = REP + 2
    def at(index):
        return (index // 2, index % 2 == 0)
    groups = []
    for g in range(2):
        base = g * per
        groups.append(
            ([at(base + r) for r in range(REP)], at(base + REP), at(base + REP + 1))
        )
    return groups


def chunk_span(a, tok):
    reach = -(-(SEQ_MAX - 1) // tok)
    return max(0, a - reach) * tok, (a + 1) * tok


def mask_bias(start_row, a, tok):
    low, high = chunk_span(a, tok)
    shape = (high - low, tok)
    keys = lax.broadcasted_iota(jnp.int32, shape, 0) + low
    queries = lax.broadcasted_iota(jnp.int32, shape, 1) + a * tok
    allowed = (keys >= start_row) & (keys <= queries)
    return jnp.where(allowed, 0.0, MASKED_SCORE)


def attn_forward_body(
    chunks, here_ref, *refs,
):
    ins, (w_ref, cos_ref, sin_ref, start_ref, qkv_ref, kk_ref, vv_ref, lse_ref, heads_ref) = (
        refs[:chunks],
        refs[chunks:],
    )
    tok = ins[0].shape[0]
    here = here_ref[0]
    places = head_places()
    for k in range(chunks):
        a = lax.rem(here + (chunks - k), chunks)
        at = pl.ds(pl.multiple_of(a * tok, tok), tok)
        mixed = dot_nn(ins[k][...], w_ref[...])
        cos = cos_ref[at, :]
        sin = sin_ref[at, :]
        tiles = [mixed[:, 128 * i : 128 * (i + 1)] for i in range(mixed.shape[1] // 128)]
        turned = [t * cos + twist(t) * sin for t in tiles]
        for g, (queries, key, value) in enumerate(places):
            for r, (tile_at, low) in enumerate(queries):
                part = jnp.where(lane_low(tiles[0].shape) == low, turned[tile_at], 0.0)
                slot = 128 * (g * REP + r)
                qkv_ref[at, slot : slot + 128] = part.astype(BF16)
            kk_ref[at, 128 * g : 128 * (g + 1)] = both_halves(turned[key[0]], key[1]).astype(BF16)
            vv_ref[at, 128 * g : 128 * (g + 1)] = both_halves(tiles[value[0]], value[1]).astype(BF16)
    for a in range(chunks):
        low_key, high_key = chunk_span(a, tok)
        bias = mask_bias(start_ref[a : a + 1, :], a, tok)
        out = [None] * REP
        for g, (queries, _, _) in enumerate(places):
            keys = kk_ref[low_key:high_key, 128 * g : 128 * (g + 1)]
            vals = vv_ref[low_key:high_key, 128 * g : 128 * (g + 1)]
            for r in range(REP):
                head = g * REP + r
                q = qkv_ref[a * tok : (a + 1) * tok, 128 * head : 128 * (head + 1)]
                scores = dot_nt(keys, q) * HD ** (-0.5) + bias
                top = jnp.max(scores, axis=0, keepdims=True)
                terms = jnp.exp(scores - top)
                total = jnp.sum(terms, axis=0, keepdims=True)
                probs = (terms * (1.0 / total)).astype(BF16)
                lse_ref[head, a : a + 1, :] = top + jnp.log(total)
                mix = dot_tn(probs, vals)
                t = head // 2
                low = lane_low(mix.shape)
                out[t] = mix if head % 2 == 0 else jnp.where(low, out[t], mix)
        to = pl.ds(pl.multiple_of(lax.rem(here + (chunks - a), chunks) * tok, tok), tok)
        for t in range(REP):
            heads_ref[to, 128 * t : 128 * (t + 1)] = out[t].astype(BF16)


def attn_forward(here, parts, w_cols, cos, sin, starts):
    chunks = len(parts)
    tok, feat = parts[0].shape
    total = chunks * tok
    cols = w_cols.shape[1]
    return pl.pallas_call(
        functools.partial(attn_forward_body, chunks),
        in_specs=[pl.BlockSpec(memory_space=pltpu.SMEM)]
        + [pl.BlockSpec(memory_space=pltpu.VMEM)] * (chunks + 4),
        out_specs=[pl.BlockSpec(memory_space=pltpu.VMEM)] * 5,
        out_shape=[
            jax.ShapeDtypeStruct((total, 128 * 2 * REP), BF16),
            jax.ShapeDtypeStruct((total, 256), BF16),
            jax.ShapeDtypeStruct((total, 256), BF16),
            jax.ShapeDtypeStruct((2 * REP, 8, tok), F32),
            jax.ShapeDtypeStruct((total, 2 * REP * HD), BF16),
        ],
        compiler_params=pltpu.CompilerParams(vmem_limit_bytes=48 * 1024 * 1024),
        cost_estimate=pl.CostEstimate(
            flops=2 * total * feat * cols * 4, bytes_accessed=8 * total * cols, transcendentals=0
        ),
        name="attn_forward",
    )(here, *parts, w_cols, cos, sin, starts)


def attn_backward_body(
    chunks, here_ref, grads_ref, q_ref, kk_ref, vv_ref, lse_ref, cos_ref, sin_ref, start_ref,
    out_ref, dk, dv, dq,
):
    tok = q_ref.shape[0] // chunks
    here = here_ref[0]
    dk[...] = jnp.zeros_like(dk)
    dv[...] = jnp.zeros_like(dv)
    for a in range(chunks):
        low_key, high_key = chunk_span(a, tok)
        bias = mask_bias(start_ref[a : a + 1, :], a, tok)
        at = pl.ds(pl.multiple_of(lax.rem(here + (chunks - a), chunks) * tok, tok), tok)
        for g in range(2):
            keys = kk_ref[low_key:high_key, 128 * g : 128 * (g + 1)]
            vals = vv_ref[low_key:high_key, 128 * g : 128 * (g + 1)]
            for r in range(REP):
                head = g * REP + r
                q = q_ref[a * tok : (a + 1) * tok, 128 * head : 128 * (head + 1)]
                t, is_low = head // 2, head % 2 == 0
                pair = grads_ref[at, 128 * t : 128 * (t + 1)]
                grad = jnp.where(lane_low(pair.shape) == is_low, pair, jnp.zeros_like(pair))
                scores = dot_nt(keys, q) * HD ** (-0.5) + bias
                probs = jnp.exp(scores - lse_ref[head, a : a + 1, :])
                grad_probs = dot_nt(vals, grad)
                dv[low_key:high_key, 128 * g : 128 * (g + 1)] += dot_nn(probs.astype(BF16), grad)
                inner = jnp.sum(probs * grad_probs, axis=0, keepdims=True)
                grad_scores = (probs * (grad_probs - inner)).astype(BF16)
                dk[low_key:high_key, 128 * g : 128 * (g + 1)] += dot_nn(grad_scores, q)
                part = dot_tn(grad_scores, keys)
                here_at = slice(128 * t, 128 * (t + 1))
                rows = slice(a * tok, (a + 1) * tok)
                if is_low:
                    dq[rows, here_at] = part
                else:
                    dq[rows, here_at] = jnp.where(lane_low(part.shape), dq[rows, here_at], part)
    for a in range(chunks):
        rows = slice(a * tok, (a + 1) * tok)
        to = pl.ds(pl.multiple_of(lax.rem(here + (chunks - a), chunks) * tok, tok), tok)
        cos = cos_ref[rows, :]
        sin = sin_ref[rows, :]

        def back(vals):
            return (vals * cos - twist(vals) * sin) * HD ** (-0.5)

        def whole(vals):
            return vals + pltpu.roll(vals, HD, 1)

        low = lane_low((tok, 128))
        keys = [back(whole(dk[rows, 128 * g : 128 * (g + 1)])) for g in range(2)]
        vals = [whole(dv[rows, 128 * g : 128 * (g + 1)]) for g in range(2)]
        qs = [back(dq[rows, 128 * t : 128 * (t + 1)]) for t in range(REP)]
        tiles = [
            qs[0],
            jnp.where(low, qs[1], keys[0]),
            jnp.where(low, vals[0], qs[1]),
            qs[2],
            jnp.where(low, keys[1], vals[1]),
        ]
        for i, vals_of in enumerate(tiles):
            out_ref[to, 128 * i : 128 * (i + 1)] = vals_of.astype(BF16)


def attn_backward(here, grads, q_rows, key_rows, value_rows, lse, cos, sin, starts, chunks):
    total = q_rows.shape[0]
    cols = 2 * (REP + 2) * HD
    return pl.pallas_call(
        functools.partial(attn_backward_body, chunks),
        in_specs=[pl.BlockSpec(memory_space=pltpu.SMEM)]
        + [pl.BlockSpec(memory_space=pltpu.VMEM)] * 8,
        out_specs=pl.BlockSpec(memory_space=pltpu.VMEM),
        out_shape=jax.ShapeDtypeStruct((total, cols), BF16),
        scratch_shapes=[
            pltpu.VMEM((total, 256), F32),
            pltpu.VMEM((total, 256), F32),
            pltpu.VMEM((total, 2 * REP * HD), F32),
        ],
        compiler_params=pltpu.CompilerParams(vmem_limit_bytes=48 * 1024 * 1024),
        cost_estimate=pl.CostEstimate(
            flops=12 * total * total * cols, bytes_accessed=8 * total * cols, transcendentals=0
        ),
        name="attn_backward",
    )(here, grads, q_rows, key_rows, value_rows, lse, cos, sin, starts)


def rope_rows(positions):
    freq_index = jnp.arange(HD // 2, dtype=F32)
    inverse = jnp.exp(freq_index * (-2.0 * math.log(10000.0) / HD))
    angles = positions.astype(F32)[:, None] * inverse[None, :]
    return jnp.tile(jnp.cos(angles), (1, 4)), jnp.tile(jnp.sin(angles), (1, 4))


def seq_layout(block_lengths, block_tok):
    seq_ends = jnp.cumsum(block_lengths)
    starts = seq_ends - block_lengths
    places = jnp.arange(block_tok, dtype=jnp.int32)
    segment = jnp.sum((places[:, None] >= seq_ends[None, :]).astype(jnp.int32), axis=1)
    owners = segment[:, None] == jnp.arange(block_lengths.shape[0], dtype=jnp.int32)[None, :]
    offset = jnp.sum(jnp.where(owners, starts[None, :], 0), axis=1)
    return places - offset, offset


def norm_apply(row_vals, gain_vec):
    scale_row = lax.rsqrt(jnp.mean(row_vals * row_vals, axis=1, keepdims=True) + EPSILON)
    return row_vals * scale_row * gain_vec


def norm_back(row_vals, gain_vec, grad):
    scale_row = lax.rsqrt(jnp.mean(row_vals * row_vals, axis=1, keepdims=True) + EPSILON)
    weighted = grad * gain_vec
    inner = jnp.mean(weighted * row_vals, axis=1, keepdims=True)
    return scale_row * weighted - row_vals * (scale_row * scale_row * scale_row * inner)


def shift(values, axis, by):
    size = lax.axis_size(axis)
    return lax.ppermute(values, axis, [(i, (i + by) % size) for i in range(size)])


def swap(values, axis, bit):
    size = lax.axis_size(axis)
    return lax.ppermute(values, axis, [(i, i ^ bit) for i in range(size)])


def sum_everywhere(values, axes):
    for axis in axes:
        bit = 1
        while bit < lax.axis_size(axis):
            values = values + swap(values, axis, bit)
            bit *= 2
    return values


def shards(
    hidden_in,
    norm_gain_attn,
    norm_gain_moe,
    w_qkv,
    w_out,
    router,
    w_in,
    w_down,
    lengths,
    routes,
    out_grad,
):
    tok, feat = hidden_in.shape
    cols = lax.axis_size("col")
    rows = lax.axis_size("row")
    block_tok = tok * cols
    experts = router.shape[1]
    sources = rows * cols
    local = w_in.shape[0]
    cap = tok * TOP * 2 // experts
    head_cols = w_out.shape[1]
    plane = ("row", "col")
    here = lax.axis_index("col").astype(jnp.int32).reshape(1)
    first = (lax.axis_index(plane) * local).astype(jnp.int32).reshape(1)
    rows_in = hidden_in.astype(F32)
    grad_out = out_grad.astype(F32)

    normed_attn = norm_apply(rows_in, norm_gain_attn).astype(BF16)
    parts = [normed_attn]
    for _ in range(cols - 1):
        parts.append(shift(parts[-1], "col", 1))
    qkv_own = lax.all_gather(w_qkv, ("dp", "row"), axis=0, tiled=True)
    out_line = jnp.concatenate([w_out] + [shift(w_out, "col", -k) for k in range(1, cols)], axis=1)
    out_full = lax.all_gather(out_line, ("dp", "row"), axis=0, tiled=True)
    dy_all = lax.all_gather(out_grad, plane, axis=0, tiled=True)
    rt_all = lax.all_gather(routes.T, plane, axis=0)

    positions, seq_start = seq_layout(lengths[0], block_tok)
    cos, sin = rope_rows(positions)
    starts = jnp.pad(seq_start.reshape(cols, tok), ((0, -cols % 8), (0, 0)))
    q_rows, key_rows, value_rows, lse, heads_block = attn_forward(
        here, parts, qkv_own, cos, sin, starts
    )
    heads = jnp.concatenate(
        [
            shift(heads_block[k * tok : (k + 1) * tok], "col", -k) if k else heads_block[:tok]
            for k in range(cols)
        ],
        axis=1,
    )
    middle = rows_in + dot_nt(heads, out_full)
    normed_moe = norm_apply(middle, norm_gain_moe).astype(BF16)

    x_all = lax.all_gather(normed_moe, plane, axis=0, tiled=True)
    res_part, gn_part, dg, dwi, dwd = moe_experts(
        first, x_all, dy_all, rt_all, split_router(router), w_in, w_down, cap
    )
    if lax.axis_size("dp") == 2:
        grad_w_in = dwi.astype(F32) + swap(dwi, "dp", 1).astype(F32)
        grad_w_down = dwd.astype(F32) + swap(dwd, "dp", 1).astype(F32)
    else:
        grad_w_in = lax.psum(dwi, "dp").astype(F32)
        grad_w_down = lax.psum(dwd, "dp").astype(F32)

    normed_wide = normed_moe.astype(F32)
    logits = jnp.dot(normed_wide, router, precision=HIGHEST, preferred_element_type=F32)
    expert_ids = jnp.arange(experts, dtype=jnp.int32)
    used = jnp.any(routes[:, :, None] == expert_ids[None, None, :], axis=1)
    top = jnp.max(jnp.where(used, logits, MASKED_SCORE), axis=1, keepdims=True)
    terms = jnp.where(used, jnp.exp(logits - top), 0.0)
    gates = terms / jnp.sum(terms, axis=1, keepdims=True)
    dg_back = lax.all_to_all(dg, plane, split_axis=0, concat_axis=0, tiled=True)
    grad_gates = dg_back[:, :local].reshape(experts, tok).T
    grad_logits = gates * (grad_gates - jnp.sum(gates * grad_gates, axis=1, keepdims=True))
    router_term = lax.dot_general(
        grad_logits, router, (((1,), (1,)), ((), ())), precision=HIGHEST, preferred_element_type=F32
    )
    grad_router = lax.dot_general(
        normed_wide, grad_logits, (((0,), (0,)), ((), ())), precision=HIGHEST, preferred_element_type=F32
    )

    gn = lax.psum_scatter(gn_part, plane, scatter_dimension=0, tiled=True)
    grad_nm = gn.astype(F32) + router_term
    grad_middle = grad_out + norm_back(middle, norm_gain_moe, grad_nm)
    middle_scale = lax.rsqrt(jnp.mean(middle * middle, axis=1, keepdims=True) + EPSILON)
    gain_moe_part = jnp.sum(grad_nm * middle * middle_scale, axis=0)
    grad_attn = grad_middle.astype(BF16)

    grad_heads = dot_nn(grad_attn, out_full).astype(BF16)
    grads_block = jnp.concatenate(
        [
            shift(grad_heads[:, k * head_cols : (k + 1) * head_cols], "col", k)
            if k
            else grad_heads[:, :head_cols]
            for k in range(cols)
        ],
        axis=0,
    )
    res = lax.psum_scatter(res_part, plane, scatter_dimension=0, tiled=True)
    result = middle + res.astype(F32)

    grad_mixed = attn_backward(
        here, grads_block, q_rows, key_rows, value_rows, lse, cos, sin, starts, cols
    )
    mixed_back = [
        shift(grad_mixed[k * tok : (k + 1) * tok], "col", -k) if k else grad_mixed[:tok]
        for k in range(cols)
    ]
    qkv_line = jnp.concatenate([shift(w_qkv, "col", -k) for k in range(1, cols)], axis=1)
    qkv_rest = lax.all_gather(qkv_line, ("dp", "row"), axis=0, tiled=True)
    grad_na = dot_nt(mixed_back[0], qkv_own) + dot_nt(
        jnp.concatenate(mixed_back[1:], axis=1), qkv_rest
    )
    grad_hidden = grad_middle + norm_back(rows_in, norm_gain_attn, grad_na)

    block_rows = jnp.concatenate(parts, axis=0)
    w_qkv_part = dot_tn(block_rows, grad_mixed)
    gain_attn_part = jnp.sum(w_qkv_part * qkv_own.astype(F32), axis=1) / norm_gain_attn
    grad_parts = [grad_attn]
    for _ in range(cols - 1):
        grad_parts.append(shift(grad_parts[-1], "col", 1))
    w_out_part = dot_tn(jnp.concatenate(grad_parts, axis=0), heads_block)

    grad_w_qkv = lax.psum_scatter(
        w_qkv_part.astype(BF16), ("dp", "row"), scatter_dimension=0, tiled=True
    ).astype(F32)
    grad_w_out = lax.psum_scatter(
        w_out_part.astype(BF16), ("dp", "row"), scatter_dimension=0, tiled=True
    ).astype(F32)
    axes = ("row", "col", "dp")
    grad_router_all = sum_everywhere(grad_router, axes)
    gains = sum_everywhere(jnp.stack([gain_attn_part, gain_moe_part]), axes)
    return (
        result,
        grad_hidden,
        gains[0],
        gains[1],
        grad_w_qkv,
        grad_w_out,
        grad_router_all,
        grad_w_in,
        grad_w_down,
    )


def solution(mesh):
    in_specs = (
        P(("dp", "row", "col"), None),
        P(),
        P(),
        P(("dp", "row"), "col"),
        P(("dp", "row"), "col"),
        P(),
        P(("row", "col"), None, None),
        P(("row", "col"), None, None),
        P(("dp", "row"), None),
        P(("dp", "row", "col"), None),
        P(("dp", "row", "col"), None),
    )
    out_specs = (
        P(("dp", "row", "col"), None),
        P(("dp", "row", "col"), None),
        P(),
        P(),
        P(("dp", "row"), "col"),
        P(("dp", "row"), "col"),
        P(),
        P(("row", "col"), None, None),
        P(("row", "col"), None, None),
    )
    return jax.shard_map(shards, mesh=mesh, in_specs=in_specs, out_specs=out_specs, check_vma=False)
```

time: 2160 us -> 908 us (0.42)
  waiting for transfers between devices: 1260 us -> 565 us
  blocking collectives: 320 us -> 34 us
  matrix products: 219 us -> 30.1 us
  local copies, waits for them, and re-layouts: 183 us -> 21.2 us
  Pallas kernels: 0 us -> 114 us
  other arithmetic: 125 us -> 40.8 us
  starting transfers between devices: 15.7 us -> 81.9 us
    all_to_all x3 -> x1, waiting for transfers between devices: 741 us -> 6.47 us  [shards(): dg_back = lax.all_to_all(dg, plane, split_axis=0, concat_axis=0, tiled=True)]
    all_to_all x1 -> x0, blocking collectives: 280 us -> none  [shards(): lax.all_to_all(pack_rows(), ('row', 'col'), split_axis=0, concat_axis=0,...]
    ppermute x0 -> x33, waiting for transfers between devices: none -> 261 us  [the longest x21 200 us: shift(): lax.ppermute(values, axis, [(i, (i + by) % size) for i in range(size)])]
    dot_general x27 -> x7, matrix products: 215 us -> 26 us  [the longest x3 11 us: dot_nt(): lax.dot_general(left, right, (((1,), (1,)), ((), ())), preferred_element_...]
    psum x2 -> x0, waiting for transfers between devices: 148 us -> none  [the longest x1 80.6 us: shards(): lax.psum((grad_gain_attn, grad_gain_moe, grad_router), ('dp', 'row', 'col'))]
    pallas_call x0 -> x3, Pallas kernels: none -> 114 us  [the longest x1 87.6 us: moe_experts(): pl.pallas_call(functools.partial(moe_body, cap, tile, tiles), grid_spec=p...]
    reduce_scatter x4 -> x3, waiting for transfers between devices: 252 us -> 142 us  [the longest x1 103 us: shards(): gn = lax.psum_scatter(gn_part, plane, scatter_dimension=0, tiled=True)]
    gather x4 -> x0, local copies, waits for them, and re-layouts: 94.8 us -> none  [the longest x1 28.8 us: shards(): pair_grads[source_pair]]
  transfers between devices with their start and end apart: 13 -> 43, of which waited for: 12 -> 22; matrix products, arithmetic and copies ran while one was open for 17% -> 9% of each run, Pallas kernels for 0% -> 3%
where the time goes in v1:
time: 908 us; the launch traced here: 902 us
  waiting for transfers between devices  565 us (62%)
  Pallas kernels  114 us (13%)
  starting transfers between devices  81.9 us (9%)
  other arithmetic  40.8 us (4%)
  blocking collectives  34 us (4%)
  matrix products  30.1 us (3%)
  local copies, waits for them, and re-layouts  21.2 us (2%)
  between operations  14.9 us (2%)
    ppermute x21, waiting for transfers between devices, shift(): lax.ppermute(values, axis, [(i, (i + by) % size) for i in range(size)])  200 us
    reduce_scatter x1, waiting for transfers between devices, shards(): gn = lax.psum_scatter(gn_part, plane, scatter_dimension=0, tiled=True)  103 us
    all_gather x1, waiting for transfers between devices, shards(): x_all = lax.all_gather(normed_moe, plane, axis=0, tiled=True)  102 us
    pallas_call x1, Pallas kernels, moe_experts(): pl.pallas_call(functools.partial(moe_body, cap, tile, tiles), grid_spec=p...  87.6 us
    ppermute x12, waiting for transfers between devices, swap(): return lax.ppermute(values, axis, [(i, i ^ bit) for i in range(size)])  60.6 us
    ppermute x21, starting transfers between devices, shift(): lax.ppermute(values, axis, [(i, (i + by) % size) for i in range(size)])  50.3 us
    reduce_scatter x1, waiting for transfers between devices, shards(): lax.psum_scatter(w_out_part.astype(BF16), ('dp', 'row'), scatter_dimensio...  38.3 us
    all_gather x1, blocking collectives, shards(): rt_all = lax.all_gather(routes.T, plane, axis=0)  34 us
  transfers between devices with their start and end apart: 43, of which 22 were waited for; matrix products, arithmetic and copies ran while one was open for 9% of the time, Pallas kernels for 3%

profile of v1, /device:TPU:0, one launch (start us, length us, event | category | flops | bytes accessed | tf_op | source)
XLA Modules:
  0.0 902.0 jit_solution(4863494518935616385)
XLA Ops:
  8.0 5.1 collective-permute-start.6
  17.7 8.1 collective-permute-done.7
  29.9 19.7 %collective-permute-done.refs_1_ = bf16[256,1536]{1,0:T(8,128)(2,1)S(1)} collective-permute-done((bf16[256,1536]{1,0:T(8,128)(2,1)S(1)}, bf16[256,1536]{1,0:T(8,128)(2,1)S(1)}, u32[]{:S(2)}, u32[]{:S(2)}) %collective-permute-start) | collective-permute-done | bytes 786464 | tf_op jit(solution)/shard_map/ppermute | solution.py:483
  49.8 19.5 %collective-permute-done.1.refs_2_ = bf16[256,1536]{1,0:T(8,128)(2,1)S(1)} collective-permute-done((bf16[256,1536]{1,0:T(8,128)(2,1)S(1)}, bf16[256,1536]{1,0:T(8,128)(2,1)S(1)}, u32[]{:S(2)}, u32[]{:S(2)}) %collective-permute-start.1) | collective-permute-done | bytes 786464 | tf_op jit(solution)/shard_map/ppermute | solution.py:483
  74.0 14.2 %collective-permute-done.2.refs_3_ = bf16[256,1536]{1,0:T(8,128)(2,1)} collective-permute-done((bf16[256,1536]{1,0:T(8,128)(2,1)S(1)}, bf16[256,1536]{1,0:T(8,128)(2,1)}, u32[]{:S(2)}, u32[]{:S(2)}) %collective-permute-start.2) | collective-permute-done | bytes 786464 | tf_op jit(solution)/shard_map/ppermute | solution.py:483
  89.3 11.9 %attn_forward.1 = (bf16[1024,768]{1,0:T(8,128)(2,1)}, bf16[1024,256]{1,0:T(8,128)(2,1)S(1)}, bf16[1024,256]{1,0:T(8,128)(2,1)S(1)}, f32[6,8,256]{2,1,0:T(8,128)S(1)}, bf16[1024,384]{1,0:T(8,128)(2,1)S(1)}) custom-call(s32[1]{0:T(128)} %bitcast.here_ref, bf16[256,1536]{1,0:T(8,128)(2,1)S(1)} %fusion.22.refs_0_, ...), custom_call_target="tpu_custom_call" | custom-call | flops 8053063680 | bytes 5242880 | tf_op jit(solution)/shard_map/attn_forward/pallas_call | solution.py:348
  105.3 10.2 %collective-permute-done.3 = bf16[256,384]{1,0:T(8,128)(2,1)S(1)} collective-permute-done((bf16[256,384]{1,0:T(8,128)(2,1)S(1)}, bf16[256,384]{1,0:T(8,128)(2,1)S(1)}, u32[]{:S(2)}, u32[]{:S(2)}) %collective-permute-start.3) | collective-permute-done | bytes 196640 | tf_op jit(solution)/shard_map/ppermute | solution.py:483
  115.5 22.6 %collective-permute-done.4 = bf16[256,384]{1,0:T(8,128)(2,1)S(1)} collective-permute-done((bf16[256,384]{1,0:T(8,128)(2,1)S(1)}, bf16[256,384]{1,0:T(8,128)(2,1)S(1)}, u32[]{:S(2)}, u32[]{:S(2)}) %collective-permute-start.4) | collective-permute-done | bytes 196640 | tf_op jit(solution)/shard_map/ppermute | solution.py:483
  145.2 34.0 %all-gather = s32[128,256]{1,0:T(8,128)} all-gather(s32[8,256]{1,0:T(8,128)S(1)} %bitcast.53), channel_id=2, replica_groups=mesh['dp'=2,'row'=4,'col'=4] {'row','col'}, dimensions={0}, use_global_device_ids=true | all-gather | bytes 139264 | tf_op jit(solution)/shard_map/all_gather | solution.py:536
  180.0 21.3 %all-gather.13.cloned.1.call-done.dy_ref = bf16[4096,1536]{1,0:T(8,128)(2,1)} async-done(((bf16[256,1536]{1,0:T(8,128)(2,1)}), bf16[4096,1536]{1,0:T(8,128)(2,1)}) %all-gather.13.cloned.1.call-update) | async-done | bytes 12582928 | tf_op jit(solution)/shard_map/all_gather | solution.py:535
  201.3 102.3 %all-gather.11.cloned.1.call-done.x_ref = bf16[4096,1536]{1,0:T(8,128)(2,1)} async-done(((bf16[256,1536]{1,0:T(8,128)(2,1)}), bf16[4096,1536]{1,0:T(8,128)(2,1)}) %all-gather.11.cloned.1.call-update) | async-done | bytes 12582928 | tf_op jit(solution)/shard_map/all_gather | solution.py:554
  303.6 87.6 %moe_experts.1 = (bf16[4096,1536]{1,0:T(8,128)(2,1)}, bf16[4096,1536]{1,0:T(8,128)(2,1)}, f32[16,8,256]{2,1,0:T(8,128)}, bf16[2,1536,1024]{2,1,0:T(8,128)(2,1)}, bf16[2,512,1536]{2,1,0:T(8,128)(2,1)}) custom-call(s32[1]{0:T(128)} %bitcast.7.first_ref, bf16[4096,1536]{1,0:T(8,128)(2,1)} %all-gather.11.cloned.1.call-done.x_ref, ...), custom_call_target="tpu_custom_call" | custom-call | flops 28991029248 | bytes 62914560 | tf_op jit(solution)/shard_map/moe_experts/pallas_call | solution.py:191
  392.1 5.6 collective-permute-start.16
  400.5 16.5 %collective-permute-done.16 = bf16[192,640]{1,0:T(8,128)(2,1)S(1)} collective-permute-done((bf16[192,640]{1,0:T(8,128)(2,1)S(1)}, bf16[192,640]{1,0:T(8,128)(2,1)S(1)}, u32[]{:S(2)}, u32[]{:S(2)}) %collective-permute-start.16) | collective-permute-done | bytes 245792 | tf_op jit(solution)/shard_map/ppermute | solution.py:483
  418.7 19.0 %all-to-all-start = ((f32[16,8,256]{2,1,0:T(8,128)}), f32[16,8,256]{2,1,0:T(8,128)S(1)}, u32[]{:S(2)}, u32[]{:S(2)}) async-start(f32[16,8,256]{2,1,0:T(8,128)} %get-tuple-element.22), calls=%async_computation.2 | async-start | bytes 262144 | tf_op jit(solution)/shard_map/all_to_all | solution.py:572
  438.6 6.5 all-to-all-done
  448.3 8.3 collective-permute-done.27
  456.7 103.4 %reduce-scatter.9.cloned.1.call-done = bf16[256,1536]{1,0:T(8,128)(2,1)} async-done(((bf16[4096,1536]{1,0:T(8,128)(2,1)}), bf16[256,1536]{1,0:T(8,128)(2,1)}) %reduce-scatter.9.cloned.1.call-update) | async-done | bytes 786448 | tf_op jit(solution)/shard_map/reduce_scatter | solution.py:582
  572.4 9.0 collective-permute-start.9
  589.9 14.2 %attn_backward.1 = bf16[1024,640]{1,0:T(8,128)(2,1)S(1)} custom-call(s32[1]{0:T(128)} %bitcast.here_ref, bf16[1024,384]{1,0:T(8,128)(2,1)S(1)} %pad_maximum_fusion.grads_ref, bf16[1024,768]{1,0:T(8,128)(2,1)S(1)} %copy-done.7, bf16[1024,256]{1,0:T(8,128)(2,1)S(1)} %copy-done.9, bf16[1024,256]{1,0:T(8,128)(2,1)S(1)} %copy-done.11, ...), custom_call_target="tpu_custom_call" | custom-call | flops 8053063680 | bytes 5242880 | tf_op jit(solution)/shard_map/attn_backward/pallas_call | solution.py:433
  604.1 6.0 fusion.63
  610.1 5.4 copy.41
  626.9 52.3 %collective-permute-done.30 = f32[1536,32]{0,1:T(8,128)S(1)} collective-permute-done((f32[1536,32]{0,1:T(8,128)S(1)}, f32[1536,32]{0,1:T(8,128)S(1)}, u32[]{:S(2)}, u32[]{:S(2)}) %collective-permute-start.30) | collective-permute-done | bytes 196640 | tf_op jit(solution)/shard_map/ppermute | solution.py:488
  686.1 6.5 convert_add_fusion.1
  693.5 30.4 %collective-permute-done.24 = bf16[256,1536]{1,0:T(8,128)(2,1)S(1)} collective-permute-done((bf16[256,1536]{1,0:T(8,128)(2,1)}, bf16[256,1536]{1,0:T(8,128)(2,1)S(1)}, u32[]{:S(2)}, u32[]{:S(2)}) %collective-permute-start.24) | collective-permute-done | bytes 786464 | tf_op jit(solution)/shard_map/ppermute | solution.py:483
  723.9 12.7 %collective-permute-start.25 = (bf16[256,1536]{1,0:T(8,128)(2,1)S(1)}, bf16[256,1536]{1,0:T(8,128)(2,1)S(1)}, u32[]{:S(2)}, u32[]{:S(2)}) collective-permute-start(bf16[256,1536]{1,0:T(8,128)(2,1)S(1)} %collective-permute-done.24), channel_id=1, source_target_pairs={{0,1},{1,2},{2,3},{3,0},{4,5},{5,6},{6,7},{7,4},{8,9},{9,10},{10,1... | collective-permute-start | bytes 2359304 | tf_op jit(solution)/shard_map/ppermute | solution.py:483
  736.5 12.7 %convert_add_fusion = f32[2,1536,1024]{2,1,0:T(8,128)} fusion(bf16[2,1536,1024]{2,1,0:T(8,128)(2,1)} %collective-permute-done.31, bf16[2,1536,1024]{2,1,0:T(8,128)(2,1)} %get-tuple-element.27), kind=kLoop, calls=%fused_computation | loop fusion | flops 9437184 | bytes 25165824 | tf_op jit(solution)/shard_map/add | solution.py:559
  762.4 12.9 %collective-permute-done.12 = bf16[256,640]{1,0:T(8,128)(2,1)} collective-permute-done((bf16[256,640]{1,0:T(8,128)(2,1)S(1)}, bf16[256,640]{1,0:T(8,128)(2,1)}, u32[]{:S(2)}, u32[]{:S(2)}) %collective-permute-start.12) | collective-permute-done | bytes 327712 | tf_op jit(solution)/shard_map/ppermute | solution.py:483
  775.3 35.1 %collective-permute-done.13 = bf16[256,640]{1,0:T(8,128)(2,1)} collective-permute-done((bf16[256,640]{1,0:T(8,128)(2,1)S(1)}, bf16[256,640]{1,0:T(8,128)(2,1)}, u32[]{:S(2)}, u32[]{:S(2)}) %collective-permute-start.13) | collective-permute-done | bytes 327712 | tf_op jit(solution)/shard_map/ppermute | solution.py:483
  817.3 5.1 fusion.25
  822.4 30.6 %reduce-scatter.13.cloned.1.call-done = bf16[192,640]{1,0:T(8,128)(2,1)} async-done(((bf16[1536,640]{1,0:T(8,128)(2,1)}), bf16[192,640]{1,0:T(8,128)(2,1)}) %reduce-scatter.13.cloned.1.call-update) | async-done | bytes 245776
  855.1 38.3 %reduce-scatter.11.cloned.1.call-done = bf16[192,384]{1,0:T(8,128)(2,1)} async-done(((bf16[1536,384]{1,0:T(8,128)(2,1)}), bf16[192,384]{1,0:T(8,128)(2,1)}) %reduce-scatter.11.cloned.1.call-update) | async-done | bytes 147472 | tf_op jit(solution)/shard_map/reduce_scatter | solution.py:627
  (193 shorter events, 100.1 us)
Async XLA Ops:
  7.2 81.0 %all-gather.7.cloned.1.call-start = ((), (), s32[]{:S(2)}) async-start(), calls=%async_computation.5 | async-start | bytes 2211840 | tf_op jit(solution)/shard_map/all_gather | solution.py:532
  7.9 130.9 %all-gather.9.cloned.1.call-start = ((), (), s32[]{:S(2)}) async-start(), calls=%async_computation.6 | async-start | bytes 5308416 | tf_op jit(solution)/shard_map/all_gather | solution.py:534
  27.6 173.7 %all-gather.13.cloned.1.call-start = ((), (), s32[]{:S(2)}) async-start(), calls=%async_computation.8 | async-start | bytes 13369344 | tf_op jit(solution)/shard_map/all_gather | solution.py:535
  28.3 275.3 %all-gather.11.cloned.1.call-start = ((), (), s32[]{:S(2)}) async-start(), calls=%async_computation.7 | async-start | bytes 13369344 | tf_op jit(solution)/shard_map/all_gather | solution.py:554
  28.9 20.7 %collective-permute-start = (bf16[256,1536]{1,0:T(8,128)(2,1)S(1)}, bf16[256,1536]{1,0:T(8,128)(2,1)S(1)}, u32[]{:S(2)}, u32[]{:S(2)}) collective-permute-start(bf16[256,1536]{1,0:T(8,128)(2,1)S(1)} %fusion.22.refs_0_), channel_id=1, source_target_pairs={{0,1},{1,2},{2,3},{3,0},{4,5},{5,6},{6,7},{7,4},{8,9},{9,10},{10,1... | collective-permute-start | bytes 2359304 | tf_op jit(solution)/shard_map/ppermute | solution.py:483
  49.6 19.7 %collective-permute-start.1 = (bf16[256,1536]{1,0:T(8,128)(2,1)S(1)}, bf16[256,1536]{1,0:T(8,128)(2,1)S(1)}, u32[]{:S(2)}, u32[]{:S(2)}) collective-permute-start(bf16[256,1536]{1,0:T(8,128)(2,1)S(1)} %collective-permute-done.refs_1_), channel_id=1, source_target_pairs={{0,1},{1,2},{2,3},{3,0},{4,5},{5,6},{6,7},{7,4},{8,9},{9,10},{10,1... | collective-permute-start | bytes 2359304 | tf_op jit(solution)/shard_map/ppermute | solution.py:483
  69.3 18.9 %collective-permute-start.2 = (bf16[256,1536]{1,0:T(8,128)(2,1)S(1)}, bf16[256,1536]{1,0:T(8,128)(2,1)}, u32[]{:S(2)}, u32[]{:S(2)}) collective-permute-start(bf16[256,1536]{1,0:T(8,128)(2,1)S(1)} %collective-permute-done.1.refs_2_), channel_id=1, source_target_pairs={{0,1},{1,2},{2,3},{3,0},{4,5},{5,6},{6,7},{7,4},{8,9},{9,10},{10,1... | collective-permute-start | bytes 2359304 | tf_op jit(solution)/shard_map/ppermute | solution.py:483
  103.0 35.1 %collective-permute-start.4 = (bf16[256,384]{1,0:T(8,128)(2,1)S(1)}, bf16[256,384]{1,0:T(8,128)(2,1)S(1)}, u32[]{:S(2)}, u32[]{:S(2)}) collective-permute-start(bf16[256,384]{1,0:T(8,128)(2,1)S(1)} %get-tuple-element.80), channel_id=1, source_target_pairs={{0,2},{1,3},{2,0},{3,1},{4,6},{5,7},{6,4},{7,5},{8,10},{9,11},{10,... | collective-permute-start | bytes 589832 | tf_op jit(solution)/shard_map/ppermute | solution.py:483
  103.1 35.7 %collective-permute-start.5 = (bf16[256,384]{1,0:T(8,128)(2,1)S(1)}, bf16[256,384]{1,0:T(8,128)(2,1)}, u32[]{:S(2)}, u32[]{:S(2)}) collective-permute-start(bf16[256,384]{1,0:T(8,128)(2,1)S(1)} %get-tuple-element.79), channel_id=1, source_target_pairs={{0,1},{1,2},{2,3},{3,0},{4,5},{5,6},{6,7},{7,4},{8,9},{9,10},{10,1... | collective-permute-start | bytes 589832 | tf_op jit(solution)/shard_map/ppermute | solution.py:483
  145.1 415.0 %reduce-scatter.9.cloned.1.call-start = ((), (), s32[]{:S(2)}) async-start(), calls=%async_computation.10 | async-start | bytes 13369344 | tf_op jit(solution)/shard_map/reduce_scatter | solution.py:582
  391.2 371.1 %all-gather.15.cloned.1.call-start = ((), (), s32[]{:S(2)}) async-start(), calls=%async_computation.11 | async-start | bytes 6635520 | tf_op jit(solution)/shard_map/all_gather | solution.py:610
  392.1 24.8 %collective-permute-start.16 = (bf16[192,640]{1,0:T(8,128)(2,1)S(1)}, bf16[192,640]{1,0:T(8,128)(2,1)S(1)}, u32[]{:S(2)}, u32[]{:S(2)}) collective-permute-start(bf16[192,640]{1,0:T(8,128)(2,1)S(1)} %copy-done.23), channel_id=1, source_target_pairs={{0,2},{1,3},{2,0},{3,1},{4,6},{5,7},{6,4},{7,5},{8,10},{9,11},{10,... | collective-permute-start | bytes 737288 | tf_op jit(solution)/shard_map/ppermute | solution.py:483
  397.8 19.2 %collective-permute-start.17 = (bf16[192,640]{1,0:T(8,128)(2,1)S(1)}, bf16[192,640]{1,0:T(8,128)(2,1)S(1)}, u32[]{:S(2)}, u32[]{:S(2)}) collective-permute-start(bf16[192,640]{1,0:T(8,128)(2,1)S(1)} %copy-done.23), channel_id=1, source_target_pairs={{0,1},{1,2},{2,3},{3,0},{4,5},{5,6},{6,7},{7,4},{8,9},{9,10},{10,1... | collective-permute-start | bytes 737288 | tf_op jit(solution)/shard_map/ppermute | solution.py:483
  418.0 399.4 %reduce-scatter.7.cloned.1.call-start = ((), (), s32[]{:S(2)}) async-start(), calls=%async_computation.9 | async-start | bytes 13369344 | tf_op jit(solution)/shard_map/reduce_scatter | solution.py:599
  418.7 26.3 %all-to-all-start = ((f32[16,8,256]{2,1,0:T(8,128)}), f32[16,8,256]{2,1,0:T(8,128)S(1)}, u32[]{:S(2)}, u32[]{:S(2)}) async-start(f32[16,8,256]{2,1,0:T(8,128)} %get-tuple-element.22), calls=%async_computation.2 | async-start | bytes 262144 | tf_op jit(solution)/shard_map/all_to_all | solution.py:572
  437.7 415.3 %reduce-scatter.13.cloned.1.call-start = ((), (), s32[]{:S(2)}) async-start(), calls=%async_computation.13 | async-start | bytes 2211840
  445.8 290.7 %collective-permute-start.31 = (bf16[2,1536,1024]{2,1,0:T(8,128)(2,1)}, bf16[2,1536,1024]{2,1,0:T(8,128)(2,1)}, u32[]{:S(2)}, u32[]{:S(2)}) collective-permute-start(bf16[2,1536,1024]{2,1,0:T(8,128)(2,1)} %get-tuple-element.27), channel_id=1, source_target_pairs={{0,16},{16,0},{1,17},{17,1},{2,18},{18,2},{3,19},{19,3},{4,20},{20... | collective-permute-start | bytes 18874376 | tf_op jit(solution)/shard_map/ppermute | solution.py:488
  456.6 124.7 %collective-permute-start.28 = (f32[1536,32]{0,1:T(8,128)S(1)}, f32[1536,32]{0,1:T(8,128)}, u32[]{:S(2)}, u32[]{:S(2)}) collective-permute-start(f32[1536,32]{0,1:T(8,128)S(1)} %add.107), channel_id=1, source_target_pairs={{0,1},{1,0},{2,3},{3,2},{4,5},{5,4},{6,7},{7,6},{8,9},{9,8},{10,11... | collective-permute-start | bytes 589832 | tf_op jit(solution)/shard_map/ppermute | solution.py:488
  569.3 15.2 %collective-permute-start.10 = (bf16[256,384]{1,0:T(8,128)(2,1)S(1)}, bf16[256,384]{1,0:T(8,128)(2,1)S(1)}, u32[]{:S(2)}, u32[]{:S(2)}) collective-permute-start(bf16[256,384]{1,0:T(8,128)(2,1)S(1)} %get-tuple-element.76), channel_id=1, source_target_pairs={{0,2},{1,3},{2,0},{3,1},{4,6},{5,7},{6,4},{7,5},{8,10},{9,11},{10,... | collective-permute-start | bytes 589832 | tf_op jit(solution)/shard_map/ppermute | solution.py:483
  572.4 17.4 %collective-permute-start.9 = (bf16[256,384]{1,0:T(8,128)(2,1)S(1)}, bf16[256,384]{1,0:T(8,128)(2,1)S(1)}, u32[]{:S(2)}, u32[]{:S(2)}) collective-permute-start(bf16[256,384]{1,0:T(8,128)(2,1)S(1)} %get-tuple-element.77), channel_id=1, source_target_pairs={{0,1},{1,2},{2,3},{3,0},{4,5},{5,6},{6,7},{7,4},{8,9},{9,10},{10,1... | collective-permute-start | bytes 589832 | tf_op jit(solution)/shard_map/ppermute | solution.py:483
  581.4 104.8 %collective-permute-start.32 = (bf16[2,512,1536]{2,1,0:T(8,128)(2,1)}, bf16[2,512,1536]{2,1,0:T(8,128)(2,1)}, u32[]{:S(2)}, u32[]{:S(2)}) collective-permute-start(bf16[2,512,1536]{2,1,0:T(8,128)(2,1)} %get-tuple-element.28), channel_id=1, source_target_pairs={{0,16},{16,0},{1,17},{17,1},{2,18},{18,2},{3,19},{19,3},{4,20},{20... | collective-permute-start | bytes 9437192 | tf_op jit(solution)/shard_map/ppermute | solution.py:488
  584.5 34.4 %collective-permute-start.29 = (f32[1536,32]{0,1:T(8,128)}, f32[1536,32]{0,1:T(8,128)}, u32[]{:S(2)}, u32[]{:S(2)}) collective-permute-start(f32[1536,32]{0,1:T(8,128)} %add.108), channel_id=1, source_target_pairs={{0,2},{1,3},{2,0},{3,1},{4,6},{5,7},{6,4},{7,5},{8,10},{9,11},{10,... | collective-permute-start | bytes 589832 | tf_op jit(solution)/shard_map/ppermute | solution.py:488
  620.0 59.3 %collective-permute-start.30 = (f32[1536,32]{0,1:T(8,128)S(1)}, f32[1536,32]{0,1:T(8,128)S(1)}, u32[]{:S(2)}, u32[]{:S(2)}) collective-permute-start(f32[1536,32]{0,1:T(8,128)S(1)} %add.109), channel_id=1, source_target_pairs={{0,16},{16,0},{1,17},{17,1},{2,18},{18,2},{3,19},{19,3},{4,20},{20... | collective-permute-start | bytes 589832 | tf_op jit(solution)/shard_map/ppermute | solution.py:488
  621.7 63.0 %collective-permute-start.23 = (bf16[256,1536]{1,0:T(8,128)(2,1)}, bf16[256,1536]{1,0:T(8,128)(2,1)}, u32[]{:S(2)}, u32[]{:S(2)}) collective-permute-start(bf16[256,1536]{1,0:T(8,128)(2,1)} %fusion.59), channel_id=1, source_target_pairs={{0,1},{1,2},{2,3},{3,0},{4,5},{5,6},{6,7},{7,4},{8,9},{9,10},{10,1... | collective-permute-start | bytes 2359304 | tf_op jit(solution)/shard_map/ppermute | solution.py:483
  625.4 58.6 %collective-permute-start.19 = (f32[2,1536]{1,0:T(2,128)S(1)}, f32[2,1536]{1,0:T(2,128)S(1)}, u32[]{:S(2)}, u32[]{:S(2)}) collective-permute-start(f32[2,1536]{1,0:T(2,128)S(1)} %fusion.56), channel_id=1, source_target_pairs={{0,8},{4,12},{8,0},{12,4},{1,9},{5,13},{9,1},{13,5},{2,10},{6,14},... | collective-permute-start | bytes 36872 | tf_op jit(solution)/shard_map/ppermute | solution.py:488
  684.0 209.4 %reduce-scatter.11.cloned.1.call-start = ((), (), s32[]{:S(2)}) async-start(), calls=%async_computation.12 | async-start | bytes 1327104 | tf_op jit(solution)/shard_map/reduce_scatter | solution.py:627
  684.8 39.1 %collective-permute-start.24 = (bf16[256,1536]{1,0:T(8,128)(2,1)}, bf16[256,1536]{1,0:T(8,128)(2,1)S(1)}, u32[]{:S(2)}, u32[]{:S(2)}) collective-permute-start(bf16[256,1536]{1,0:T(8,128)(2,1)} %collective-permute-done.23), channel_id=1, source_target_pairs={{0,1},{1,2},{2,3},{3,0},{4,5},{5,6},{6,7},{7,4},{8,9},{9,10},{10,1... | collective-permute-start | bytes 2359304 | tf_op jit(solution)/shard_map/ppermute | solution.py:483
  692.7 56.5 %collective-permute-start.21 = (f32[2,1536]{1,0:T(2,128)S(1)}, f32[2,1536]{1,0:T(2,128)S(1)}, u32[]{:S(2)}, u32[]{:S(2)}) collective-permute-start(f32[2,1536]{1,0:T(2,128)S(1)} %add.103), channel_id=1, source_target_pairs={{0,2},{1,3},{2,0},{3,1},{4,6},{5,7},{6,4},{7,5},{8,10},{9,11},{10,... | collective-permute-start | bytes 36872 | tf_op jit(solution)/shard_map/ppermute | solution.py:488
  723.9 34.2 %collective-permute-start.25 = (bf16[256,1536]{1,0:T(8,128)(2,1)S(1)}, bf16[256,1536]{1,0:T(8,128)(2,1)S(1)}, u32[]{:S(2)}, u32[]{:S(2)}) collective-permute-start(bf16[256,1536]{1,0:T(8,128)(2,1)S(1)} %collective-permute-done.24), channel_id=1, source_target_pairs={{0,1},{1,2},{2,3},{3,0},{4,5},{5,6},{6,7},{7,4},{8,9},{9,10},{10,1... | collective-permute-start | bytes 2359304 | tf_op jit(solution)/shard_map/ppermute | solution.py:483
  751.1 24.1 %collective-permute-start.12 = (bf16[256,640]{1,0:T(8,128)(2,1)S(1)}, bf16[256,640]{1,0:T(8,128)(2,1)}, u32[]{:S(2)}, u32[]{:S(2)}) collective-permute-start(bf16[256,640]{1,0:T(8,128)(2,1)S(1)} %get-tuple-element.71), channel_id=1, source_target_pairs={{0,3},{1,0},{2,1},{3,2},{4,7},{5,4},{6,5},{7,6},{8,11},{9,8},{10,9... | collective-permute-start | bytes 983048 | tf_op jit(solution)/shard_map/ppermute | solution.py:483
  753.7 56.6 %collective-permute-start.13 = (bf16[256,640]{1,0:T(8,128)(2,1)S(1)}, bf16[256,640]{1,0:T(8,128)(2,1)}, u32[]{:S(2)}, u32[]{:S(2)}) collective-permute-start(bf16[256,640]{1,0:T(8,128)(2,1)S(1)} %get-tuple-element.73), channel_id=1, source_target_pairs={{0,2},{1,3},{2,0},{3,1},{4,6},{5,7},{6,4},{7,5},{8,10},{9,11},{10,... | collective-permute-start | bytes 983048 | tf_op jit(solution)/shard_map/ppermute | solution.py:483
  754.9 55.4 %collective-permute-start.14 = (bf16[256,640]{1,0:T(8,128)(2,1)S(1)}, bf16[256,640]{1,0:T(8,128)(2,1)}, u32[]{:S(2)}, u32[]{:S(2)}) collective-permute-start(bf16[256,640]{1,0:T(8,128)(2,1)S(1)} %get-tuple-element.72), channel_id=1, source_target_pairs={{0,1},{1,2},{2,3},{3,0},{4,5},{5,6},{6,7},{7,4},{8,9},{9,10},{10,1... | collective-permute-start | bytes 983048 | tf_op jit(solution)/shard_map/ppermute | solution.py:483
  (40 other events, 672.8 us)
Sparse Core Ops, SparseCore 0:
  9.9 30.0 all-gather.6
  42.4 38.9 all-gather.8
  83.7 117.5 all-gather.12
  203.5 100.0 all-gather.10
  391.4 168.6 reduce-scatter.8
  561.8 66.9 all-gather.14
  632.8 178.2 reduce-scatter.6
  814.6 38.4 reduce-scatter.12
  856.6 36.7 reduce-scatter.10

commit v2 on v1

v2 whole, which is shorter than its diff:
```python
import functools
import math

import jax
import jax.numpy as jnp
from jax import lax
from jax.experimental import pallas as pl
from jax.experimental.pallas import tpu as pltpu
from jax.sharding import PartitionSpec as P

HD = 64
FFE = 512
TOP = 8
REP = 3
SEQ_MAX = 512

EPSILON = 1e-06
HIGHEST = lax.Precision.HIGHEST
MASKED_SCORE = -1e30
F32 = jnp.float32
BF16 = jnp.bfloat16


def dot_nn(left, right):
    return lax.dot_general(left, right, (((1,), (0,)), ((), ())), preferred_element_type=F32)


def dot_nt(left, right):
    return lax.dot_general(left, right, (((1,), (1,)), ((), ())), preferred_element_type=F32)


def dot_tn(left, right):
    return lax.dot_general(left, right, (((0,), (0,)), ((), ())), preferred_element_type=F32)


def hot_rows(srow, cap, tok):
    places = lax.broadcasted_iota(jnp.int32, (cap, tok), 0).astype(F32)
    return srow == places


def one_zero(mask):
    return jnp.where(mask, 1.0, 0.0).astype(BF16)


def front_body(
    cap, tile, tiles, group, sources,
    first_ref, ids_ref, *refs,
):
    x_refs = refs[:sources]
    (
        rt_ref, rs_ref, win_ref, wdn_ref, res_ref, rows_ref, gate_ref, slot_ref, offs_ref,
        buf, gate, run, arena, sems,
    ) = refs[sources:]
    step = pl.program_id(0)
    tok, feat = arena.shape[1:]
    experts = rs_ref.shape[0] // 3
    local = buf.shape[0]
    ff = wdn_ref.shape[1]
    first_work = sources // group

    def fetch(at):
        where = at % 2 * group
        return [
            pltpu.make_async_copy(x_refs[at * group + s], arena.at[where + s], sems.at[where + s])
            for s in range(group)
        ]

    @pl.when(step < first_work)
    def _gather():
        @pl.when(step == 0)
        def _():
            for e in range(local):
                run[e] = 0
            for copy in fetch(0) + fetch(1):
                copy.start()

        here = step % 2 * group
        for s in range(group):
            pltpu.make_async_copy(x_refs[0], arena.at[here + s], sems.at[here + s]).wait()

        ids = lax.broadcasted_iota(jnp.int32, (experts, tok), 0)
        before = one_zero(
            lax.broadcasted_iota(jnp.int32, (tok, tok), 0)
            < lax.broadcasted_iota(jnp.int32, (tok, tok), 1)
        )
        srows, grows, counts = [], [], []
        for s in range(group):
            thirds = dot_nt(rs_ref[...], arena[here + s])
            logits = (thirds[2 * experts :] + thirds[experts : 2 * experts]) + thirds[:experts]
            rt = rt_ref[ids_ref[0, step * group + s]]
            used = ids == rt[0:1]
            for k in range(1, rt.shape[0]):
                used = used | (ids == rt[k : k + 1])
            top = jnp.max(jnp.where(used, logits, MASKED_SCORE), axis=0, keepdims=True)
            terms = jnp.where(used, jnp.exp(logits - top), 0.0)
            gates = terms / jnp.sum(terms, axis=0, keepdims=True)
            used_f = jnp.where(used, 1.0, 0.0)
            rank = dot_nn(used_f.astype(BF16), before)
            for e in range(local):
                mine = ids == first_ref[0] + e
                grows.append(jnp.sum(jnp.where(mine, gates, 0.0), axis=0, keepdims=True))
                srow = jnp.sum(jnp.where(mine & used, rank + 1.0, 0.0), axis=0, keepdims=True) - 1.0
                srows.append(srow)
                counts.append(jnp.max(srow).astype(jnp.int32) + 1)
        offs = []
        ends = [run[e] for e in range(local)]
        for s in range(group):
            for e in range(local):
                offs.append(pl.multiple_of(ends[e], 16))
                offs_ref[e, step * group + s] = ends[e]
                ends[e] = ends[e] + ((counts[s * local + e] + 15) & -16)
        for e in range(local):
            run[e] = ends[e]
        for s in range(group):
            hots = [hot_rows(srows[s * local + e], cap, tok) for e in range(local)]
            picked = dot_nn(one_zero(jnp.concatenate(hots, axis=0)), arena[here + s]).astype(BF16)
            for e in range(local):
                at = pl.ds(offs[s * local + e], cap)
                slot_ref[e, pl.ds(step * group + s, 1), :] = srows[s * local + e]
                gcol = jnp.sum(
                    jnp.where(hots[e], grows[s * local + e], 0.0), axis=1, keepdims=True
                )
                gate[e, at, :] = jnp.broadcast_to(gcol, (cap, 128))
                buf[e, at, :] = picked[e * cap : (e + 1) * cap]

        for later in range(2, first_work):

            @pl.when(step + 2 == later)
            def _(later=later):
                for copy in fetch(later):
                    copy.start()

        @pl.when(step == first_work - 1)
        def _():
            for e in range(local):
                end = pl.multiple_of(run[e], 16)
                offs_ref[e, sources] = run[e]
                buf[e, pl.ds(end, tile), :] = jnp.zeros((tile, feat), BF16)
                gate[e, pl.ds(end, tile), :] = jnp.zeros((tile, 128), F32)

    work = step - first_work
    e = work // tiles
    j = work % tiles

    @pl.when((work >= 0) & (work < local * tiles))
    def _experts():
        @pl.when(j * tile < run[e])
        def _():
            at = pl.ds(pl.multiple_of(j * tile, tile), tile)
            rows = buf[e, at, :]
            g = gate[e, at, :]
            rows_ref[0] = rows
            gate_ref[0] = g
            a = dot_nn(rows, win_ref[0, :, :ff])
            b = dot_nn(rows, win_ref[0, :, ff:])
            act_g = (g[:, 0:1] * (a / (1.0 + jnp.exp(-a)) * b)).astype(BF16)
            buf[e, at, :] = dot_nn(act_g, wdn_ref[0]).astype(BF16)

    back = work - local * tiles

    @pl.when(back >= 0)
    def _scatter():
        for s in range(group):
            source = ids_ref[1, back * group + s]
            hots, terms = [], []
            for e in range(local):
                hots.append(hot_rows(slot_ref[e, pl.ds(source, 1), :], cap, tok))
                off = pl.multiple_of(offs_ref[e, source], 16)
                terms.append(buf[e, pl.ds(off, cap), :])
            total = dot_tn(
                one_zero(jnp.concatenate(hots, axis=0)), jnp.concatenate(terms, axis=0)
            )
            res_ref[s * tok : (s + 1) * tok, :] = total.astype(BF16)


def moe_front(first, ids, x_parts, rt_all, router_parts, w_in, w_down, cap, group):
    sources, top, tok = rt_all.shape
    feat = x_parts[0].shape[1]
    local, _, ff2 = w_in.shape
    ff = ff2 // 2
    most = sources * cap
    tile = min(256, most)
    tiles = most // tile
    room = most + max(tile, cap)
    steps = sources // group
    middle = local * tiles

    def exp3(i, f, ids):
        return (jnp.clip((i - steps) // tiles, 0, local - 1), 0, 0)

    def tile3(i, f, ids):
        at = jnp.clip(i - steps, 0, middle - 1)
        return (at // tiles, at % tiles, 0)

    return pl.pallas_call(
        functools.partial(front_body, cap, tile, tiles, group, sources),
        grid_spec=pltpu.PrefetchScalarGridSpec(
            num_scalar_prefetch=2,
            grid=(2 * steps + middle,),
            in_specs=[pl.BlockSpec(memory_space=pl.ANY)] * sources
            + [
                pl.BlockSpec(rt_all.shape, lambda i, f, ids: (0, 0, 0)),
                pl.BlockSpec(router_parts.shape, lambda i, f, ids: (0, 0)),
                pl.BlockSpec((1, feat, ff2), exp3),
                pl.BlockSpec((1, ff, feat), exp3),
            ],
            out_specs=[
                pl.BlockSpec(
                    (group * tok, feat), lambda i, f, ids: (jnp.maximum(i - steps - middle, 0), 0)
                ),
                pl.BlockSpec((1, tile, feat), tile3),
                pl.BlockSpec((1, tile, 128), tile3),
                pl.BlockSpec((local, sources, tok), lambda i, f, ids: (0, 0, 0)),
                pl.BlockSpec(memory_space=pltpu.SMEM),
            ],
            scratch_shapes=[
                pltpu.VMEM((local, room, feat), BF16),
                pltpu.VMEM((local, room, 128), F32),
                pltpu.SMEM((local,), jnp.int32),
                pltpu.VMEM((2 * group, tok, feat), BF16),
                pltpu.SemaphoreType.DMA((2 * group,)),
            ],
        ),
        out_shape=[
            jax.ShapeDtypeStruct((sources * tok, feat), BF16),
            jax.ShapeDtypeStruct((local, most, feat), BF16),
            jax.ShapeDtypeStruct((local, most, 128), F32),
            jax.ShapeDtypeStruct((local, sources, tok), F32),
            jax.ShapeDtypeStruct((local, sources + 1), jnp.int32),
        ],
        compiler_params=pltpu.CompilerParams(vmem_limit_bytes=56 * 1024 * 1024),
        cost_estimate=pl.CostEstimate(
            flops=2 * most * feat * ff * 3, bytes_accessed=10 * most * feat, transcendentals=0
        ),
        name="moe_front",
    )(first, ids, *x_parts, rt_all, router_parts, w_in, w_down)


def back_tile(rows, grads, g, win_ref, wdn_ref, acc_i, acc_d):
    ff = wdn_ref.shape[1]
    a = dot_nn(rows, win_ref[0, :, :ff])
    b = dot_nn(rows, win_ref[0, :, ff:])
    ga = dot_nt(grads, wdn_ref[0])
    sig = 1.0 / (1.0 + jnp.exp(-a))
    silu = a * sig
    act = silu * b
    gate_grad = jnp.sum(act * ga, axis=1, keepdims=True)
    gag = g * ga
    da = (gag * b * (sig * (1.0 + a * (1.0 - sig)))).astype(BF16)
    db = (gag * silu).astype(BF16)
    act_g = (g * act).astype(BF16)
    acc_d[...] += dot_tn(act_g, grads)
    acc_i[:, :ff] += dot_tn(rows, da)
    acc_i[:, ff:] += dot_tn(rows, db)
    pair = dot_nt(da, win_ref[0, :, :ff]) + dot_nt(db, win_ref[0, :, ff:])
    return pair.astype(BF16), gate_grad


def piece_shapes(feat, ff):
    return [(ff // 2, feat)] * 2 + [(feat // 4, 2 * ff)] * 4


def write_pieces(acc_i, acc_d, refs):
    downs = acc_d.shape[0] // 2
    ins = acc_i.shape[0] // 4
    for p in range(2):
        refs[p][...] = acc_d[p * downs : (p + 1) * downs, :].astype(BF16)
    for p in range(4):
        refs[2 + p][...] = acc_i[p * ins : (p + 1) * ins, :].astype(BF16)


def back_first_body(
    cap, tile, tiles, group,
    offs_ref, ids_ref, *refs,
):
    dy_refs = refs[:group]
    (slot_ref, rows_ref, gate_ref, win_ref, wdn_ref, pair_ref, gg_ref, other_ref, *piece_refs, buf, acc_i, acc_d) = refs[group:]
    step = pl.program_id(0)
    sources = slot_ref.shape[1]
    local = buf.shape[0]
    tok, feat = dy_refs[0].shape
    first_work = sources // group

    @pl.when(step < first_work)
    def _gather():
        for s in range(group):
            source = step * group + s
            hots = [hot_rows(slot_ref[e, pl.ds(source, 1), :], cap, tok) for e in range(local)]
            picked = dot_nn(
                one_zero(jnp.concatenate(hots, axis=0)), dy_refs[s][...]
            ).astype(BF16)
            for e in range(local):
                off = pl.multiple_of(offs_ref[e, source], 16)
                buf[e, pl.ds(off, cap), :] = picked[e * cap : (e + 1) * cap]

        @pl.when(step == first_work - 1)
        def _():
            for e in range(local):
                end = pl.multiple_of(offs_ref[e, sources], 16)
                buf[e, pl.ds(end, tile), :] = jnp.zeros((tile, feat), BF16)
            acc_i[...] = jnp.zeros_like(acc_i)
            acc_d[...] = jnp.zeros_like(acc_d)

    j = step - first_work

    @pl.when(j >= 0)
    def _experts():
        at = pl.ds(pl.multiple_of(j * tile, tile), tile)

        @pl.when(j * tile < offs_ref[1, sources])
        def _():
            other_ref[0] = buf[1, at, :]

        @pl.when(j * tile < offs_ref[0, sources])
        def _():
            pair, gate_grad = back_tile(
                rows_ref[0], buf[0, at, :], gate_ref[0, :, 0:1], win_ref, wdn_ref, acc_i, acc_d
            )
            pair_ref[...] = pair
            gg_ref[...] = jnp.broadcast_to(gate_grad, (tile, 128))

        @pl.when(j * tile >= offs_ref[0, sources])
        def _():
            pair_ref[...] = jnp.zeros_like(pair_ref)
            gg_ref[...] = jnp.zeros_like(gg_ref)

        @pl.when(j == tiles - 1)
        def _():
            write_pieces(acc_i, acc_d, piece_refs)


def used_tile(j, offs, e, sources, tile):
    return jnp.clip(j, 0, jnp.maximum((offs[e, sources] + (tile - 1)) // tile - 1, 0))


def moe_back_first(offs, ids, dy_all, slot, rows, gate, w_in, w_down, cap, group):
    local, sources, tok = slot.shape
    most, feat = rows.shape[1:]
    ff2 = w_in.shape[2]
    ff = ff2 // 2
    tile = min(256, most)
    tiles = most // tile
    room = most + max(tile, cap)
    steps = sources // group

    def in_tile(i, offs, ids):
        return (0, used_tile(i - steps, offs, 0, sources, tile), 0)

    def out_tile(i, offs, ids):
        return (jnp.maximum(i - steps, 0), 0)

    def other_tile(i, offs, ids):
        return (0, used_tile(i - steps, offs, 1, sources, tile), 0)

    def source(s):
        return lambda i, offs, ids: (ids[2, jnp.minimum(i, steps - 1) * group + s], 0)

    return pl.pallas_call(
        functools.partial(back_first_body, cap, tile, tiles, group),
        grid_spec=pltpu.PrefetchScalarGridSpec(
            num_scalar_prefetch=2,
            grid=(steps + tiles,),
            in_specs=[pl.BlockSpec((tok, feat), source(s)) for s in range(group)]
            + [
                pl.BlockSpec(slot.shape, lambda i, offs, ids: (0, 0, 0)),
                pl.BlockSpec((1, tile, feat), in_tile),
                pl.BlockSpec((1, tile, 128), in_tile),
                pl.BlockSpec((1, feat, ff2), lambda i, offs, ids: (0, 0, 0)),
                pl.BlockSpec((1, ff, feat), lambda i, offs, ids: (0, 0, 0)),
            ],
            out_specs=[
                pl.BlockSpec((tile, feat), out_tile),
                pl.BlockSpec((tile, 128), out_tile),
                pl.BlockSpec((1, tile, feat), other_tile),
                *[pl.BlockSpec(s, lambda i, offs, ids: (0, 0)) for s in piece_shapes(feat, ff)],
            ],
            scratch_shapes=[
                pltpu.VMEM((local, room, feat), BF16),
                pltpu.VMEM((feat, ff2), F32),
                pltpu.VMEM((ff, feat), F32),
            ],
        ),
        out_shape=[
            jax.ShapeDtypeStruct((most, feat), BF16),
            jax.ShapeDtypeStruct((most, 128), F32),
            jax.ShapeDtypeStruct((1, most, feat), BF16),
            *[jax.ShapeDtypeStruct(s, BF16) for s in piece_shapes(feat, ff)],
        ],
        compiler_params=pltpu.CompilerParams(vmem_limit_bytes=56 * 1024 * 1024),
        cost_estimate=pl.CostEstimate(
            flops=2 * most * feat * ff * 4, bytes_accessed=5 * dy_all.size * 2, transcendentals=0
        ),
        name="moe_back_first",
    )(offs, ids, *[dy_all] * group, slot, rows, gate, w_in, w_down)


def back_last_body(
    cap, tile, tiles, group,
    offs_ref, ids_ref, slot_ref, rows_ref, grads_ref, gate_ref, win_ref, wdn_ref, pair0_ref, gg0_ref,
    far_ref, near_ref, dg_ref, *rest,
):
    *piece_refs, buf, gg, acc_i, acc_d = rest
    step = pl.program_id(0)
    sources, tok = slot_ref.shape[1:]
    feat = far_ref.shape[1]

    @pl.when(step == 0)
    def _():
        acc_i[...] = jnp.zeros_like(acc_i)
        acc_d[...] = jnp.zeros_like(acc_d)

    @pl.when(step < tiles)
    def _experts():
        at = pl.ds(pl.multiple_of(step * tile, tile), tile)

        @pl.when(step * tile < offs_ref[1, sources])
        def _():
            pair, gate_grad = back_tile(
                rows_ref[0], grads_ref[0], gate_ref[0, :, 0:1], win_ref, wdn_ref, acc_i, acc_d
            )
            buf[at, :] = pair
            gg[at, :] = jnp.broadcast_to(gate_grad, (tile, 128))

        @pl.when(step * tile >= offs_ref[1, sources])
        def _():
            buf[at, :] = jnp.zeros((tile, feat), BF16)
            gg[at, :] = jnp.zeros((tile, 128), F32)

        @pl.when(step == tiles - 1)
        def _():
            write_pieces(acc_i, acc_d, piece_refs)

    back = step - tiles

    @pl.when(back >= 0)
    def _scatter():
        for s in range(group):
            source = lax.rem(back * group + s + sources // 2, sources)
            to = ids_ref[3, source]
            hots, terms = [], []
            for e, (pair, grads) in enumerate(((pair0_ref, gg0_ref), (buf, gg))):
                hot = hot_rows(slot_ref[e, pl.ds(source, 1), :], cap, tok)
                at = pl.ds(pl.multiple_of(offs_ref[e, source], 16), cap)
                hots.append(hot)
                terms.append(pair[at, :])
                dg_ref[to, e : e + 1, :] = jnp.sum(
                    jnp.where(hot, grads[at, 0:1], 0.0), axis=0, keepdims=True
                )
            dg_ref[to, 2:, :] = jnp.zeros((dg_ref.shape[1] - 2, tok), F32)
            total = dot_tn(
                one_zero(jnp.concatenate(hots, axis=0)), jnp.concatenate(terms, axis=0)
            )
            total = total.astype(BF16)

            @pl.when(back < sources // (2 * group))
            def _(total=total, s=s):
                far_ref[s * tok : (s + 1) * tok, :] = total

            @pl.when(back >= sources // (2 * group))
            def _(total=total, s=s):
                near_ref[s * tok : (s + 1) * tok, :] = total


def moe_back_last(offs, ids, slot, rows, grads, gate, w_in, w_down, pair0, gg0, cap, group):
    local, sources, tok = slot.shape
    most, feat = rows.shape[1:]
    ff2 = w_in.shape[2]
    ff = ff2 // 2
    tile = min(256, most)
    tiles = most // tile
    steps = sources // group

    def in_tile(i, offs, ids):
        return (1, used_tile(i, offs, 1, sources, tile), 0)

    def own_tile(i, offs, ids):
        return (0, used_tile(i, offs, 1, sources, tile), 0)

    def whole(i, offs, ids):
        return (0, 0)

    def far(i, offs, ids):
        return (jnp.clip(i - tiles, 0, steps // 2 - 1), 0)

    def near(i, offs, ids):
        return (jnp.clip(i - tiles - steps // 2, 0, steps // 2 - 1), 0)

    return pl.pallas_call(
        functools.partial(back_last_body, cap, tile, tiles, group),
        grid_spec=pltpu.PrefetchScalarGridSpec(
            num_scalar_prefetch=2,
            grid=(steps + tiles,),
            in_specs=[
                pl.BlockSpec(slot.shape, lambda i, offs, ids: (0, 0, 0)),
                pl.BlockSpec((1, tile, feat), in_tile),
                pl.BlockSpec((1, tile, feat), own_tile),
                pl.BlockSpec((1, tile, 128), in_tile),
                pl.BlockSpec((1, feat, ff2), lambda i, offs, ids: (1, 0, 0)),
                pl.BlockSpec((1, ff, feat), lambda i, offs, ids: (1, 0, 0)),
                pl.BlockSpec((most, feat), whole),
                pl.BlockSpec((most, 128), whole),
            ],
            out_specs=[
                pl.BlockSpec((group * tok, feat), far),
                pl.BlockSpec((group * tok, feat), near),
                pl.BlockSpec((sources, 8, tok), lambda i, offs, ids: (0, 0, 0)),
                *[pl.BlockSpec(s, whole) for s in piece_shapes(feat, ff)],
            ],
            scratch_shapes=[
                pltpu.VMEM((most, feat), BF16),
                pltpu.VMEM((most, 128), F32),
                pltpu.VMEM((feat, ff2), F32),
                pltpu.VMEM((ff, feat), F32),
            ],
        ),
        out_shape=[
            jax.ShapeDtypeStruct((sources // 2 * tok, feat), BF16),
            jax.ShapeDtypeStruct((sources // 2 * tok, feat), BF16),
            jax.ShapeDtypeStruct((sources, 8, tok), F32),
            *[jax.ShapeDtypeStruct(s, BF16) for s in piece_shapes(feat, ff)],
        ],
        compiler_params=pltpu.CompilerParams(vmem_limit_bytes=56 * 1024 * 1024),
        cost_estimate=pl.CostEstimate(
            flops=2 * most * feat * ff * 4, bytes_accessed=10 * most * feat, transcendentals=0
        ),
        name="moe_back_last",
    )(offs, ids, slot, rows, grads, gate, w_in, w_down, pair0, gg0)


def split_router(router):
    flat = router.T
    one = flat.astype(BF16)
    rest = flat - one.astype(F32)
    two = rest.astype(BF16)
    three = (rest - two.astype(F32)).astype(BF16)
    return jnp.concatenate([one, two, three], axis=0)


def add_body(pieces, *refs):
    step = pl.program_id(0)
    own, far, out_ref = refs[:pieces], refs[pieces : 2 * pieces], refs[-1]
    for p in range(pieces):

        @pl.when(step == p)
        def _(p=p):
            out_ref[0] = own[p][...].astype(F32) + far[p][...].astype(F32)


def add_pairs(own, far, index, local, held=None):
    pieces = len(own)
    rows, width = own[0].shape
    return pl.pallas_call(
        functools.partial(add_body, pieces),
        grid=(pieces,),
        in_specs=[pl.BlockSpec((rows, width), lambda i: (0, 0), pipeline_mode=pl.Buffered(1))]
        * (2 * pieces)
        + ([] if held is None else [pl.BlockSpec(memory_space=pl.ANY)]),
        out_specs=pl.BlockSpec((1, rows, width), lambda i: (index, i, 0)),
        out_shape=jax.ShapeDtypeStruct((local, pieces * rows, width), F32),
        input_output_aliases={} if held is None else {2 * pieces: 0},
        compiler_params=pltpu.CompilerParams(vmem_limit_bytes=40 * 1024 * 1024),
        cost_estimate=pl.CostEstimate(
            flops=pieces * rows * width, bytes_accessed=8 * pieces * rows * width, transcendentals=0
        ),
        name="add_pairs",
    )(*own, *far, *([] if held is None else [held]))


def lane_low(shape):
    return lax.broadcasted_iota(jnp.int32, shape, 1) < HD


def twist(tile_vals):
    width = tile_vals.shape[1]
    lane = lax.broadcasted_iota(jnp.int32, tile_vals.shape, 1)
    ahead = pltpu.roll(tile_vals, width - HD // 2, 1)
    behind = pltpu.roll(tile_vals, HD // 2, 1)
    return jnp.where(lane % HD < HD // 2, -ahead, behind)


def both_halves(tile_vals, low):
    kept = jnp.where(lane_low(tile_vals.shape) == low, tile_vals, 0.0)
    return kept + pltpu.roll(kept, HD, 1)


def head_places():
    per = REP + 2
    def at(index):
        return (index // 2, index % 2 == 0)
    groups = []
    for g in range(2):
        base = g * per
        groups.append(
            ([at(base + r) for r in range(REP)], at(base + REP), at(base + REP + 1))
        )
    return groups


def chunk_span(a, tok):
    reach = -(-(SEQ_MAX - 1) // tok)
    return max(0, a - reach) * tok, (a + 1) * tok


def mask_bias(start_row, a, tok):
    low, high = chunk_span(a, tok)
    shape = (high - low, tok)
    keys = lax.broadcasted_iota(jnp.int32, shape, 0) + low
    queries = lax.broadcasted_iota(jnp.int32, shape, 1) + a * tok
    allowed = (keys >= start_row) & (keys <= queries)
    return jnp.where(allowed, 0.0, MASKED_SCORE)


def attn_forward_body(
    chunks, here_ref, *refs,
):
    ins, (w_ref, cos_ref, sin_ref, start_ref, qkv_ref, kk_ref, vv_ref, lse_ref, heads_ref) = (
        refs[:chunks],
        refs[chunks:],
    )
    tok = ins[0].shape[0]
    here = here_ref[0]
    places = head_places()
    for k in range(chunks):
        a = lax.rem(here + (chunks - k), chunks)
        at = pl.ds(pl.multiple_of(a * tok, tok), tok)
        mixed = dot_nn(ins[k][...], w_ref[...])
        cos = cos_ref[at, :]
        sin = sin_ref[at, :]
        tiles = [mixed[:, 128 * i : 128 * (i + 1)] for i in range(mixed.shape[1] // 128)]
        turned = [t * cos + twist(t) * sin for t in tiles]
        for g, (queries, key, value) in enumerate(places):
            for r, (tile_at, low) in enumerate(queries):
                part = jnp.where(lane_low(tiles[0].shape) == low, turned[tile_at], 0.0)
                slot = 128 * (g * REP + r)
                qkv_ref[at, slot : slot + 128] = part.astype(BF16)
            kk_ref[at, 128 * g : 128 * (g + 1)] = both_halves(turned[key[0]], key[1]).astype(BF16)
            vv_ref[at, 128 * g : 128 * (g + 1)] = both_halves(tiles[value[0]], value[1]).astype(BF16)
    for a in range(chunks):
        low_key, high_key = chunk_span(a, tok)
        bias = mask_bias(start_ref[a : a + 1, :], a, tok)
        out = [None] * REP
        for g, (queries, _, _) in enumerate(places):
            keys = kk_ref[low_key:high_key, 128 * g : 128 * (g + 1)]
            vals = vv_ref[low_key:high_key, 128 * g : 128 * (g + 1)]
            for r in range(REP):
                head = g * REP + r
                q = qkv_ref[a * tok : (a + 1) * tok, 128 * head : 128 * (head + 1)]
                scores = dot_nt(keys, q) * HD ** (-0.5) + bias
                top = jnp.max(scores, axis=0, keepdims=True)
                terms = jnp.exp(scores - top)
                total = jnp.sum(terms, axis=0, keepdims=True)
                probs = (terms * (1.0 / total)).astype(BF16)
                lse_ref[head, a : a + 1, :] = top + jnp.log(total)
                mix = dot_tn(probs, vals)
                t = head // 2
                low = lane_low(mix.shape)
                out[t] = mix if head % 2 == 0 else jnp.where(low, out[t], mix)
        for t in range(REP):
            heads_ref[a * tok : (a + 1) * tok, 128 * t : 128 * (t + 1)] = out[t].astype(BF16)


def attn_forward(here, parts, w_cols, cos, sin, starts):
    chunks = len(parts)
    tok, feat = parts[0].shape
    total = chunks * tok
    cols = w_cols.shape[1]
    return pl.pallas_call(
        functools.partial(attn_forward_body, chunks),
        in_specs=[pl.BlockSpec(memory_space=pltpu.SMEM)]
        + [pl.BlockSpec(memory_space=pltpu.VMEM)] * (chunks + 4),
        out_specs=[pl.BlockSpec(memory_space=pltpu.VMEM)] * 5,
        out_shape=[
            jax.ShapeDtypeStruct((total, 128 * 2 * REP), BF16),
            jax.ShapeDtypeStruct((total, 256), BF16),
            jax.ShapeDtypeStruct((total, 256), BF16),
            jax.ShapeDtypeStruct((2 * REP, 8, tok), F32),
            jax.ShapeDtypeStruct((total, 2 * REP * HD), BF16),
        ],
        compiler_params=pltpu.CompilerParams(vmem_limit_bytes=48 * 1024 * 1024),
        cost_estimate=pl.CostEstimate(
            flops=2 * total * feat * cols * 4, bytes_accessed=8 * total * cols, transcendentals=0
        ),
        name="attn_forward",
    )(here, *parts, w_cols, cos, sin, starts)


def attn_backward_body(
    chunks, here_ref, grads_ref, q_ref, kk_ref, vv_ref, lse_ref, cos_ref, sin_ref, start_ref,
    out_ref, turned_ref, dk, dv, dq,
):
    tok = q_ref.shape[0] // chunks
    here = here_ref[0]
    dk[...] = jnp.zeros_like(dk)
    dv[...] = jnp.zeros_like(dv)
    for a in range(chunks):
        low_key, high_key = chunk_span(a, tok)
        bias = mask_bias(start_ref[a : a + 1, :], a, tok)
        for g in range(2):
            keys = kk_ref[low_key:high_key, 128 * g : 128 * (g + 1)]
            vals = vv_ref[low_key:high_key, 128 * g : 128 * (g + 1)]
            for r in range(REP):
                head = g * REP + r
                q = q_ref[a * tok : (a + 1) * tok, 128 * head : 128 * (head + 1)]
                t, is_low = head // 2, head % 2 == 0
                pair = grads_ref[a * tok : (a + 1) * tok, 128 * t : 128 * (t + 1)]
                grad = jnp.where(lane_low(pair.shape) == is_low, pair, jnp.zeros_like(pair))
                scores = dot_nt(keys, q) * HD ** (-0.5) + bias
                probs = jnp.exp(scores - lse_ref[head, a : a + 1, :])
                grad_probs = dot_nt(vals, grad)
                dv[low_key:high_key, 128 * g : 128 * (g + 1)] += dot_nn(probs.astype(BF16), grad)
                inner = jnp.sum(probs * grad_probs, axis=0, keepdims=True)
                grad_scores = (probs * (grad_probs - inner)).astype(BF16)
                dk[low_key:high_key, 128 * g : 128 * (g + 1)] += dot_nn(grad_scores, q)
                part = dot_tn(grad_scores, keys)
                here_at = slice(128 * t, 128 * (t + 1))
                rows = slice(a * tok, (a + 1) * tok)
                if is_low:
                    dq[rows, here_at] = part
                else:
                    dq[rows, here_at] = jnp.where(lane_low(part.shape), dq[rows, here_at], part)
    for a in range(chunks):
        rows = slice(a * tok, (a + 1) * tok)
        to = pl.ds(pl.multiple_of(lax.rem(here + (chunks - a), chunks) * tok, tok), tok)
        cos = cos_ref[rows, :]
        sin = sin_ref[rows, :]

        def back(vals):
            return (vals * cos - twist(vals) * sin) * HD ** (-0.5)

        def whole(vals):
            return vals + pltpu.roll(vals, HD, 1)

        low = lane_low((tok, 128))
        keys = [back(whole(dk[rows, 128 * g : 128 * (g + 1)])) for g in range(2)]
        vals = [whole(dv[rows, 128 * g : 128 * (g + 1)]) for g in range(2)]
        qs = [back(dq[rows, 128 * t : 128 * (t + 1)]) for t in range(REP)]
        tiles = [
            qs[0],
            jnp.where(low, qs[1], keys[0]),
            jnp.where(low, vals[0], qs[1]),
            qs[2],
            jnp.where(low, keys[1], vals[1]),
        ]
        for i, vals_of in enumerate(tiles):
            out_ref[rows, 128 * i : 128 * (i + 1)] = vals_of.astype(BF16)
            turned_ref[to, 128 * i : 128 * (i + 1)] = vals_of.astype(BF16)


def attn_backward(here, grads, q_rows, key_rows, value_rows, lse, cos, sin, starts, chunks):
    total = q_rows.shape[0]
    cols = 2 * (REP + 2) * HD
    return pl.pallas_call(
        functools.partial(attn_backward_body, chunks),
        in_specs=[pl.BlockSpec(memory_space=pltpu.SMEM)]
        + [pl.BlockSpec(memory_space=pltpu.VMEM)] * 8,
        out_specs=[pl.BlockSpec(memory_space=pltpu.VMEM)] * 2,
        out_shape=[jax.ShapeDtypeStruct((total, cols), BF16)] * 2,
        scratch_shapes=[
            pltpu.VMEM((total, 256), F32),
            pltpu.VMEM((total, 256), F32),
            pltpu.VMEM((total, 2 * REP * HD), F32),
        ],
        compiler_params=pltpu.CompilerParams(vmem_limit_bytes=48 * 1024 * 1024),
        cost_estimate=pl.CostEstimate(
            flops=12 * total * total * cols, bytes_accessed=8 * total * cols, transcendentals=0
        ),
        name="attn_backward",
    )(here, grads, q_rows, key_rows, value_rows, lse, cos, sin, starts)


def rope_rows(positions):
    freq_index = jnp.arange(HD // 2, dtype=F32)
    inverse = jnp.exp(freq_index * (-2.0 * math.log(10000.0) / HD))
    angles = positions.astype(F32)[:, None] * inverse[None, :]
    return jnp.tile(jnp.cos(angles), (1, 4)), jnp.tile(jnp.sin(angles), (1, 4))


def seq_layout(block_lengths, block_tok):
    seq_ends = jnp.cumsum(block_lengths)
    starts = seq_ends - block_lengths
    places = jnp.arange(block_tok, dtype=jnp.int32)
    segment = jnp.sum((places[:, None] >= seq_ends[None, :]).astype(jnp.int32), axis=1)
    owners = segment[:, None] == jnp.arange(block_lengths.shape[0], dtype=jnp.int32)[None, :]
    offset = jnp.sum(jnp.where(owners, starts[None, :], 0), axis=1)
    return places - offset, offset


def norm_apply(row_vals, gain_vec):
    scale_row = lax.rsqrt(jnp.mean(row_vals * row_vals, axis=1, keepdims=True) + EPSILON)
    return row_vals * scale_row * gain_vec


def norm_back(row_vals, gain_vec, grad):
    scale_row = lax.rsqrt(jnp.mean(row_vals * row_vals, axis=1, keepdims=True) + EPSILON)
    weighted = grad * gain_vec
    inner = jnp.mean(weighted * row_vals, axis=1, keepdims=True)
    return scale_row * weighted - row_vals * (scale_row * scale_row * scale_row * inner)


def shift(values, axis, by):
    size = lax.axis_size(axis)
    return lax.ppermute(values, axis, [(i, (i + by) % size) for i in range(size)])


def swap(values, axis, bit):
    size = lax.axis_size(axis)
    return lax.ppermute(values, axis, [(i, i ^ bit) for i in range(size)])


def plane_places(row, col):
    rows, cols = lax.axis_size("row"), lax.axis_size("col")
    index = jnp.arange(rows * cols, dtype=jnp.int32)
    core, side, back = index // (2 * cols), index // cols % 2, index % cols
    return row ^ (core + 2 * side), (col - back + cols) % cols


def gather_small_steps(row, col):
    rows = lax.axis_size("row")
    steps = []
    for axis in ("row", "col"):
        bit = 1
        while bit < lax.axis_size(axis):
            steps.append(
                lambda v, axis=axis, bit=bit: jnp.concatenate([v, swap(v, axis, bit)], axis=0)
            )
            bit *= 2
    from_row, from_col = plane_places(row, col)
    return steps, (from_row ^ row) + rows * (from_col ^ col)


def in_step(stages, *chains):
    values = [value for value, _ in chains]
    for stage in range(stages):
        for index, (_, steps) in enumerate(chains):
            mine = steps[stage : stage + 1] if stage + 1 < stages else steps[stage:]
            for step in mine:
                values[index] = step(values[index])
        values = list(lax.optimization_barrier(tuple(values)))
    return values


def ring_steps(by):
    return [lambda held: held + [shift(held[-1], "col", by)]] * (lax.axis_size("col") - 1)


def gather_plane(values, beside, steps):
    cols = lax.axis_size("col")
    line, across = [values], []
    for k in range(cols):
        side = swap(line[k], "row", 2)
        later = shift(line[k], "col", 1) if k + 1 < cols else None
        for step in steps[k : k + 1] if k + 1 < cols else steps[k:]:
            beside = step(beside)
        side, later, beside = lax.optimization_barrier((side, later, beside))
        line.append(later)
        across.append(side)
    own = line[:cols] + across
    return own + [swap(part, "row", 1) for part in own], beside


def after(values, *earlier):
    return lax.optimization_barrier((values, *earlier))[0]


def gather_rows_steps(row):
    dps = lax.axis_size("dp")
    dp = lax.axis_index("dp").astype(jnp.int32)
    places = []
    bit = 1
    while bit < dps:
        places.append(("dp", bit, dp // bit % 2, 0))
        bit *= 2
    places += [("row", 2, row // 2, 1), ("row", 1, row % 2, 2)]

    def send(values, axis, bit):
        return swap(values, axis, bit)

    def join(values, other, place, dim):
        return jnp.where(
            place == 0,
            jnp.concatenate([values, other], axis=dim),
            jnp.concatenate([other, values], axis=dim),
        )

    return [
        (functools.partial(send, axis=a, bit=b), functools.partial(join, place=p, dim=d))
        for a, b, p, d in places
    ]


def sum_rows_steps(row):
    dps = lax.axis_size("dp")
    dp = lax.axis_index("dp").astype(jnp.int32)
    places = [("row", 1, row % 2, 2), ("row", 2, row // 2, 1)]
    bit = dps // 2
    while bit:
        places.append(("dp", bit, dp // bit % 2, 0))
        bit //= 2

    def cut(values, place, dim):
        half = values.shape[dim] // 2
        return [
            lax.dynamic_slice_in_dim(values, at * half, half, dim) for at in (place, 1 - place)
        ]

    def add(halves, axis, bit):
        kept, given = halves
        return (kept.astype(F32) + swap(given, axis, bit).astype(F32)).astype(BF16)

    return [
        (functools.partial(cut, place=p, dim=d), functools.partial(add, axis=a, bit=b))
        for a, b, p, d in places
    ]


def sum_steps():
    steps = []
    for axis in ("row", "col", "dp"):
        bit = 1
        while bit < lax.axis_size(axis):
            steps.append(lambda v, axis=axis, bit=bit: v + swap(v, axis, bit))
            bit *= 2
    return steps


def shards(
    hidden_in,
    norm_gain_attn,
    norm_gain_moe,
    w_qkv,
    w_out,
    router,
    w_in,
    w_down,
    lengths,
    routes,
    out_grad,
):
    tok, feat = hidden_in.shape
    cols = lax.axis_size("col")
    rows = lax.axis_size("row")
    block_tok = tok * cols
    experts = router.shape[1]
    sources = rows * cols
    local = w_in.shape[0]
    cap = tok * TOP * 2 // experts
    head_cols = w_out.shape[1]
    group = 4
    plane = ("row", "col")
    col = lax.axis_index("col").astype(jnp.int32)
    row = lax.axis_index("row").astype(jnp.int32)
    here = col.reshape(1)
    first = ((row * cols + col) * local).reshape(1)
    rows_in = hidden_in.astype(F32)
    grad_out = out_grad.astype(F32)

    normed_attn = norm_apply(rows_in, norm_gain_attn).astype(BF16)
    row_steps = gather_rows_steps(row)
    small_steps, rt_ids = gather_small_steps(row, col)
    parts, out_line, qkv_own = in_step(
        cols - 1,
        ([normed_attn], ring_steps(1)),
        ([w_out], ring_steps(-1)),
        (w_qkv[None, None, None], [lambda v, s=s, j=j: j(v, s(v)) for s, j in row_steps]),
    )
    qkv_own = qkv_own.reshape(feat, -1)
    qkv_all = lax.all_gather(
        after(w_qkv, parts[2]), ("col", "dp", "row"), axis=0, tiled=True
    ).reshape(cols, feat, -1)
    out_line = jnp.concatenate(out_line, axis=1)
    out_line = jnp.concatenate([out_line, out_line], axis=1)
    out_line = lax.dynamic_slice_in_dim(
        out_line, (cols - col) % cols * head_cols, cols * head_cols, 1
    )[None, None, None]

    positions, seq_start = seq_layout(lengths[0], block_tok)
    cos, sin = rope_rows(positions)
    starts = jnp.pad(seq_start.reshape(cols, tok), ((0, -cols % 8), (0, 0)))
    q_rows, key_rows, value_rows, lse, heads_block = attn_forward(
        here, parts, qkv_own, cos, sin, starts
    )
    for send, join in row_steps[:-3]:
        out_line = join(out_line, send(out_line))
    (send_dp, join_dp), (send_side, join_side), (send_core, join_core) = row_steps[-3:]
    heads_block, other = lax.optimization_barrier((heads_block, send_dp(out_line)))
    out_line = join_dp(out_line, other)
    heads = lax.all_to_all(
        heads_block.reshape(cols, tok, head_cols), "col", split_axis=0, concat_axis=0, tiled=True
    )
    heads, other = lax.optimization_barrier((heads, send_side(out_line)))
    heads = jnp.concatenate([heads[k] for k in range(cols)], axis=1)
    out_line = join_side(out_line, other)
    out_full = join_core(out_line, send_core(out_line)).reshape(feat, -1)
    middle = rows_in + dot_nt(heads, out_full)
    normed_moe = norm_apply(middle, norm_gain_moe).astype(BF16)

    x_parts, rt_all = gather_plane(normed_moe, routes.T[None], small_steps)
    dy_all = lax.all_gather(after(out_grad, x_parts[cols - 2]), plane, axis=0, tiled=True)
    from_row, from_col = plane_places(row, col)
    whole_ids = from_row * cols + from_col
    index = jnp.arange(sources, dtype=jnp.int32)
    twist_row, back_col = index // cols ^ row, (col - index % cols + cols) % cols
    places = (twist_row % 2 * 2 + twist_row // 2) * cols + back_col
    ids = jnp.stack([rt_ids, places, whole_ids, whole_ids])

    res_part, rows_kept, gate, slot, offs = moe_front(
        first, ids, x_parts, rt_all, split_router(router), w_in, w_down, cap, group
    )
    res = lax.psum_scatter(res_part, plane, scatter_dimension=0, tiled=True)
    pair0, gg0, dy_kept, *own0 = moe_back_first(
        offs, ids, dy_all, slot, rows_kept, gate, w_in, w_down, cap, group
    )
    paired = lax.axis_size("dp") == 2
    pieces = len(own0)
    own, far = list(own0), []

    def exchange(count, *earlier):
        if not paired:
            return []
        at = len(far)
        sent = [swap(after(piece, *earlier), "dp", 1) for piece in own[at : at + count]]
        far.extend(sent)
        return sent

    def arrived(values, sent):
        if sent:
            values, kept = lax.optimization_barrier((values, sent))
            far[len(far) - len(sent) :] = kept
        return values

    sent = exchange(2, pair0)
    gn_far, gn_near, dg, *own1 = moe_back_last(
        offs, ids, slot, rows_kept, dy_kept, gate, w_in, w_down, pair0, gg0, cap, group
    )
    own += own1
    gn_far = arrived(gn_far, sent)

    from_far = swap(gn_far, "row", 1)
    sent = exchange(1, gn_far)
    from_far = arrived(from_far, sent)

    def near_terms(k, source):
        terms = []
        for index in (cols + k, k):
            at = slice(index * tok, (index + 1) * tok)
            terms.append((gn_near[at].astype(F32) + source[at].astype(F32)).astype(BF16))
        return terms

    gn, terms = None, near_terms(cols - 1, from_far)
    for k in range(cols - 1, -1, -1):
        side = swap(terms[0], "row", 2)
        sent = exchange(1, terms[0])
        total = terms[1].astype(F32)
        if gn is not None:
            total = total + shift(gn, "col", -1).astype(F32)
        terms = near_terms(k - 1, after(from_far, terms[0])) if k else None
        if k == cols - 1:
            normed_wide = normed_moe.astype(F32)
            logits = jnp.dot(
                normed_wide, router, precision=HIGHEST, preferred_element_type=F32
            )
            expert_ids = jnp.arange(experts, dtype=jnp.int32)
            used = jnp.any(routes[:, :, None] == expert_ids[None, None, :], axis=1)
            top = jnp.max(jnp.where(used, logits, MASKED_SCORE), axis=1, keepdims=True)
            exps = jnp.where(used, jnp.exp(logits - top), 0.0)
            gates = exps / jnp.sum(exps, axis=1, keepdims=True)
            dg_back = lax.all_to_all(
                after(dg, from_far), plane, split_axis=0, concat_axis=0, tiled=True
            )
            side, gates, dg_back = lax.optimization_barrier((side, gates, dg_back))
        if k == cols - 2:
            grad_gates = after(dg_back, gates)[:, :local].reshape(experts, tok).T
            grad_logits = gates * (
                grad_gates - jnp.sum(gates * grad_gates, axis=1, keepdims=True)
            )
            router_term = lax.dot_general(
                grad_logits,
                router,
                (((1,), (1,)), ((), ())),
                precision=HIGHEST,
                preferred_element_type=F32,
            )
            side, router_term, grad_logits = lax.optimization_barrier(
                (side, router_term, grad_logits)
            )
        if k == cols - 3:
            grad_router = lax.dot_general(
                grad_logits,
                normed_wide,
                (((0,), (0,)), ((), ())),
                precision=HIGHEST,
                preferred_element_type=F32,
            )
            side, grad_router = lax.optimization_barrier((side, grad_router))
        if k == 1:
            side, res = lax.optimization_barrier((side, res))
        total, side, terms = arrived(lax.optimization_barrier((total, side, terms)), sent)
        gn = total + side.astype(F32)
        if k:
            gn = gn.astype(BF16)

    grad_nm = gn + router_term
    grad_middle = grad_out + norm_back(middle, norm_gain_moe, grad_nm)
    grad_attn = grad_middle.astype(BF16)
    grad_heads = dot_nn(grad_attn, out_full).astype(BF16)

    sum_out, sum_all = sum_rows_steps(row), sum_steps()
    sent = exchange(1, gn)
    grads_block = lax.all_to_all(
        jnp.stack([grad_heads[:, k * head_cols : (k + 1) * head_cols] for k in range(cols)]),
        "col",
        split_axis=0,
        concat_axis=0,
        tiled=True,
    )
    w_out_sum = dot_tn(after(grad_attn, grad_heads), heads).astype(BF16)
    w_out_sum = sum_out[0][0](w_out_sum.reshape(-1, 2, 2, w_out.shape[0], feat))
    small = sum_all[1](sum_all[0](after(grad_router, grad_heads)))
    w_out_sum = sum_out[1][0](sum_out[0][1](w_out_sum))
    grads_block, w_out_sum, small = arrived(
        lax.optimization_barrier((grads_block, w_out_sum, small)), sent
    )

    sent = exchange(1, grads_block)
    w_out_sum = sum_out[1][1](w_out_sum)
    small = sum_all[3](sum_all[2](small))
    grad_mixed, turned_mixed = attn_backward(
        here, grads_block.reshape(cols * tok, head_cols), q_rows, key_rows, value_rows, lse,
        cos, sin, starts, cols,
    )
    grad_mixed, turned_mixed, w_out_sum, small = arrived(
        lax.optimization_barrier((grad_mixed, turned_mixed, w_out_sum, small)), sent
    )

    mixed_back = lax.all_to_all(
        grad_mixed.reshape(cols, tok, -1), "col", split_axis=0, concat_axis=0, tiled=True
    )
    sent = exchange(1, grad_mixed)
    w_qkv_part = dot_tn(jnp.concatenate(parts, axis=0), turned_mixed)
    w_qkv_part = arrived(w_qkv_part, sent)
    sent = exchange(1, w_qkv_part)
    for step in sum_out[2:]:
        w_out_sum = step[1](step[0](after(w_out_sum, w_qkv_part)))
    gain_attn_part = jnp.sum(w_qkv_part * qkv_own.astype(F32), axis=1) / norm_gain_attn
    w_qkv_sum = sum_out[0][0](w_qkv_part.astype(BF16).reshape(-1, 2, 2, *w_qkv.shape))
    w_qkv_sum = sum_out[0][1](w_qkv_sum)
    middle_scale = lax.rsqrt(jnp.mean(middle * middle, axis=1, keepdims=True) + EPSILON)
    gain_moe_part = jnp.sum(
        after(grad_nm, w_qkv_part) * middle * middle_scale, axis=0, keepdims=True
    )
    gains = sum_all[1](sum_all[0](jnp.concatenate([gain_moe_part, gain_attn_part[None]], axis=0)))
    if paired:
        grad_w_in = add_pairs(own[2:pieces], after(far[2:pieces], w_qkv_part), 0, local)
        grad_w_down = add_pairs(own[:2], after(far[:2], w_qkv_part), 0, local)
    else:
        grad_w_in = lax.psum(
            jnp.stack([jnp.concatenate(own[e * pieces + 2 : (e + 1) * pieces]) for e in range(local)]), "dp"
        ).astype(F32)
        grad_w_down = lax.psum(
            jnp.stack([jnp.concatenate(own[e * pieces : e * pieces + 2]) for e in range(local)]), "dp"
        ).astype(F32)
    mixed_back, w_qkv_sum, w_out_sum, gains, grad_w_in, grad_w_down = arrived(
        lax.optimization_barrier(
            (mixed_back, w_qkv_sum, w_out_sum, gains, grad_w_in, grad_w_down)
        ),
        sent,
    )

    sent = exchange(1, mixed_back)
    w_qkv_sum = sum_out[1][1](sum_out[1][0](w_qkv_sum))
    gains = sum_all[3](sum_all[2](gains))
    lines = lax.all_to_all(
        jnp.stack([w_out_sum[..., k * head_cols : (k + 1) * head_cols] for k in range(cols)]),
        "col",
        split_axis=0,
        concat_axis=0,
        tiled=True,
    )
    grad_na = sum(dot_nt(mixed_back[k], qkv_all[k]) for k in range(cols))
    grad_hidden = grad_middle + norm_back(rows_in, norm_gain_attn, grad_na)
    result = middle + res.astype(F32)
    grad_hidden, w_qkv_sum, gains, lines, result = arrived(
        lax.optimization_barrier((grad_hidden, w_qkv_sum, gains, lines, result)), sent
    )
    small = jnp.concatenate([small, gains], axis=0)
    for step in sum_all[4:]:
        small = step(small)
    for step in sum_out[2:]:
        w_qkv_sum = step[1](step[0](w_qkv_sum))
    if paired:
        grad_w_in = add_pairs(own[pieces + 2 :], far[pieces + 2 :], 1, local, grad_w_in)
        grad_w_down = add_pairs(
            own[pieces : pieces + 2], far[pieces : pieces + 2], 1, local, grad_w_down
        )
    grad_w_qkv = w_qkv_sum.reshape(w_qkv.shape).astype(F32)
    grad_w_out = jnp.sum(lines.astype(F32), axis=0).reshape(w_out.shape)
    return (
        result,
        grad_hidden,
        small[experts + 1],
        small[experts],
        grad_w_qkv,
        grad_w_out,
        small[:experts].T,
        grad_w_in,
        grad_w_down,
    )


def solution(mesh):
    in_specs = (
        P(("dp", "row", "col"), None),
        P(),
        P(),
        P(("dp", "row"), "col"),
        P(("dp", "row"), "col"),
        P(),
        P(("row", "col"), None, None),
        P(("row", "col"), None, None),
        P(("dp", "row"), None),
        P(("dp", "row", "col"), None),
        P(("dp", "row", "col"), None),
    )
    out_specs = (
        P(("dp", "row", "col"), None),
        P(("dp", "row", "col"), None),
        P(),
        P(),
        P(("dp", "row"), "col"),
        P(("dp", "row"), "col"),
        P(),
        P(("row", "col"), None, None),
        P(("row", "col"), None, None),
    )
    return jax.shard_map(shards, mesh=mesh, in_specs=in_specs, out_specs=out_specs, check_vma=False)
```

time: 908 us -> 720 us (0.79)
  waiting for transfers between devices: 565 us -> 301 us
  starting transfers between devices: 81.9 us -> 128 us
  Pallas kernels: 114 us -> 156 us
  blocking collectives: 34 us -> 0 us
  other arithmetic: 40.8 us -> 62.2 us
    reduce_scatter x2 -> x0, waiting for transfers between devices: 142 us -> none  [the longest x1 103 us: shards(): gn = lax.psum_scatter(gn_part, plane, scatter_dimension=0, tiled=True)]
    ppermute x21 -> x12, waiting for transfers between devices: 200 us -> 84 us  [shift(): lax.ppermute(values, axis, [(i, (i + by) % size) for i in range(size)])]
    ppermute x12 -> x54, waiting for transfers between devices: 60.6 us -> 174 us  [swap(): return lax.ppermute(values, axis, [(i, i ^ bit) for i in range(size)])]
    all_gather x5 -> x2, waiting for transfers between devices: 124 us -> 13.2 us  [the longest x1 13.2 us: shards(): lax.all_gather(after(out_grad, x_parts[cols - 2]), plane, axis=0, tiled=T...]
    ppermute x12 -> x54, starting transfers between devices: 12.2 us -> 75.6 us  [swap(): return lax.ppermute(values, axis, [(i, i ^ bit) for i in range(size)])]
    pallas_call x1 -> x7, Pallas kernels: 87.6 us -> 127 us  [the longest x1 41.8 us: moe_front(): pl.pallas_call(functools.partial(front_body, cap, tile, tiles, group, sou...]
    all_gather x1 -> x0, blocking collectives: 34 us -> none  [shards(): rt_all = lax.all_gather(routes.T, plane, axis=0)]
    unnamed x10 -> x3, waiting for transfers between devices: 32.8 us -> 0.05 us
  transfers between devices with their start and end apart: 43 -> 74, of which waited for: 22 -> 37; matrix products, arithmetic and copies ran while one was open for 9% -> 13% of each run, Pallas kernels for 3% -> 22%
where the time goes in v2:
time: 720 us; the launch traced here: 716 us
  waiting for transfers between devices  301 us (42%)
  Pallas kernels  156 us (22%)
  starting transfers between devices  128 us (18%)
  other arithmetic  62.2 us (9%)
  local copies, waits for them, and re-layouts  26.4 us (4%)
  matrix products  25.4 us (4%)
  between operations  17.1 us (2%)
    ppermute x54, waiting for transfers between devices, swap(): return lax.ppermute(values, axis, [(i, i ^ bit) for i in range(size)])  174 us
    ppermute x12, waiting for transfers between devices, shift(): lax.ppermute(values, axis, [(i, (i + by) % size) for i in range(size)])  84 us
    ppermute x54, starting transfers between devices, swap(): return lax.ppermute(values, axis, [(i, i ^ bit) for i in range(size)])  75.6 us
    pallas_call x1, Pallas kernels, moe_front(): pl.pallas_call(functools.partial(front_body, cap, tile, tiles, group, sou...  41.8 us
    pallas_call x1, Pallas kernels, moe_back_last(): pl.pallas_call(functools.partial(back_last_body, cap, tile, tiles, group)...  39.1 us
    pallas_call x1, Pallas kernels, moe_back_first(): pl.pallas_call(functools.partial(back_first_body, cap, tile, tiles, group...  31.7 us
    ppermute x12, starting transfers between devices, shift(): lax.ppermute(values, axis, [(i, (i + by) % size) for i in range(size)])  27.9 us
    pallas_call x1, Pallas kernels, attn_backward(): pl.pallas_call(functools.partial(attn_backward_body, chunks), in_specs=[p...  17.1 us
  transfers between devices with their start and end apart: 74, of which 37 were waited for; matrix products, arithmetic and copies ran while one was open for 13% of the time, Pallas kernels for 22%

profile of v2, /device:TPU:0, one launch (start us, length us, event | category | flops | bytes accessed | tf_op | source)
XLA Modules:
  0.0 716.1 jit_solution(17518846169204803540)
XLA Ops:
  21.5 15.2 %collective-permute-done.1 = bf16[192,384]{1,0:T(8,128)(2,1)S(1)} collective-permute-done((bf16[192,384]{1,0:T(8,128)(2,1)S(1)}, bf16[192,384]{1,0:T(8,128)(2,1)S(1)}, u32[]{:S(2)}, u32[]{:S(2)}) %collective-permute-start.1) | collective-permute-done | bytes 147488 | tf_op jit(solution)/shard_map/ppermute | solution.py:802
  42.2 8.0 %collective-permute-done.5 = bf16[2,1,1,192,640]{4,3,2,1,0:T(8,128)(2,1)} collective-permute-done((bf16[2,1,1,192,640]{4,3,2,1,0:T(8,128)(2,1)S(1)}, bf16[2,1,1,192,640]{4,3,2,1,0:T(8,128)(2,1)}, u32[]{:S(2)}, u32[]{:S(2)}) %collective-permute-start.5) | collective-permute-done | bytes 491552 | tf_op jit(solution)/shard_map/ppermute | solution.py:807
  52.6 8.3 %collective-permute-done.4 = bf16[192,384]{1,0:T(8,128)(2,1)S(1)} collective-permute-done((bf16[192,384]{1,0:T(8,128)(2,1)S(1)}, bf16[192,384]{1,0:T(8,128)(2,1)S(1)}, u32[]{:S(2)}, u32[]{:S(2)}) %collective-permute-start.4) | collective-permute-done | bytes 147488 | tf_op jit(solution)/shard_map/ppermute | solution.py:802
  72.3 13.7 %collective-permute-done.7 = bf16[192,384]{1,0:T(8,128)(2,1)S(1)} collective-permute-done((bf16[192,384]{1,0:T(8,128)(2,1)}, bf16[192,384]{1,0:T(8,128)(2,1)S(1)}, u32[]{:S(2)}, u32[]{:S(2)}) %collective-permute-start.7) | collective-permute-done | bytes 147488 | tf_op jit(solution)/shard_map/ppermute | solution.py:802
  88.3 12.1 %attn_forward.1 = (bf16[1024,768]{1,0:T(8,128)(2,1)}, bf16[1024,256]{1,0:T(8,128)(2,1)S(1)}, bf16[1024,256]{1,0:T(8,128)(2,1)S(1)}, f32[6,8,256]{2,1,0:T(8,128)S(1)}, bf16[1024,384]{1,0:T(8,128)(2,1)}) custom-call(s32[1]{0:T(128)} %bitcast.here_ref, bf16[256,1536]{1,0:T(8,128)(2,1)S(1)} %fusion.16.refs_0_, ...), custom_call_target="tpu_custom_call" | custom-call | flops 8053063680 | bytes 5242880 | tf_op jit(solution)/shard_map/attn_forward/pallas_call | solution.py:667
  111.2 14.8 %all-to-all-done = bf16[4,256,384]{2,1,0:T(8,128)(2,1)S(1)} async-done(((bf16[4,256,384]{2,1,0:T(8,128)(2,1)}), bf16[4,256,384]{2,1,0:T(8,128)(2,1)S(1)}, u32[]{:S(2)}, u32[]{:S(2)}) %all-to-all-start) | async-done | bytes 786464 | tf_op jit(solution)/shard_map/all_to_all | solution.py:987
  126.0 10.6 %collective-permute-done.10 = bf16[2,1,1,192,1536]{4,3,2,1,0:T(8,128)(2,1)} collective-permute-done((bf16[2,1,1,192,1536]{4,3,2,1,0:T(8,128)(2,1)}, bf16[2,1,1,192,1536]{4,3,2,1,0:T(8,128)(2,1)}, u32[]{:S(2)}, u32[]{:S(2)}) %collective-permute-start.10) | collective-permute-done | bytes 1179680 | tf_op jit(solution)/shard_map/ppermute | solution.py:807
  150.2 17.6 %collective-permute-done.13.refs_1_ = bf16[256,1536]{1,0:T(8,128)(2,1)S(1)} collective-permute-done((bf16[256,1536]{1,0:T(8,128)(2,1)S(1)}, bf16[256,1536]{1,0:T(8,128)(2,1)S(1)}, u32[]{:S(2)}, u32[]{:S(2)}) %collective-permute-start.13) | collective-permute-done | bytes 786464 | tf_op jit(solution)/shard_map/ppermute | solution.py:802
  170.9 16.5 %collective-permute-done.17 = s32[2,8,256]{2,1,0:T(8,128)S(1)} collective-permute-done((s32[2,8,256]{2,1,0:T(8,128)S(1)}, s32[2,8,256]{2,1,0:T(8,128)S(1)}, u32[]{:S(2)}, u32[]{:S(2)}) %collective-permute-start.17) | collective-permute-done | bytes 16416 | tf_op jit(solution)/shard_map/ppermute | solution.py:807
  192.0 25.3 %collective-permute-done.20 = s32[4,8,256]{2,1,0:T(8,128)S(1)} collective-permute-done((s32[4,8,256]{2,1,0:T(8,128)S(1)}, s32[4,8,256]{2,1,0:T(8,128)S(1)}, u32[]{:S(2)}, u32[]{:S(2)}) %collective-permute-start.20) | collective-permute-done | bytes 32800 | tf_op jit(solution)/shard_map/ppermute | solution.py:807
  220.8 11.4 %collective-permute-start.22 = (s32[8,8,256]{2,1,0:T(8,128)S(1)}, s32[8,8,256]{2,1,0:T(8,128)S(1)}, u32[]{:S(2)}, u32[]{:S(2)}) collective-permute-start(s32[8,8,256]{2,1,0:T(8,128)S(1)} %pad_add_fusion.1), channel_id=1, source_target_pairs={{0,2},{1,3},{2,0},{3,1},{4,6},{5,7},{6,4},{7,5},{8,10},{9,11},{10,... | collective-permute-start | bytes 196616 | tf_op jit(solution)/shard_map/ppermute | solution.py:807
  232.2 5.4 collective-permute-done.22
  248.7 41.8 %moe_front.1 = (bf16[4096,1536]{1,0:T(8,128)(2,1)}, bf16[2,2048,1536]{2,1,0:T(8,128)(2,1)}, f32[2,2048,128]{2,1,0:T(8,128)}, f32[2,16,256]{2,1,0:T(8,128)}, s32[2,17]{1,0:T(2,128)}) custom-call(s32[1]{0:T(128)} %bitcast.19.first_ref, s32[4,16]{1,0:T(4,128)} %pad_add_fusion.4.ids_ref, bf16[256,1536]{1,0:T(8,128)(2,1)} %copy-done.44, ...), custom_call_target="tpu_custom_call" | custom-call | flops 9663676416 | bytes 31457280 | tf_op jit(solution)/shard_map/moe_front/pallas_call | solution.py:195
  290.6 13.2 %all-gather.3.cloned.1.call-done.refs_0_.refs_1_.refs_2_.refs_3_ = bf16[4096,1536]{1,0:T(8,128)(2,1)} async-done(((bf16[256,1536]{1,0:T(8,128)(2,1)}), bf16[4096,1536]{1,0:T(8,128)(2,1)}) %all-gather.3.cloned.1.call-update) | async-done | bytes 12582928 | tf_op jit(solution)/shard_map/all_gather | solution.py:998
  303.8 31.7 %moe_back_first.1 = (bf16[2048,1536]{1,0:T(8,128)(2,1)}, f32[2048,128]{1,0:T(8,128)}, bf16[1,2048,1536]{2,1,0:T(8,128)(2,1)}, bf16[256,1536]{1,0:T(8,128)(2,1)},...) custom-call(s32[2,17]{1,0:T(2,128)} %get-tuple-element.232.offs_ref,, ...), custom_call_target="tpu_custom_call" | custom-call | flops 12884901888 | bytes 62914560 | tf_op jit(solution)/shard_map/moe_back_first/pallas_call | solution.py:358
  337.5 39.1 %moe_back_last.1 = (bf16[2048,1536]{1,0:T(8,128)(2,1)}, bf16[2048,1536]{1,0:T(8,128)(2,1)}, f32[16,8,256]{2,1,0:T(8,128)}, bf16[256,1536]{1,0:T(8,128)(2,1)}, bf...) custom-call(s32[2,17]{1,0:T(2,128)} %get-tuple-element.232.offs_ref,, ...), custom_call_target="tpu_custom_call" | custom-call | flops 12884901888 | bytes 31457280 | tf_op jit(solution)/shard_map/moe_back_last/pallas_call | solution.py:488
  379.5 18.9 %collective-permute-done.34.refs_4_ = bf16[384,1024]{1,0:T(8,128)(2,1)S(1)} collective-permute-done((bf16[384,1024]{1,0:T(8,128)(2,1)S(1)}, bf16[384,1024]{1,0:T(8,128)(2,1)S(1)}, u32[]{:S(2)}, u32[]{:S(2)}) %collective-permute-start.34) | collective-permute-done | bytes 786464 | tf_op jit(solution)/shard_map/ppermute | solution.py:807
  403.0 20.8 %collective-permute-start.35 = (bf16[256,1536]{1,0:T(8,128)(2,1)}, bf16[256,1536]{1,0:T(8,128)(2,1)}, u32[]{:S(2)}, u32[]{:S(2)}) collective-permute-start(bf16[256,1536]{1,0:T(8,128)(2,1)} %get-tuple-element.392), channel_id=1, source_target_pairs={{0,8},{4,12},{8,0},{12,4},{1,9},{5,13},{9,1},{13,5},{2,10},{6,14},... | collective-permute-start | bytes 2359304 | tf_op jit(solution)/shard_map/ppermute | solution.py:807
  425.6 6.9 all-to-all-start.1
  435.7 7.8 %all-to-all-done.1 = f32[16,8,256]{2,1,0:T(8,128)} async-done(((f32[16,8,256]{2,1,0:T(8,128)}), f32[16,8,256]{2,1,0:T(8,128)}, u32[]{:S(2)}, u32[]{:S(2)}) %all-to-all-start.1) | async-done | bytes 131104 | tf_op jit(solution)/shard_map/all_to_all | solution.py:1067
  457.5 11.9 %collective-permute-done.38 = bf16[256,1536]{1,0:T(8,128)(2,1)} collective-permute-done((bf16[256,1536]{1,0:T(8,128)(2,1)}, bf16[256,1536]{1,0:T(8,128)(2,1)}, u32[]{:S(2)}, u32[]{:S(2)}) %collective-permute-start.38) | collective-permute-done | bytes 786464 | tf_op jit(solution)/shard_map/ppermute | solution.py:807
  469.3 6.2 collective-permute-done.37
  479.2 5.4 collective-permute-start.40
  489.2 18.7 %collective-permute-done.41 = bf16[256,1536]{1,0:T(8,128)(2,1)} collective-permute-done((bf16[256,1536]{1,0:T(8,128)(2,1)S(1)}, bf16[256,1536]{1,0:T(8,128)(2,1)}, u32[]{:S(2)}, u32[]{:S(2)}) %collective-permute-start.41) | collective-permute-done | bytes 786464 | tf_op jit(solution)/shard_map/ppermute | solution.py:807
  507.9 6.7 collective-permute-done.40
  526.5 12.4 %collective-permute-done.43 = bf16[256,1536]{1,0:T(8,128)(2,1)} collective-permute-done((bf16[256,1536]{1,0:T(8,128)(2,1)}, bf16[256,1536]{1,0:T(8,128)(2,1)}, u32[]{:S(2)}, u32[]{:S(2)}) %collective-permute-start.43) | collective-permute-done | bytes 786464 | tf_op jit(solution)/shard_map/ppermute | solution.py:802
  562.9 5.2 collective-permute-done.48
  573.7 6.5 all-to-all-done.2
  595.2 17.1 %attn_backward.1 = (bf16[1024,640]{1,0:T(8,128)(2,1)}, bf16[1024,640]{1,0:T(8,128)(2,1)S(1)}) custom-call(s32[1]{0:T(128)} %bitcast.here_ref, bf16[1024,384]{1,0:T(8,128)(2,1)} %bitcast.30.grads_ref, bf16[1024,768]{1,0:T(8,128)(2,1)} %get-tuple-element.311.q_ref, bf16[1024,256]{1,0:T(8,128)(2,1)S(1)} %copy-done.30, bf16[1024,256]{1,0:T(8,128)(2,1)S(1)} %copy-done.32, ...), custom_call_target="tpu_custom_call" | custom-call | flops 8053063680 | bytes 5242880 | tf_op jit(solution)/shard_map/attn_backward/pallas_call | solution.py:752
  625.6 6.7 collective-permute-done.54.refs_5_
  642.8 7.2 %collective-permute-done.56 = bf16[1,1,1,192,1536]{4,3,2,1,0:T(8,128)(2,1)S(1)} collective-permute-done((bf16[1,1,1,192,1536]{4,3,2,1,0:T(8,128)(2,1)S(1)}, bf16[1,1,1,192,1536]{4,3,2,1,0:T(8,128)(2,1)S(1)}, u32[]{:S(2)}, u32[]{:S(2)}) %collective-permute-start.56) | collective-permute-done | bytes 589856 | tf_op jit(solution)/shard_map/ppermute | solution.py:807
  650.5 15.8 %collective-permute-done.59.refs_6_ = bf16[384,1024]{1,0:T(8,128)(2,1)} collective-permute-done((bf16[384,1024]{1,0:T(8,128)(2,1)}, bf16[384,1024]{1,0:T(8,128)(2,1)}, u32[]{:S(2)}, u32[]{:S(2)}) %collective-permute-start.59) | collective-permute-done | bytes 786464 | tf_op jit(solution)/shard_map/ppermute | solution.py:807
  (436 shorter events, 240.1 us)
Async XLA Ops:
  10.9 25.8 %collective-permute-start = (bf16[256,1536]{1,0:T(8,128)(2,1)S(1)}, bf16[256,1536]{1,0:T(8,128)(2,1)S(1)}, u32[]{:S(2)}, u32[]{:S(2)}) collective-permute-start(bf16[256,1536]{1,0:T(8,128)(2,1)S(1)} %fusion.16.refs_0_), channel_id=1, source_target_pairs={{0,1},{1,2},{2,3},{3,0},{4,5},{5,6},{6,7},{7,4},{8,9},{9,10},{10,1... | collective-permute-start | bytes 2359304 | tf_op jit(solution)/shard_map/ppermute | solution.py:802
  36.7 24.2 %collective-permute-start.3 = (bf16[256,1536]{1,0:T(8,128)(2,1)S(1)}, bf16[256,1536]{1,0:T(8,128)(2,1)S(1)}, u32[]{:S(2)}, u32[]{:S(2)}) collective-permute-start(bf16[256,1536]{1,0:T(8,128)(2,1)S(1)} %collective-permute-done.refs_1_), channel_id=1, source_target_pairs={{0,1},{1,2},{2,3},{3,0},{4,5},{5,6},{6,7},{7,4},{8,9},{9,10},{10,1... | collective-permute-start | bytes 2359304 | tf_op jit(solution)/shard_map/ppermute | solution.py:802
  38.8 22.1 %collective-permute-start.4 = (bf16[192,384]{1,0:T(8,128)(2,1)S(1)}, bf16[192,384]{1,0:T(8,128)(2,1)S(1)}, u32[]{:S(2)}, u32[]{:S(2)}) collective-permute-start(bf16[192,384]{1,0:T(8,128)(2,1)S(1)} %collective-permute-done.1), channel_id=1, source_target_pairs={{0,3},{1,0},{2,1},{3,2},{4,7},{5,4},{6,5},{7,6},{8,11},{9,8},{10,9... | collective-permute-start | bytes 442376 | tf_op jit(solution)/shard_map/ppermute | solution.py:802
  61.0 25.0 %collective-permute-start.6 = (bf16[256,1536]{1,0:T(8,128)(2,1)S(1)}, bf16[256,1536]{1,0:T(8,128)(2,1)}, u32[]{:S(2)}, u32[]{:S(2)}) collective-permute-start(bf16[256,1536]{1,0:T(8,128)(2,1)S(1)} %collective-permute-done.3.refs_2_), channel_id=1, source_target_pairs={{0,1},{1,2},{2,3},{3,0},{4,5},{5,6},{6,7},{7,4},{8,9},{9,10},{10,1... | collective-permute-start | bytes 2359304 | tf_op jit(solution)/shard_map/ppermute | solution.py:802
  102.6 23.4 %all-to-all-start = ((bf16[4,256,384]{2,1,0:T(8,128)(2,1)}), bf16[4,256,384]{2,1,0:T(8,128)(2,1)S(1)}, u32[]{:S(2)}, u32[]{:S(2)}) async-start(bf16[4,256,384]{2,1,0:T(8,128)(2,1)} %bitcast.10), calls=%async_computation | async-start | bytes 1572864 | tf_op jit(solution)/shard_map/all_to_all | solution.py:987
  106.2 197.5 %all-gather.3.cloned.1.call-start = ((), (), s32[]{:S(2)}) async-start(), calls=%async_computation.6 | async-start | bytes 13369344 | tf_op jit(solution)/shard_map/all_gather | solution.py:998
  109.2 27.4 %collective-permute-start.10 = (bf16[2,1,1,192,1536]{4,3,2,1,0:T(8,128)(2,1)}, bf16[2,1,1,192,1536]{4,3,2,1,0:T(8,128)(2,1)}, u32[]{:S(2)}, u32[]{:S(2)}) collective-permute-start(bf16[2,1,1,192,1536]{4,3,2,1,0:T(8,128)(2,1)} %maximum_select_fusion.3), channel_id=1, source_target_pairs={{0,8},{4,12},{8,0},{12,4},{1,9},{5,13},{9,1},{13,5},{2,10},{6,14},... | collective-permute-start | bytes 3538952 | tf_op jit(solution)/shard_map/ppermute | solution.py:807
  146.4 21.4 %collective-permute-start.13 = (bf16[256,1536]{1,0:T(8,128)(2,1)S(1)}, bf16[256,1536]{1,0:T(8,128)(2,1)S(1)}, u32[]{:S(2)}, u32[]{:S(2)}) collective-permute-start(bf16[256,1536]{1,0:T(8,128)(2,1)S(1)} %multiply_convert_fusion.refs_0_), channel_id=1, source_target_pairs={{0,1},{1,2},{2,3},{3,0},{4,5},{5,6},{6,7},{7,4},{8,9},{9,10},{10,1... | collective-permute-start | bytes 2359304 | tf_op jit(solution)/shard_map/ppermute | solution.py:802
  189.3 318.6 %reduce-scatter.2.cloned.1.call-start = ((), (), s32[]{:S(2)}) async-start(), calls=%async_computation.7 | async-start | bytes 13369344 | tf_op jit(solution)/shard_map/reduce_scatter | solution.py:1009
  189.4 30.8 %collective-permute-start.19 = (bf16[256,1536]{1,0:T(8,128)(2,1)}, bf16[256,1536]{1,0:T(8,128)(2,1)S(1)}, u32[]{:S(2)}, u32[]{:S(2)}) collective-permute-start(bf16[256,1536]{1,0:T(8,128)(2,1)} %copy-done.84), channel_id=1, source_target_pairs={{0,1},{1,2},{2,3},{3,0},{4,5},{5,6},{6,7},{7,4},{8,9},{9,10},{10,1... | collective-permute-start | bytes 2359304 | tf_op jit(solution)/shard_map/ppermute | solution.py:802
  189.8 30.3 %collective-permute-start.18 = (bf16[256,1536]{1,0:T(8,128)(2,1)}, bf16[256,1536]{1,0:T(8,128)(2,1)S(1)}, u32[]{:S(2)}, u32[]{:S(2)}) collective-permute-start(bf16[256,1536]{1,0:T(8,128)(2,1)} %copy-done.84), channel_id=1, source_target_pairs={{0,8},{4,12},{8,0},{12,4},{1,9},{5,13},{9,1},{13,5},{2,10},{6,14},... | collective-permute-start | bytes 2359304 | tf_op jit(solution)/shard_map/ppermute | solution.py:807
  190.8 26.4 %collective-permute-start.20 = (s32[4,8,256]{2,1,0:T(8,128)S(1)}, s32[4,8,256]{2,1,0:T(8,128)S(1)}, u32[]{:S(2)}, u32[]{:S(2)}) collective-permute-start(s32[4,8,256]{2,1,0:T(8,128)S(1)} %pad_add_fusion.2), channel_id=1, source_target_pairs={{0,1},{1,0},{2,3},{3,2},{4,5},{5,4},{6,7},{7,6},{8,9},{9,8},{10,11... | collective-permute-start | bytes 98312 | tf_op jit(solution)/shard_map/ppermute | solution.py:807
  191.5 47.3 %collective-permute-start.23 = (bf16[256,1536]{1,0:T(8,128)(2,1)S(1)}, bf16[256,1536]{1,0:T(8,128)(2,1)S(1)}, u32[]{:S(2)}, u32[]{:S(2)}) collective-permute-start(bf16[256,1536]{1,0:T(8,128)(2,1)S(1)} %multiply_convert_fusion.refs_0_), channel_id=1, source_target_pairs={{0,4},{4,0},{8,12},{12,8},{1,5},{5,1},{9,13},{13,9},{2,6},{6,2},{1... | collective-permute-start | bytes 2359304 | tf_op jit(solution)/shard_map/ppermute | solution.py:807
  191.5 47.8 %collective-permute-start.24 = (bf16[256,1536]{1,0:T(8,128)(2,1)}, bf16[256,1536]{1,0:T(8,128)(2,1)S(1)}, u32[]{:S(2)}, u32[]{:S(2)}) collective-permute-start(bf16[256,1536]{1,0:T(8,128)(2,1)} %copy-done.82), channel_id=1, source_target_pairs={{0,4},{4,0},{8,12},{12,8},{1,5},{5,1},{9,13},{13,9},{2,6},{6,2},{1... | collective-permute-start | bytes 2359304 | tf_op jit(solution)/shard_map/ppermute | solution.py:807
  217.2 21.6 %collective-permute-start.27 = (bf16[256,1536]{1,0:T(8,128)(2,1)}, bf16[256,1536]{1,0:T(8,128)(2,1)S(1)}, u32[]{:S(2)}, u32[]{:S(2)}) collective-permute-start(bf16[256,1536]{1,0:T(8,128)(2,1)} %copy-done.83), channel_id=1, source_target_pairs={{0,4},{4,0},{8,12},{12,8},{1,5},{5,1},{9,13},{13,9},{2,6},{6,2},{1... | collective-permute-start | bytes 2359304 | tf_op jit(solution)/shard_map/ppermute | solution.py:807
  290.5 385.8 %all-gather.5.cloned.1.call-start = ((), (), s32[]{:S(2)}) async-start(), calls=%async_computation.8 | async-start | bytes 8110080 | tf_op jit(solution)/shard_map/all_gather | solution.py:967
  335.4 41.2 %collective-permute-start.32 = (bf16[256,1536]{1,0:T(8,128)(2,1)}, bf16[256,1536]{1,0:T(8,128)(2,1)S(1)}, u32[]{:S(2)}, u32[]{:S(2)}) collective-permute-start(bf16[256,1536]{1,0:T(8,128)(2,1)} %get-tuple-element.245.refs_1_), channel_id=1, source_target_pairs={{0,16},{16,0},{1,17},{17,1},{2,18},{18,2},{3,19},{19,3},{4,20},{20... | collective-permute-start | bytes 2359304 | tf_op jit(solution)/shard_map/ppermute | solution.py:807
  335.5 42.0 %collective-permute-start.31 = (bf16[256,1536]{1,0:T(8,128)(2,1)}, bf16[256,1536]{1,0:T(8,128)(2,1)S(1)}, u32[]{:S(2)}, u32[]{:S(2)}) collective-permute-start(bf16[256,1536]{1,0:T(8,128)(2,1)} %get-tuple-element.243.refs_0_), channel_id=1, source_target_pairs={{0,16},{16,0},{1,17},{17,1},{2,18},{18,2},{3,19},{19,3},{4,20},{20... | collective-permute-start | bytes 2359304 | tf_op jit(solution)/shard_map/ppermute | solution.py:807
  403.0 40.5 %collective-permute-start.35 = (bf16[256,1536]{1,0:T(8,128)(2,1)}, bf16[256,1536]{1,0:T(8,128)(2,1)}, u32[]{:S(2)}, u32[]{:S(2)}) collective-permute-start(bf16[256,1536]{1,0:T(8,128)(2,1)} %get-tuple-element.392), channel_id=1, source_target_pairs={{0,8},{4,12},{8,0},{12,4},{1,9},{5,13},{9,1},{13,5},{2,10},{6,14},... | collective-permute-start | bytes 2359304 | tf_op jit(solution)/shard_map/ppermute | solution.py:807
  444.4 24.9 %collective-permute-start.38 = (bf16[256,1536]{1,0:T(8,128)(2,1)}, bf16[256,1536]{1,0:T(8,128)(2,1)}, u32[]{:S(2)}, u32[]{:S(2)}) collective-permute-start(bf16[256,1536]{1,0:T(8,128)(2,1)} %get-tuple-element.263), channel_id=1, source_target_pairs={{0,8},{4,12},{8,0},{12,4},{1,9},{5,13},{9,1},{13,5},{2,10},{6,14},... | collective-permute-start | bytes 2359304 | tf_op jit(solution)/shard_map/ppermute | solution.py:807
  448.7 26.8 %collective-permute-start.37 = (bf16[256,1536]{1,0:T(8,128)(2,1)S(1)}, bf16[256,1536]{1,0:T(8,128)(2,1)S(1)}, u32[]{:S(2)}, u32[]{:S(2)}) collective-permute-start(bf16[256,1536]{1,0:T(8,128)(2,1)S(1)} %add_convert_fusion.9), channel_id=1, source_target_pairs={{0,3},{1,0},{2,1},{3,2},{4,7},{5,4},{6,5},{7,6},{8,11},{9,8},{10,9... | collective-permute-start | bytes 2359304 | tf_op jit(solution)/shard_map/ppermute | solution.py:802
  450.5 25.3 %collective-permute-start.39 = (bf16[384,1024]{1,0:T(8,128)(2,1)S(1)}, bf16[384,1024]{1,0:T(8,128)(2,1)S(1)}, u32[]{:S(2)}, u32[]{:S(2)}) collective-permute-start(bf16[384,1024]{1,0:T(8,128)(2,1)S(1)} %copy-done.2), channel_id=1, source_target_pairs={{0,16},{16,0},{1,17},{17,1},{2,18},{18,2},{3,19},{19,3},{4,20},{20... | collective-permute-start | bytes 2359304 | tf_op jit(solution)/shard_map/ppermute | solution.py:807
  475.8 32.1 %collective-permute-start.41 = (bf16[256,1536]{1,0:T(8,128)(2,1)S(1)}, bf16[256,1536]{1,0:T(8,128)(2,1)}, u32[]{:S(2)}, u32[]{:S(2)}) collective-permute-start(bf16[256,1536]{1,0:T(8,128)(2,1)S(1)} %get-tuple-element.278), channel_id=1, source_target_pairs={{0,8},{4,12},{8,0},{12,4},{1,9},{5,13},{9,1},{13,5},{2,10},{6,14},... | collective-permute-start | bytes 2359304 | tf_op jit(solution)/shard_map/ppermute | solution.py:807
  479.2 35.5 %collective-permute-start.40 = (bf16[256,1536]{1,0:T(8,128)(2,1)}, bf16[256,1536]{1,0:T(8,128)(2,1)}, u32[]{:S(2)}, u32[]{:S(2)}) collective-permute-start(bf16[256,1536]{1,0:T(8,128)(2,1)} %add_convert_fusion.6), channel_id=1, source_target_pairs={{0,3},{1,0},{2,1},{3,2},{4,7},{5,4},{6,5},{7,6},{8,11},{9,8},{10,9... | collective-permute-start | bytes 2359304 | tf_op jit(solution)/shard_map/ppermute | solution.py:802
  484.6 31.6 %collective-permute-start.42 = (bf16[384,1024]{1,0:T(8,128)(2,1)S(1)}, bf16[384,1024]{1,0:T(8,128)(2,1)}, u32[]{:S(2)}, u32[]{:S(2)}) collective-permute-start(bf16[384,1024]{1,0:T(8,128)(2,1)S(1)} %copy-done.3), channel_id=1, source_target_pairs={{0,16},{16,0},{1,17},{17,1},{2,18},{18,2},{3,19},{19,3},{4,20},{20... | collective-permute-start | bytes 2359304 | tf_op jit(solution)/shard_map/ppermute | solution.py:807
  555.5 24.8 %all-to-all-start.2 = ((bf16[4,256,384]{2,1,0:T(8,128)(2,1)}), bf16[4,256,384]{2,1,0:T(8,128)(2,1)}, u32[]{:S(2)}, u32[]{:S(2)}) async-start(bf16[4,256,384]{2,1,0:T(8,128)(2,1)} %pad_maximum_fusion.1), calls=%async_computation.3 | async-start | bytes 1572864 | tf_op jit(solution)/shard_map/all_to_all | solution.py:1109
  581.5 31.6 %collective-permute-start.50 = (bf16[2,1,1,192,1536]{4,3,2,1,0:T(8,128)(2,1)}, bf16[2,1,1,192,1536]{4,3,2,1,0:T(8,128)(2,1)S(1)}, u32[]{:S(2)}, u32[]{:S(2)}) collective-permute-start(bf16[2,1,1,192,1536]{4,3,2,1,0:T(8,128)(2,1)} %get-tuple-element.318), channel_id=1, source_target_pairs={{0,8},{4,12},{8,0},{12,4},{1,9},{5,13},{9,1},{13,5},{2,10},{6,14},... | collective-permute-start | bytes 3538952 | tf_op jit(solution)/shard_map/ppermute | solution.py:807
  584.4 30.0 %collective-permute-start.53 = (bf16[384,1024]{1,0:T(8,128)(2,1)}, bf16[384,1024]{1,0:T(8,128)(2,1)S(1)}, u32[]{:S(2)}, u32[]{:S(2)}) collective-permute-start(bf16[384,1024]{1,0:T(8,128)(2,1)} %get-tuple-element.325.refs_0_), channel_id=1, source_target_pairs={{0,16},{16,0},{1,17},{17,1},{2,18},{18,2},{3,19},{19,3},{4,20},{20... | collective-permute-start | bytes 2359304 | tf_op jit(solution)/shard_map/ppermute | solution.py:807
  588.4 23.9 %collective-permute-start.52 = (f32[32,1536]{1,0:T(8,128)S(1)}, f32[32,1536]{1,0:T(8,128)S(1)}, u32[]{:S(2)}, u32[]{:S(2)}) collective-permute-start(f32[32,1536]{1,0:T(8,128)S(1)} %add.420), channel_id=1, source_target_pairs={{0,2},{1,3},{2,0},{3,1},{4,6},{5,7},{6,4},{7,5},{8,10},{9,11},{10,... | collective-permute-start | bytes 589832 | tf_op jit(solution)/shard_map/ppermute | solution.py:807
  616.4 34.1 %all-to-all-start.3 = ((bf16[4,256,640]{2,1,0:T(8,128)(2,1)}), bf16[4,256,640]{2,1,0:T(8,128)(2,1)}, u32[]{:S(2)}, u32[]{:S(2)}) async-start(bf16[4,256,640]{2,1,0:T(8,128)(2,1)} %bitcast.31), calls=%async_computation.4 | async-start | bytes 2621440 | tf_op jit(solution)/shard_map/all_to_all | solution.py:1135
  635.9 30.4 %collective-permute-start.59 = (bf16[384,1024]{1,0:T(8,128)(2,1)}, bf16[384,1024]{1,0:T(8,128)(2,1)}, u32[]{:S(2)}, u32[]{:S(2)}) collective-permute-start(bf16[384,1024]{1,0:T(8,128)(2,1)} %get-tuple-element.353.refs_2_), channel_id=1, source_target_pairs={{0,16},{16,0},{1,17},{17,1},{2,18},{18,2},{3,19},{19,3},{4,20},{20... | collective-permute-start | bytes 2359304 | tf_op jit(solution)/shard_map/ppermute | solution.py:807
  667.3 28.9 %all-to-all-start.4 = ((bf16[4,1,1,1,192,384]{5,4,3,2,1,0:T(8,128)(2,1)}), bf16[4,1,1,1,192,384]{5,4,3,2,1,0:T(8,128)(2,1)}, u32[]{:S(2)}, u32[]{:S(2)}) async-start(bf16[4,1,1,1,192,384]{5,4,3,2,1,0:T(8,128)(2,1)} %pad_maximum_fusion.2), calls=%async_computation.5 | async-start | bytes 1179648 | tf_op jit(solution)/shard_map/all_to_all | solution.py:1172
  (139 other events, 1691.5 us)
Sparse Core Ops, SparseCore 0:
  189.4 114.2 all-gather.2
  308.4 142.1 reduce-scatter.1
Sparse Core Ops, SparseCore 1:
  378.8 144.7 all-gather.4

commit v3 on v1

v3 whole, which is shorter than its diff:
```python
import functools
import math

import jax
import jax.numpy as jnp
from jax import lax
from jax.experimental import pallas as pl
from jax.experimental.pallas import tpu as pltpu
from jax.sharding import PartitionSpec as P

HD = 64
FFE = 512
TOP = 8
REP = 3
SEQ_MAX = 512

EPSILON = 1e-06
HIGHEST = lax.Precision.HIGHEST
MASKED_SCORE = -1e30
F32 = jnp.float32
BF16 = jnp.bfloat16


def dot_nn(left, right):
    return lax.dot_general(left, right, (((1,), (0,)), ((), ())), preferred_element_type=F32)


def dot_nt(left, right):
    return lax.dot_general(left, right, (((1,), (1,)), ((), ())), preferred_element_type=F32)


def dot_tn(left, right):
    return lax.dot_general(left, right, (((0,), (0,)), ((), ())), preferred_element_type=F32)


def lane_low(shape):
    return lax.broadcasted_iota(jnp.int32, shape, 1) < HD


def twist(tile_vals):
    width = tile_vals.shape[1]
    lane = lax.broadcasted_iota(jnp.int32, tile_vals.shape, 1)
    ahead = pltpu.roll(tile_vals, width - HD // 2, 1)
    behind = pltpu.roll(tile_vals, HD // 2, 1)
    return jnp.where(lane % HD < HD // 2, -ahead, behind)


def both_halves(tile_vals, low):
    kept = jnp.where(lane_low(tile_vals.shape) == low, tile_vals, 0.0)
    return kept + pltpu.roll(kept, HD, 1)


def head_places():
    per = REP + 2
    def at(index):
        return (index // 2, index % 2 == 0)
    groups = []
    for g in range(2):
        base = g * per
        groups.append(
            ([at(base + r) for r in range(REP)], at(base + REP), at(base + REP + 1))
        )
    return groups


def chunk_span(a, tok):
    reach = -(-(SEQ_MAX - 1) // tok)
    return max(0, a - reach) * tok, (a + 1) * tok


def mask_bias(start_row, a, tok):
    low, high = chunk_span(a, tok)
    shape = (high - low, tok)
    keys = lax.broadcasted_iota(jnp.int32, shape, 0) + low
    queries = lax.broadcasted_iota(jnp.int32, shape, 1) + a * tok
    allowed = (keys >= start_row) & (keys <= queries)
    return jnp.where(allowed, 0.0, MASKED_SCORE)


def attn_forward_body(
    chunks, here_ref, *refs,
):
    ins, (w_ref, cos_ref, sin_ref, start_ref, qkv_ref, kk_ref, vv_ref, lse_ref, heads_ref) = (
        refs[:chunks],
        refs[chunks:],
    )
    tok = ins[0].shape[0]
    here = here_ref[0]
    places = head_places()
    for k in range(chunks):
        a = lax.rem(here + (chunks - k), chunks)
        at = pl.ds(pl.multiple_of(a * tok, tok), tok)
        mixed = dot_nn(ins[k][...], w_ref[...])
        cos = cos_ref[at, :]
        sin = sin_ref[at, :]
        tiles = [mixed[:, 128 * i : 128 * (i + 1)] for i in range(mixed.shape[1] // 128)]
        turned = [t * cos + twist(t) * sin for t in tiles]
        for g, (queries, key, value) in enumerate(places):
            for r, (tile_at, low) in enumerate(queries):
                part = jnp.where(lane_low(tiles[0].shape) == low, turned[tile_at], 0.0)
                slot = 128 * (g * REP + r)
                qkv_ref[at, slot : slot + 128] = part.astype(BF16)
            kk_ref[at, 128 * g : 128 * (g + 1)] = both_halves(turned[key[0]], key[1]).astype(BF16)
            vv_ref[at, 128 * g : 128 * (g + 1)] = both_halves(tiles[value[0]], value[1]).astype(BF16)
    for a in range(chunks):
        low_key, high_key = chunk_span(a, tok)
        bias = mask_bias(start_ref[a : a + 1, :], a, tok)
        out = [None] * REP
        for g, (queries, _, _) in enumerate(places):
            keys = kk_ref[low_key:high_key, 128 * g : 128 * (g + 1)]
            vals = vv_ref[low_key:high_key, 128 * g : 128 * (g + 1)]
            for r in range(REP):
                head = g * REP + r
                q = qkv_ref[a * tok : (a + 1) * tok, 128 * head : 128 * (head + 1)]
                scores = dot_nt(keys, q) * HD ** (-0.5) + bias
                top = jnp.max(scores, axis=0, keepdims=True)
                terms = jnp.exp(scores - top)
                total = jnp.sum(terms, axis=0, keepdims=True)
                probs = (terms * (1.0 / total)).astype(BF16)
                lse_ref[head, a : a + 1, :] = top + jnp.log(total)
                mix = dot_tn(probs, vals)
                t = head // 2
                low = lane_low(mix.shape)
                out[t] = mix if head % 2 == 0 else jnp.where(low, out[t], mix)
        for t in range(REP):
            heads_ref[a * tok : (a + 1) * tok, 128 * t : 128 * (t + 1)] = out[t].astype(BF16)


def whole_block(values):
    zeros = (0,) * len(values.shape)
    return pl.BlockSpec(values.shape, lambda i: zeros, pipeline_mode=pl.Buffered(1))


def attn_forward(here, parts, w_cols, cos, sin, starts):
    chunks = len(parts)
    tok, feat = parts[0].shape
    total = chunks * tok
    cols = w_cols.shape[1]
    return pl.pallas_call(
        functools.partial(attn_forward_body, chunks),
        grid=(1,),
        in_specs=[pl.BlockSpec(memory_space=pltpu.SMEM)]
        + [whole_block(v) for v in (*parts, w_cols, cos, sin, starts)],
        out_specs=[
            whole_block(jax.ShapeDtypeStruct(s, F32))
            for s in (
                (total, 128 * 2 * REP), (total, 256), (total, 256), (2 * REP, 8, tok),
                (total, 2 * REP * HD),
            )
        ],
        out_shape=[
            jax.ShapeDtypeStruct((total, 128 * 2 * REP), BF16),
            jax.ShapeDtypeStruct((total, 256), BF16),
            jax.ShapeDtypeStruct((total, 256), BF16),
            jax.ShapeDtypeStruct((2 * REP, 8, tok), F32),
            jax.ShapeDtypeStruct((total, 2 * REP * HD), BF16),
        ],
        compiler_params=pltpu.CompilerParams(vmem_limit_bytes=60 * 1024 * 1024),
        cost_estimate=pl.CostEstimate(
            flops=2 * total * feat * cols * 4, bytes_accessed=8 * total * cols, transcendentals=0
        ),
        name="attn_forward",
    )(here, *parts, w_cols, cos, sin, starts)


def attn_backward_body(
    chunks, here_ref, grads_ref, q_ref, kk_ref, vv_ref, lse_ref, cos_ref, sin_ref, start_ref,
    turned_ref, dk, dv, dq,
):
    tok = q_ref.shape[0] // chunks
    here = here_ref[0]
    dk[...] = jnp.zeros_like(dk)
    dv[...] = jnp.zeros_like(dv)
    for a in range(chunks):
        low_key, high_key = chunk_span(a, tok)
        bias = mask_bias(start_ref[a : a + 1, :], a, tok)
        for g in range(2):
            keys = kk_ref[low_key:high_key, 128 * g : 128 * (g + 1)]
            vals = vv_ref[low_key:high_key, 128 * g : 128 * (g + 1)]
            for r in range(REP):
                head = g * REP + r
                q = q_ref[a * tok : (a + 1) * tok, 128 * head : 128 * (head + 1)]
                t, is_low = head // 2, head % 2 == 0
                pair = grads_ref[a * tok : (a + 1) * tok, 128 * t : 128 * (t + 1)]
                grad = jnp.where(lane_low(pair.shape) == is_low, pair, jnp.zeros_like(pair))
                scores = dot_nt(keys, q) * HD ** (-0.5) + bias
                probs = jnp.exp(scores - lse_ref[head, a : a + 1, :])
                grad_probs = dot_nt(vals, grad)
                dv[low_key:high_key, 128 * g : 128 * (g + 1)] += dot_nn(probs.astype(BF16), grad)
                inner = jnp.sum(probs * grad_probs, axis=0, keepdims=True)
                grad_scores = (probs * (grad_probs - inner)).astype(BF16)
                dk[low_key:high_key, 128 * g : 128 * (g + 1)] += dot_nn(grad_scores, q)
                part = dot_tn(grad_scores, keys)
                here_at = slice(128 * t, 128 * (t + 1))
                rows = slice(a * tok, (a + 1) * tok)
                if is_low:
                    dq[rows, here_at] = part
                else:
                    dq[rows, here_at] = jnp.where(lane_low(part.shape), dq[rows, here_at], part)
    for a in range(chunks):
        rows = slice(a * tok, (a + 1) * tok)
        to = pl.ds(pl.multiple_of(lax.rem(here + (chunks - a), chunks) * tok, tok), tok)
        cos = cos_ref[rows, :]
        sin = sin_ref[rows, :]

        def back(vals):
            return (vals * cos - twist(vals) * sin) * HD ** (-0.5)

        def whole(vals):
            return vals + pltpu.roll(vals, HD, 1)

        low = lane_low((tok, 128))
        keys = [back(whole(dk[rows, 128 * g : 128 * (g + 1)])) for g in range(2)]
        vals = [whole(dv[rows, 128 * g : 128 * (g + 1)]) for g in range(2)]
        qs = [back(dq[rows, 128 * t : 128 * (t + 1)]) for t in range(REP)]
        tiles = [
            qs[0],
            jnp.where(low, qs[1], keys[0]),
            jnp.where(low, vals[0], qs[1]),
            qs[2],
            jnp.where(low, keys[1], vals[1]),
        ]
        for i, vals_of in enumerate(tiles):
            turned_ref[to, 128 * i : 128 * (i + 1)] = vals_of.astype(BF16)


def attn_backward(here, grads, q_rows, key_rows, value_rows, lse, cos, sin, starts, chunks):
    total = q_rows.shape[0]
    cols = 2 * (REP + 2) * HD
    return pl.pallas_call(
        functools.partial(attn_backward_body, chunks),
        grid=(1,),
        in_specs=[pl.BlockSpec(memory_space=pltpu.SMEM)]
        + [
            whole_block(v)
            for v in (grads, q_rows, key_rows, value_rows, lse, cos, sin, starts)
        ],
        out_specs=whole_block(jax.ShapeDtypeStruct((total, cols), BF16)),
        out_shape=jax.ShapeDtypeStruct((total, cols), BF16),
        scratch_shapes=[
            pltpu.VMEM((total, 256), F32),
            pltpu.VMEM((total, 256), F32),
            pltpu.VMEM((total, 2 * REP * HD), F32),
        ],
        compiler_params=pltpu.CompilerParams(vmem_limit_bytes=60 * 1024 * 1024),
        cost_estimate=beside_transfers(),
        name="attn_backward",
    )(here, grads, q_rows, key_rows, value_rows, lse, cos, sin, starts)


def hot_rows(srow, cap, tok):
    places = lax.broadcasted_iota(jnp.int32, (cap, tok), 0).astype(F32)
    return srow == places


def one_zero(mask):
    return jnp.where(mask, 1.0, 0.0).astype(BF16)


def front_body(
    cap, tile, tiles, group, sources,
    first_ref, ids_ref, offs_ref, *refs,
):
    x_refs = refs[:sources]
    (
        rt_ref, rs_ref, win_ref, wdn_ref, res_ref, rows_ref, ab_ref, gate_ref, slot_ref,
        buf, gate, arena, sems,
    ) = refs[sources:]
    step = pl.program_id(0)
    tok, feat = arena.shape[1:]
    experts = rs_ref.shape[1] // 4
    local = buf.shape[0]
    ff = wdn_ref.shape[1]
    first_work = sources // group

    def fetch(at):
        where = at % 2 * group
        return [
            pltpu.make_async_copy(x_refs[at * group + s], arena.at[where + s], sems.at[where + s])
            for s in range(group)
        ]

    @pl.when(step < first_work)
    def _gather():
        @pl.when(step == 0)
        def _():
            for copy in fetch(0) + fetch(1):
                copy.start()

        here = step % 2 * group
        for s in range(group):
            pltpu.make_async_copy(x_refs[0], arena.at[here + s], sems.at[here + s]).wait()

        ids = lax.broadcasted_iota(jnp.int32, (experts, tok), 0)
        before = one_zero(
            lax.broadcasted_iota(jnp.int32, (tok, tok), 0)
            < lax.broadcasted_iota(jnp.int32, (tok, tok), 1)
        )
        srows, grows = [], []
        for s in range(group):
            thirds = dot_nn(arena[here + s], rs_ref[...]).T
            logits = (
                thirds[2 * experts : 3 * experts] + thirds[experts : 2 * experts]
            ) + thirds[:experts]
            rt = rt_ref[ids_ref[0, step * group + s]]
            used = ids == rt[0:1]
            for k in range(1, rt.shape[0]):
                used = used | (ids == rt[k : k + 1])
            top = jnp.max(jnp.where(used, logits, MASKED_SCORE), axis=0, keepdims=True)
            terms = jnp.where(used, jnp.exp(logits - top), 0.0)
            gates = terms / jnp.sum(terms, axis=0, keepdims=True)
            used_f = jnp.where(used, 1.0, 0.0)
            rank = dot_nn(used_f.astype(BF16), before)
            for e in range(local):
                mine = ids == first_ref[0] + e
                grows.append(jnp.sum(jnp.where(mine, gates, 0.0), axis=0, keepdims=True))
                srow = jnp.sum(jnp.where(mine & used, rank + 1.0, 0.0), axis=0, keepdims=True) - 1.0
                srows.append(srow)
        for s in range(group):
            hots = [hot_rows(srows[s * local + e], cap, tok) for e in range(local)]
            picked = dot_nn(one_zero(jnp.concatenate(hots, axis=0)), arena[here + s]).astype(BF16)
            for e in range(local):
                at = pl.ds(pl.multiple_of(offs_ref[e, step * group + s], 16), cap)
                slot_ref[e, pl.ds(step * group + s, 1), :] = srows[s * local + e]
                gcol = jnp.sum(
                    jnp.where(hots[e], grows[s * local + e], 0.0), axis=1, keepdims=True
                )
                gate[e, at, :] = jnp.broadcast_to(gcol, (cap, 128))
                buf[e, at, :] = picked[e * cap : (e + 1) * cap]

        for later in range(2, first_work):

            @pl.when(step + 2 == later)
            def _(later=later):
                for copy in fetch(later):
                    copy.start()

        @pl.when(step == first_work - 1)
        def _():
            for e in range(local):
                end = pl.multiple_of(offs_ref[e, sources], 16)
                buf[e, pl.ds(end, tile), :] = jnp.zeros((tile, feat), BF16)
                gate[e, pl.ds(end, tile), :] = jnp.zeros((tile, 128), F32)

    work = step - first_work
    e = work // tiles
    j = work % tiles

    @pl.when((work >= 0) & (work < local * tiles))
    def _experts():
        @pl.when(j * tile < offs_ref[e, sources])
        def _():
            at = pl.ds(pl.multiple_of(j * tile, tile), tile)
            rows = buf[e, at, :]
            g = gate[e, at, :]
            rows_ref[0] = rows
            gate_ref[0] = g
            a = dot_nn(rows, win_ref[0, :, :ff])
            b = dot_nn(rows, win_ref[0, :, ff:])
            ab_ref[0, :, :ff] = a
            ab_ref[0, :, ff:] = b
            act_g = (g[:, 0:1] * (a / (1.0 + jnp.exp(-a)) * b)).astype(BF16)
            buf[e, at, :] = dot_nn(act_g, wdn_ref[0]).astype(BF16)

    back = work - local * tiles

    @pl.when(back >= 0)
    def _scatter():
        for s in range(group):
            source = ids_ref[1, back * group + s]
            hots, terms = [], []
            for e in range(local):
                hots.append(hot_rows(slot_ref[e, pl.ds(source, 1), :], cap, tok))
                off = pl.multiple_of(offs_ref[e, source], 16)
                terms.append(buf[e, pl.ds(off, cap), :])
            total = dot_tn(
                one_zero(jnp.concatenate(hots, axis=0)), jnp.concatenate(terms, axis=0)
            )
            res_ref[s * tok : (s + 1) * tok, :] = total.astype(BF16)


def moe_front(first, ids, offs, x_parts, rt_all, router_parts, w_in, w_down, cap, group):
    sources, top, tok = rt_all.shape
    feat = x_parts[0].shape[1]
    local, _, ff2 = w_in.shape
    ff = ff2 // 2
    most = sources * cap
    tile = min(256, most)
    tiles = most // tile
    room = most + max(tile, cap)
    steps = sources // group
    middle = local * tiles

    def exp3(i, f, ids, offs):
        return (jnp.clip((i - steps) // tiles, 0, local - 1), 0, 0)

    def tile3(i, f, ids, offs):
        at = jnp.clip(i - steps, 0, middle - 1)
        return (at // tiles, at % tiles, 0)

    return pl.pallas_call(
        functools.partial(front_body, cap, tile, tiles, group, sources),
        grid_spec=pltpu.PrefetchScalarGridSpec(
            num_scalar_prefetch=3,
            grid=(2 * steps + middle,),
            in_specs=[pl.BlockSpec(memory_space=pl.ANY)] * sources
            + [
                pl.BlockSpec(rt_all.shape, lambda i, f, ids, offs: (0, 0, 0)),
                pl.BlockSpec(router_parts.shape, lambda i, f, ids, offs: (0, 0)),
                pl.BlockSpec((1, feat, ff2), exp3),
                pl.BlockSpec((1, ff, feat), exp3),
            ],
            out_specs=[
                pl.BlockSpec(
                    (group * tok, feat), lambda i, f, ids, offs: (jnp.maximum(i - steps - middle, 0), 0)
                ),
                pl.BlockSpec((1, tile, feat), tile3),
                pl.BlockSpec((1, tile, ff2), tile3),
                pl.BlockSpec((1, tile, 128), tile3),
                pl.BlockSpec((local, sources, tok), lambda i, f, ids, offs: (0, 0, 0)),
            ],
            scratch_shapes=[
                pltpu.VMEM((local, room, feat), BF16),
                pltpu.VMEM((local, room, 128), F32),
                pltpu.VMEM((2 * group, tok, feat), BF16),
                pltpu.SemaphoreType.DMA((2 * group,)),
            ],
        ),
        out_shape=[
            jax.ShapeDtypeStruct((sources * tok, feat), BF16),
            jax.ShapeDtypeStruct((local, most, feat), BF16),
            jax.ShapeDtypeStruct((local, most, ff2), F32),
            jax.ShapeDtypeStruct((local, most, 128), F32),
            jax.ShapeDtypeStruct((local, sources, tok), F32),
        ],
        compiler_params=pltpu.CompilerParams(vmem_limit_bytes=56 * 1024 * 1024),
        cost_estimate=pl.CostEstimate(
            flops=2 * most * feat * ff * 3, bytes_accessed=10 * most * feat, transcendentals=0
        ),
        name="moe_front",
    )(first, ids, offs, *x_parts, rt_all, router_parts, w_in, w_down)


def back_tile(rows, ab_ref, grads, g, win_ref, wdn_ref, acc_i, acc_d):
    ff = wdn_ref.shape[1]
    a = ab_ref[0, :, :ff]
    b = ab_ref[0, :, ff:]
    ga = dot_nt(grads, wdn_ref[0])
    sig = 1.0 / (1.0 + jnp.exp(-a))
    silu = a * sig
    act = silu * b
    gate_grad = jnp.sum(act * ga, axis=1, keepdims=True)
    gag = g * ga
    da = (gag * b * (sig * (1.0 + a * (1.0 - sig)))).astype(BF16)
    db = (gag * silu).astype(BF16)
    act_g = (g * act).astype(BF16)
    acc_d[...] += dot_tn(act_g, grads)
    acc_i[:, :ff] += dot_tn(rows, da)
    acc_i[:, ff:] += dot_tn(rows, db)
    pair = dot_nt(da, win_ref[0, :, :ff]) + dot_nt(db, win_ref[0, :, ff:])
    return pair.astype(BF16), gate_grad


def piece_shapes(feat, ff, first):
    down, rows = [ff // 2, ff // 2], [feat // 3] * 3
    if first:
        down, rows = [ff], [feat // 4, feat // 3, feat // 12 * 5]
    return [(n, feat) for n in down], [(n, 2 * ff) for n in rows]


def write_pieces(acc_i, acc_d, refs):
    at = 0
    for ref in refs:
        acc = acc_d if ref.shape[1] == acc_d.shape[1] else acc_i
        ref[...] = acc[at : at + ref.shape[0], :].astype(BF16)
        at = (at + ref.shape[0]) % acc.shape[0]


def back_first_body(
    cap, tile, tiles, group,
    offs_ref, ids_ref, *refs,
):
    dy_refs = refs[:group]
    (slot_ref, rows_ref, ab_ref, gate_ref, win_ref, wdn_ref, pair_ref, gg_ref, other_ref, *piece_refs, buf, acc_i, acc_d) = refs[group:]
    step = pl.program_id(0)
    sources = slot_ref.shape[1]
    local = buf.shape[0]
    tok, feat = dy_refs[0].shape
    first_work = sources // group

    @pl.when(step < first_work)
    def _gather():
        for s in range(group):
            source = step * group + s
            hots = [hot_rows(slot_ref[e, pl.ds(source, 1), :], cap, tok) for e in range(local)]
            picked = dot_nn(
                one_zero(jnp.concatenate(hots, axis=0)), dy_refs[s][...]
            ).astype(BF16)
            for e in range(local):
                off = pl.multiple_of(offs_ref[e, source], 16)
                buf[e, pl.ds(off, cap), :] = picked[e * cap : (e + 1) * cap]

        @pl.when(step == first_work - 1)
        def _():
            for e in range(local):
                end = pl.multiple_of(offs_ref[e, sources], 16)
                buf[e, pl.ds(end, tile), :] = jnp.zeros((tile, feat), BF16)
            acc_i[...] = jnp.zeros_like(acc_i)
            acc_d[...] = jnp.zeros_like(acc_d)

    j = step - first_work

    @pl.when(j >= 0)
    def _experts():
        at = pl.ds(pl.multiple_of(j * tile, tile), tile)

        @pl.when(j * tile < offs_ref[1, sources])
        def _():
            other_ref[0] = buf[1, at, :]

        @pl.when(j * tile < offs_ref[0, sources])
        def _():
            pair, gate_grad = back_tile(
                rows_ref[0], ab_ref, buf[0, at, :], gate_ref[0, :, 0:1], win_ref, wdn_ref, acc_i, acc_d
            )
            pair_ref[...] = pair
            gg_ref[...] = jnp.broadcast_to(gate_grad, (tile, 128))

        @pl.when(j * tile >= offs_ref[0, sources])
        def _():
            pair_ref[...] = jnp.zeros_like(pair_ref)
            gg_ref[...] = jnp.zeros_like(gg_ref)

        @pl.when(j == tiles - 1)
        def _():
            write_pieces(acc_i, acc_d, piece_refs)


def used_tile(j, offs, e, sources, tile):
    return jnp.clip(j, 0, jnp.maximum((offs[e, sources] + (tile - 1)) // tile - 1, 0))


def moe_back_first(offs, ids, dy_all, slot, rows, ab, gate, w_in, w_down, cap, group):
    local, sources, tok = slot.shape
    most, feat = rows.shape[1:]
    ff2 = w_in.shape[2]
    ff = ff2 // 2
    tile = min(256, most)
    tiles = most // tile
    room = most + max(tile, cap)
    steps = sources // group

    def in_tile(i, offs, ids):
        return (0, used_tile(i - steps, offs, 0, sources, tile), 0)

    def out_tile(i, offs, ids):
        return (jnp.maximum(i - steps, 0), 0)

    def other_tile(i, offs, ids):
        return (0, used_tile(i - steps, offs, 1, sources, tile), 0)

    def source(s):
        return lambda i, offs, ids: (ids[2, jnp.minimum(i, steps - 1) * group + s], 0)

    return pl.pallas_call(
        functools.partial(back_first_body, cap, tile, tiles, group),
        grid_spec=pltpu.PrefetchScalarGridSpec(
            num_scalar_prefetch=2,
            grid=(steps + tiles,),
            in_specs=[pl.BlockSpec((tok, feat), source(s)) for s in range(group)]
            + [
                pl.BlockSpec(slot.shape, lambda i, offs, ids: (0, 0, 0)),
                pl.BlockSpec((1, tile, feat), in_tile),
                pl.BlockSpec((1, tile, ff2), in_tile),
                pl.BlockSpec((1, tile, 128), in_tile),
                pl.BlockSpec((1, feat, ff2), lambda i, offs, ids: (0, 0, 0)),
                pl.BlockSpec((1, ff, feat), lambda i, offs, ids: (0, 0, 0)),
            ],
            out_specs=[
                pl.BlockSpec((tile, feat), out_tile),
                pl.BlockSpec((tile, 128), out_tile),
                pl.BlockSpec((1, tile, feat), other_tile),
                *[pl.BlockSpec(s, lambda i, offs, ids: (0, 0)) for s in sum(piece_shapes(feat, ff, True), [])],
            ],
            scratch_shapes=[
                pltpu.VMEM((local, room, feat), BF16),
                pltpu.VMEM((feat, ff2), F32),
                pltpu.VMEM((ff, feat), F32),
            ],
        ),
        out_shape=[
            jax.ShapeDtypeStruct((most, feat), BF16),
            jax.ShapeDtypeStruct((most, 128), F32),
            jax.ShapeDtypeStruct((1, most, feat), BF16),
            *[jax.ShapeDtypeStruct(s, BF16) for s in sum(piece_shapes(feat, ff, True), [])],
        ],
        compiler_params=pltpu.CompilerParams(vmem_limit_bytes=56 * 1024 * 1024),
        cost_estimate=pl.CostEstimate(
            flops=2 * most * feat * ff * 4, bytes_accessed=5 * dy_all.size * 2, transcendentals=0
        ),
        name="moe_back_first",
    )(offs, ids, *[dy_all] * group, slot, rows, ab, gate, w_in, w_down)


def back_last_body(
    cap, tile, tiles, group,
    offs_ref, ids_ref, slot_ref, rows_ref, ab_ref, grads_ref, gate_ref, win_ref, wdn_ref, pair0_any, gg0_any,
    far_ref, near_ref, dg_ref, *rest,
):
    *piece_refs, buf, gg, acc_i, acc_d, pair0_ref, gg0_ref, stage_d, stage_i, sems = rest
    step = pl.program_id(0)
    sources, tok = slot_ref.shape[1:]
    feat = far_ref.shape[1]

    def held_copies():
        return [
            pltpu.make_async_copy(pair0_any, pair0_ref, sems.at[0]),
            pltpu.make_async_copy(gg0_any, gg0_ref, sems.at[1]),
        ]

    def piece_copies():
        copies, at = [], 0
        for ref in piece_refs:
            stage = stage_d if ref.shape[1] == stage_d.shape[1] else stage_i
            copies.append(
                pltpu.make_async_copy(
                    stage.at[pl.ds(at, ref.shape[0]), :], ref, sems.at[2 + len(copies)]
                )
            )
            at = (at + ref.shape[0]) % stage.shape[0]
        return copies

    @pl.when(step == 0)
    def _():
        for copy in held_copies():
            copy.start()
        acc_i[...] = jnp.zeros_like(acc_i)
        acc_d[...] = jnp.zeros_like(acc_d)

    @pl.when(step < tiles)
    def _experts():
        at = pl.ds(pl.multiple_of(step * tile, tile), tile)

        @pl.when(step * tile < offs_ref[1, sources])
        def _():
            pair, gate_grad = back_tile(
                rows_ref[0], ab_ref, grads_ref[0], gate_ref[0, :, 0:1], win_ref, wdn_ref, acc_i, acc_d
            )
            buf[at, :] = pair
            gg[at, :] = jnp.broadcast_to(gate_grad, (tile, 128))

        @pl.when(step * tile >= offs_ref[1, sources])
        def _():
            buf[at, :] = jnp.zeros((tile, feat), BF16)
            gg[at, :] = jnp.zeros((tile, 128), F32)

        @pl.when(step == tiles - 1)
        def _():
            stage_d[...] = acc_d[...].astype(BF16)
            stage_i[...] = acc_i[...].astype(BF16)
            for copy in piece_copies():
                copy.start()
            for copy in held_copies():
                copy.wait()

    back = step - tiles

    @pl.when(back >= 0)
    def _scatter():
        for s in range(group):
            source = lax.rem(back * group + s + sources // 2, sources)
            to = ids_ref[3, source]
            hots, terms = [], []
            for e, (pair, grads) in enumerate(((pair0_ref, gg0_ref), (buf, gg))):
                hot = hot_rows(slot_ref[e, pl.ds(source, 1), :], cap, tok)
                at = pl.ds(pl.multiple_of(offs_ref[e, source], 16), cap)
                hots.append(hot)
                terms.append(pair[at, :])
                dg_ref[to, e : e + 1, :] = jnp.sum(
                    jnp.where(hot, grads[at, 0:1], 0.0), axis=0, keepdims=True
                )
            dg_ref[to, 2:, :] = jnp.zeros((dg_ref.shape[1] - 2, tok), F32)
            total = dot_tn(
                one_zero(jnp.concatenate(hots, axis=0)), jnp.concatenate(terms, axis=0)
            )
            total = total.astype(BF16)

            @pl.when(back < sources // (2 * group))
            def _(total=total, s=s):
                far_ref[s * tok : (s + 1) * tok, :] = total

            @pl.when(back >= sources // (2 * group))
            def _(total=total, s=s):
                near_ref[s * tok : (s + 1) * tok, :] = total

        @pl.when(step == pl.num_programs(0) - 1)
        def _():
            for copy in piece_copies():
                copy.wait()


def moe_back_last(offs, ids, slot, rows, ab, grads, gate, w_in, w_down, pair0, gg0, cap, group):
    local, sources, tok = slot.shape
    most, feat = rows.shape[1:]
    ff2 = w_in.shape[2]
    ff = ff2 // 2
    tile = min(256, most)
    tiles = most // tile
    steps = sources // group

    def in_tile(i, offs, ids):
        return (1, used_tile(i, offs, 1, sources, tile), 0)

    def own_tile(i, offs, ids):
        return (0, used_tile(i, offs, 1, sources, tile), 0)

    def whole(i, offs, ids):
        return (0, 0)

    def far(i, offs, ids):
        return (jnp.clip(i - tiles, 0, steps // 2 - 1), 0)

    def near(i, offs, ids):
        return (jnp.clip(i - tiles - steps // 2, 0, steps // 2 - 1), 0)

    return pl.pallas_call(
        functools.partial(back_last_body, cap, tile, tiles, group),
        grid_spec=pltpu.PrefetchScalarGridSpec(
            num_scalar_prefetch=2,
            grid=(steps + tiles,),
            in_specs=[
                pl.BlockSpec(slot.shape, lambda i, offs, ids: (0, 0, 0)),
                pl.BlockSpec((1, tile, feat), in_tile),
                pl.BlockSpec((1, tile, ff2), in_tile),
                pl.BlockSpec((1, tile, feat), own_tile),
                pl.BlockSpec((1, tile, 128), in_tile),
                pl.BlockSpec((1, feat, ff2), lambda i, offs, ids: (1, 0, 0)),
                pl.BlockSpec((1, ff, feat), lambda i, offs, ids: (1, 0, 0)),
                pl.BlockSpec(memory_space=pl.ANY),
                pl.BlockSpec(memory_space=pl.ANY),
            ],
            out_specs=[
                pl.BlockSpec((group * tok, feat), far),
                pl.BlockSpec((group * tok, feat), near),
                pl.BlockSpec((sources, 8, tok), lambda i, offs, ids: (0, 0, 0)),
                *[pl.BlockSpec(memory_space=pl.ANY)] * len(sum(piece_shapes(feat, ff, False), [])),
            ],
            scratch_shapes=[
                pltpu.VMEM((most, feat), BF16),
                pltpu.VMEM((most, 128), F32),
                pltpu.VMEM((feat, ff2), F32),
                pltpu.VMEM((ff, feat), F32),
                pltpu.VMEM((most, feat), BF16),
                pltpu.VMEM((most, 128), F32),
                pltpu.VMEM((ff, feat), BF16),
                pltpu.VMEM((feat, ff2), BF16),
                pltpu.SemaphoreType.DMA((2 + len(sum(piece_shapes(feat, ff, False), [])),)),
            ],
        ),
        out_shape=[
            jax.ShapeDtypeStruct((sources // 2 * tok, feat), BF16),
            jax.ShapeDtypeStruct((sources // 2 * tok, feat), BF16),
            jax.ShapeDtypeStruct((sources, 8, tok), F32),
            *[jax.ShapeDtypeStruct(s, BF16) for s in sum(piece_shapes(feat, ff, False), [])],
        ],
        compiler_params=pltpu.CompilerParams(vmem_limit_bytes=56 * 1024 * 1024),
        cost_estimate=pl.CostEstimate(
            flops=2 * most * feat * ff * 4, bytes_accessed=10 * most * feat, transcendentals=0
        ),
        name="moe_back_last",
    )(offs, ids, slot, rows, ab, grads, gate, w_in, w_down, pair0, gg0)


def split_router(router):
    one = router.astype(BF16)
    rest = router - one.astype(F32)
    two = rest.astype(BF16)
    three = (rest - two.astype(F32)).astype(BF16)
    return jnp.concatenate([one, two, three, jnp.zeros_like(one)], axis=1)


def add_body(starts, *refs):
    step = pl.program_id(0)
    pieces = len(starts) - 1
    own, far, out_ref = refs[:pieces], refs[pieces : 2 * pieces], refs[-1]
    for p in range(pieces):

        @pl.when((step >= starts[p]) & (step < starts[p + 1]))
        def _(p=p):
            out_ref[0] = own[p][...].astype(F32) + far[p][...].astype(F32)


def add_pairs(own, far, index, local, held=None):
    block = math.gcd(*[piece.shape[0] for piece in own])
    width = own[0].shape[1]
    starts = [0]
    for piece in own:
        starts.append(starts[-1] + piece.shape[0] // block)

    def piece(p):
        return lambda i: (jnp.clip(i - starts[p], 0, starts[p + 1] - starts[p] - 1), 0)

    return pl.pallas_call(
        functools.partial(add_body, starts),
        grid=(starts[-1],),
        in_specs=[pl.BlockSpec((block, width), piece(p)) for p in range(len(own))] * 2
        + ([] if held is None else [pl.BlockSpec(memory_space=pl.ANY)]),
        out_specs=pl.BlockSpec((1, block, width), lambda i: (index, i, 0)),
        out_shape=jax.ShapeDtypeStruct((local, starts[-1] * block, width), F32),
        input_output_aliases={} if held is None else {2 * len(own): 0},
        compiler_params=pltpu.CompilerParams(vmem_limit_bytes=40 * 1024 * 1024),
        cost_estimate=beside_transfers(),
        name="add_pairs",
    )(*own, *far, *([] if held is None else [held]))


def mid_back_body(
    gn_ref, term_ref, mid_ref, dy_ref, gain_ref, out_ref,
    grad_ref, low_ref, gain_grad_ref, block_ref,
):
    @pl.when(pl.program_id(0) == 0)
    def _():
        mid = mid_ref[...]
        scale = lax.rsqrt(jnp.mean(mid * mid, axis=1, keepdims=True) + EPSILON)
        grad = gn_ref[...] + term_ref[...]
        gain_grad_ref[...] = jnp.sum(grad * mid * scale, axis=0, keepdims=True)
        weighted = grad * gain_ref[...]
        inner = jnp.mean(weighted * mid, axis=1, keepdims=True)
        total = dy_ref[...].astype(F32) + scale * weighted - mid * (scale * scale * scale * inner)
        grad_ref[...] = total
        low_ref[...] = total.astype(BF16)

    block_ref[0] = dot_nn(low_ref[...], out_ref[0]).astype(BF16)


def mid_back(gn, router_term, middle, out_grad, gain, out_all):
    tok, feat = middle.shape
    groups, _, width = out_all.shape
    args = (gn, router_term, middle, out_grad, gain[None])
    outs = [
        jax.ShapeDtypeStruct((tok, feat), F32),
        jax.ShapeDtypeStruct((tok, feat), BF16),
        jax.ShapeDtypeStruct((1, feat), F32),
        jax.ShapeDtypeStruct((groups, tok, width), BF16),
    ]
    return pl.pallas_call(
        mid_back_body,
        grid=(groups,),
        in_specs=[whole_block(v) for v in args]
        + [pl.BlockSpec((1, feat, width), lambda i: (i, 0, 0))],
        out_specs=[whole_block(v) for v in outs[:-1]]
        + [pl.BlockSpec((1, tok, width), lambda i: (i, 0, 0))],
        out_shape=outs,
        compiler_params=pltpu.CompilerParams(vmem_limit_bytes=60 * 1024 * 1024),
        cost_estimate=pl.CostEstimate(
            flops=2 * tok * feat * feat, bytes_accessed=4 * feat * feat, transcendentals=0
        ),
        name="mid_back",
    )(*args, out_all)


def beside_transfers():
    return pl.CostEstimate(flops=12_000_000_000, bytes_accessed=1 << 20, transcendentals=0)


def near_terms_body(near_a, far_a, near_b, far_b, out_a, out_b):
    out_a[...] = (near_a[...].astype(F32) + far_a[...].astype(F32)).astype(BF16)
    out_b[...] = (near_b[...].astype(F32) + far_b[...].astype(F32)).astype(BF16)


def near_terms(near, far, first, second, tok):
    feat = near.shape[1]

    def block(index):
        return pl.BlockSpec((tok, feat), lambda i: (index, 0), pipeline_mode=pl.Buffered(1))

    return pl.pallas_call(
        near_terms_body,
        grid=(1,),
        in_specs=[block(first), block(first), block(second), block(second)],
        out_specs=[block(0), block(0)],
        out_shape=[jax.ShapeDtypeStruct((tok, feat), BF16)] * 2,
        compiler_params=pltpu.CompilerParams(vmem_limit_bytes=60 * 1024 * 1024),
        cost_estimate=beside_transfers(),
        name="near_terms",
    )(near, far, near, far)


def put_rows(part, first, core, kept_ref, given_ref):
    chunk = kept_ref.shape[1]
    for n in range(part.shape[0] // chunk):
        rows = part[n * chunk : (n + 1) * chunk]
        b = first + n

        @pl.when(core == b % 2)
        def _(rows=rows, b=b):
            kept_ref[b // 2] = rows

        @pl.when(core != b % 2)
        def _(rows=rows, b=b):
            given_ref[b // 2] = rows


def w_out_body(core_ref, low_ref, heads_ref, kept_ref, given_ref):
    step = low_ref.shape[1] // 4
    for c in range(4):
        part = dot_tn(low_ref[:, c * step : (c + 1) * step], heads_ref[...]).astype(BF16)
        put_rows(part, c * step // kept_ref.shape[1], core_ref[0], kept_ref, given_ref)


def w_out_part(core, low, heads, chunk):
    feat, width = low.shape[1], heads.shape[1]
    out = jax.ShapeDtypeStruct((feat // chunk // 2, chunk, width), BF16)
    return pl.pallas_call(
        w_out_body,
        grid=(1,),
        in_specs=[pl.BlockSpec(memory_space=pltpu.SMEM), whole_block(low), whole_block(heads)],
        out_specs=[whole_block(out)] * 2,
        out_shape=[out] * 2,
        compiler_params=pltpu.CompilerParams(vmem_limit_bytes=60 * 1024 * 1024),
        cost_estimate=beside_transfers(),
        name="w_out_part",
    )(core, low, heads)


def w_qkv_body(core_ref, rows_ref, mixed_ref, w_ref, gain_ref, kept_ref, given_ref, sum_ref):
    feat = rows_ref.shape[1]
    width = mixed_ref.shape[1]
    step = feat // 4
    ones = jnp.ones((8, width), F32)
    for c in range(4):
        at = slice(c * step, (c + 1) * step)
        part = dot_tn(rows_ref[:, at], mixed_ref[...])
        put_rows(
            part.astype(BF16), c * step // kept_ref.shape[1], core_ref[0], kept_ref, given_ref
        )
        sums = lax.dot_general(
            ones,
            part * w_ref[at, :].astype(F32),
            (((1,), (1,)), ((), ())),
            precision=HIGHEST,
            preferred_element_type=F32,
        )
        sum_ref[:, at] = sums[0:1] / gain_ref[:, at]


def w_qkv_part(core, rows, mixed, w_own, gain, chunk):
    feat, width = rows.shape[1], mixed.shape[1]
    out = jax.ShapeDtypeStruct((feat // chunk // 2, chunk, width), BF16)
    sums = jax.ShapeDtypeStruct((1, feat), F32)
    args = (rows, mixed, w_own, gain[None])
    return pl.pallas_call(
        w_qkv_body,
        grid=(1,),
        in_specs=[pl.BlockSpec(memory_space=pltpu.SMEM)] + [whole_block(v) for v in args],
        out_specs=[whole_block(out), whole_block(out), whole_block(sums)],
        out_shape=[out, out, sums],
        compiler_params=pltpu.CompilerParams(vmem_limit_bytes=60 * 1024 * 1024),
        cost_estimate=beside_transfers(),
        name="w_qkv_part",
    )(core, *args)


def row_places(first, local, rt_all, rt_ids):
    sources = rt_all.shape[0]
    mine = first[0] + jnp.arange(local, dtype=jnp.int32)
    named = rt_all[:, None, :, :] == mine[None, :, None, None]
    counts = jnp.sum(named.astype(jnp.int32), axis=(2, 3))
    order = rt_ids[:, None] == jnp.arange(sources, dtype=jnp.int32)[None, :]
    counts = jnp.sum(jnp.where(order[:, :, None], counts[None], 0), axis=1)
    rounded = (counts + 15) // 16 * 16
    before = (
        jnp.arange(sources, dtype=jnp.int32)[None, :]
        < jnp.arange(sources + 1, dtype=jnp.int32)[:, None]
    )
    return jnp.sum(jnp.where(before[:, :, None], rounded[None], 0), axis=1).T


def rope_rows(positions):
    freq_index = jnp.arange(HD // 2, dtype=F32)
    inverse = jnp.exp(freq_index * (-2.0 * math.log(10000.0) / HD))
    angles = positions.astype(F32)[:, None] * jnp.tile(inverse, 4)[None, :]
    return jnp.cos(angles), jnp.sin(angles)


def seq_layout(block_lengths, block_tok):
    seq_ends = jnp.cumsum(block_lengths)
    starts = seq_ends - block_lengths
    places = jnp.arange(block_tok, dtype=jnp.int32)
    segment = jnp.sum((places[:, None] >= seq_ends[None, :]).astype(jnp.int32), axis=1)
    owners = segment[:, None] == jnp.arange(block_lengths.shape[0], dtype=jnp.int32)[None, :]
    offset = jnp.sum(jnp.where(owners, starts[None, :], 0), axis=1)
    return places - offset, offset


def norm_apply(row_vals, gain_vec):
    scale_row = lax.rsqrt(jnp.mean(row_vals * row_vals, axis=1, keepdims=True) + EPSILON)
    return row_vals * scale_row * gain_vec


def norm_back(row_vals, gain_vec, grad):
    scale_row = lax.rsqrt(jnp.mean(row_vals * row_vals, axis=1, keepdims=True) + EPSILON)
    weighted = grad * gain_vec
    inner = jnp.mean(weighted * row_vals, axis=1, keepdims=True)
    return scale_row * weighted - row_vals * (scale_row * scale_row * scale_row * inner)


def shift(values, axis, by):
    size = lax.axis_size(axis)
    return lax.ppermute(values, axis, [(i, (i + by) % size) for i in range(size)])


def swap(values, axis, bit):
    size = lax.axis_size(axis)
    return lax.ppermute(values, axis, [(i, i ^ bit) for i in range(size)])


def plane_places(row, col):
    rows, cols = lax.axis_size("row"), lax.axis_size("col")
    index = jnp.arange(rows * cols, dtype=jnp.int32)
    core, side, back = index // (2 * cols), index // cols % 2, index % cols
    return row ^ (core + 2 * side), (col - back + cols) % cols


def gather_small_steps(row, col):
    rows = lax.axis_size("row")
    def over(values, axis, bits):
        for bit in bits:
            values = jnp.concatenate([values, swap(values, axis, bit)], axis=0)
        return values

    steps = [
        functools.partial(over, axis=axis, bits=bits)
        for axis, bits in (("row", (1, 2)), ("col", (1,)), ("col", (2,)))
    ]
    from_row, from_col = plane_places(row, col)
    return steps, (from_row ^ row) + rows * (from_col ^ col)


def in_step(stages, *chains):
    values = [value for value, _ in chains]
    for stage in range(stages):
        for index, (_, steps) in enumerate(chains):
            mine = steps[stage : stage + 1] if stage + 1 < stages else steps[stage:]
            for step in mine:
                values[index] = step(values[index])
        values = list(lax.optimization_barrier(tuple(values)))
    return values


def ring_steps(by):
    return [lambda held: held + [shift(held[-1], "col", by)]] * (lax.axis_size("col") - 1)


def gather_plane(values):
    cols = lax.axis_size("col")
    line, across = [values], []
    for k in range(cols):
        side = swap(line[k], "row", 2)
        later = shift(line[k], "col", 1) if k + 1 < cols else None
        side, later = lax.optimization_barrier((side, later))
        line.append(later)
        across.append(side)
    own = line[:cols] + across
    return own + [swap(part, "row", 1) for part in own]


def after(values, *earlier):
    return lax.optimization_barrier((values, *earlier))[0]


def sum_rows_steps(row):
    dps = lax.axis_size("dp")
    dp = lax.axis_index("dp").astype(jnp.int32)
    places = [("row", 1, row % 2, 2), ("row", 2, row // 2, 1)]
    bit = dps // 2
    while bit:
        places.append(("dp", bit, dp // bit % 2, 0))
        bit //= 2

    def cut(values, place, dim):
        half = values.shape[dim] // 2
        return [
            lax.dynamic_slice_in_dim(values, at * half, half, dim) for at in (place, 1 - place)
        ]

    def add(halves, axis, bit):
        kept, given = halves
        return (kept.astype(F32) + swap(given, axis, bit).astype(F32)).astype(BF16)

    return [
        (functools.partial(cut, place=p, dim=d), functools.partial(add, axis=a, bit=b))
        for a, b, p, d in places
    ]


def row_halves(row):
    def halve(values, bit, place, dim):
        kept, given = [
            lax.dynamic_slice_in_dim(values, at, 1, dim) for at in (place, 1 - place)
        ]
        return kept + swap(given, "row", bit)

    def spread(values, bit, place, dim):
        other = swap(values, "row", bit)
        return jnp.where(
            place == 0,
            jnp.concatenate([values, other], axis=dim),
            jnp.concatenate([other, values], axis=dim),
        )

    places = [(1, row % 2, 2), (2, row // 2, 1)]
    return (
        [functools.partial(halve, bit=b, place=p, dim=d) for b, p, d in places],
        [functools.partial(spread, bit=b, place=p, dim=d) for b, p, d in places[::-1]],
    )


def sum_steps():
    steps = []
    for axis in ("row", "col", "dp"):
        bit = 1
        while bit < lax.axis_size(axis):
            steps.append(lambda v, axis=axis, bit=bit: v + swap(v, axis, bit))
            bit *= 2
    return steps


def shards(
    hidden_in,
    norm_gain_attn,
    norm_gain_moe,
    w_qkv,
    w_out,
    router,
    w_in,
    w_down,
    lengths,
    routes,
    out_grad,
):
    tok, feat = hidden_in.shape
    cols = lax.axis_size("col")
    rows = lax.axis_size("row")
    block_tok = tok * cols
    experts = router.shape[1]
    sources = rows * cols
    local = w_in.shape[0]
    cap = tok * TOP * 2 // experts
    head_cols = w_out.shape[1]
    group = 4
    plane = ("row", "col")
    col = lax.axis_index("col").astype(jnp.int32)
    row = lax.axis_index("row").astype(jnp.int32)
    here = col.reshape(1)
    first = ((row * cols + col) * local).reshape(1)
    rows_in = hidden_in.astype(F32)
    grad_out = out_grad.astype(F32)

    normed_attn = norm_apply(rows_in, norm_gain_attn).astype(BF16)
    qkv_own = lax.all_gather(w_qkv, ("dp", "row"), axis=0, tiled=True)
    out_all = lax.all_gather(w_out, ("col", "dp", "row"), axis=0, tiled=True).reshape(
        cols, feat, head_cols
    )
    positions, seq_start = seq_layout(lengths[0], block_tok)
    cos, sin = rope_rows(positions)
    starts = jnp.pad(seq_start.reshape(cols, tok), ((0, -cols % 8), (0, 0)))
    small_steps, rt_ids = gather_small_steps(row, col)
    tables = (cos, sin, starts, split_router(router))
    parts, rt_all, tables = in_step(
        cols - 1, ([normed_attn], ring_steps(1)), (routes.T[None], small_steps), (tables, [])
    )
    cos, sin, starts, router_parts = tables

    q_rows, key_rows, value_rows, lse, heads_block = attn_forward(
        here, parts, qkv_own, cos, sin, starts
    )
    heads = lax.all_to_all(
        heads_block.reshape(cols, tok, head_cols), "col", split_axis=0, concat_axis=0, tiled=True
    )
    middle = rows_in + jnp.einsum(
        "ctj,cdj->td", heads, out_all, preferred_element_type=F32
    )
    normed_moe = norm_apply(middle, norm_gain_moe).astype(BF16)
    heads = jnp.concatenate([after(heads, normed_moe)[k] for k in range(cols)], axis=1)

    offs = row_places(first, local, rt_all, rt_ids)
    x_parts = gather_plane(normed_moe)
    block_rows = jnp.concatenate(after(parts, normed_moe), axis=0)
    x_parts[-1], heads, block_rows = lax.optimization_barrier((x_parts[-1], heads, block_rows))
    dy_all = lax.all_gather(after(out_grad, x_parts[2]), plane, axis=0, tiled=True)
    from_row, from_col = plane_places(row, col)
    whole_ids = from_row * cols + from_col
    index = jnp.arange(sources, dtype=jnp.int32)
    twist_row, back_col = index // cols ^ row, (col - index % cols + cols) % cols
    places = (twist_row % 2 * 2 + twist_row // 2) * cols + back_col
    ids = jnp.stack([rt_ids, places, whole_ids, whole_ids])

    res_part, rows_kept, ab_kept, gate, slot = moe_front(
        first, ids, offs, x_parts, rt_all, router_parts, w_in, w_down, cap, group
    )
    res = lax.psum_scatter(res_part, plane, scatter_dimension=0, tiled=True)
    pair0, gg0, dy_kept, *own0 = moe_back_first(
        offs, ids, dy_all, slot, rows_kept, ab_kept, gate, w_in, w_down, cap, group
    )
    paired = lax.axis_size("dp") == 2
    own = {0: list(own0)}
    far = {0: [None] * len(own0), 1: []}

    def exchange(e, p, *earlier):
        if not paired:
            return []
        far[e][p] = swap(after(own[e][p], *earlier), "dp", 1)
        return [(e, p)]

    def arrived(values, sent):
        if sent:
            values, kept = lax.optimization_barrier((values, [far[e][p] for e, p in sent]))
            for (e, p), piece in zip(sent, kept):
                far[e][p] = piece
        return values

    sent = exchange(0, 0, pair0)
    gn_far, gn_near, dg, *own1 = moe_back_last(
        offs, ids, slot, rows_kept, ab_kept, dy_kept, gate, w_in, w_down, pair0, gg0, cap,
        group,
    )
    own[1], far[1] = list(own1), [None] * len(own1)
    gn_far = arrived(gn_far, sent)

    from_far = swap(gn_far, "row", 1)
    sent = exchange(0, 1, gn_far)
    dg_back = lax.all_to_all(dg, plane, split_axis=0, concat_axis=0, tiled=True)
    from_far, dg_back = arrived(lax.optimization_barrier((from_far, dg_back)), sent)

    sum_out, sum_all = sum_rows_steps(row), sum_steps()
    halve, spread = row_halves(row)
    gn, terms = None, near_terms(gn_near, from_far, 2 * cols - 1, cols - 1, tok)
    for k in range(cols - 1, -1, -1):
        side = swap(terms[0], "row", 2)
        sent = exchange(*((0, 2), (0, 3), (1, 2), (1, 3))[cols - 1 - k], terms[0])
        total = terms[1].astype(F32)
        if gn is not None:
            total = total + shift(gn, "col", -1).astype(F32)
        if k:
            terms = near_terms(gn_near, after(from_far, terms[0]), cols + k - 1, k - 1, tok)
        if k == cols - 1:
            normed_wide = normed_moe.astype(F32)
            logits = jnp.dot(
                normed_wide, router, precision=HIGHEST, preferred_element_type=F32
            )
            expert_ids = jnp.arange(experts, dtype=jnp.int32)
            used = jnp.any(routes[:, :, None] == expert_ids[None, None, :], axis=1)
            top = jnp.max(jnp.where(used, logits, MASKED_SCORE), axis=1, keepdims=True)
            exps = jnp.where(used, jnp.exp(logits - top), 0.0)
            gates = exps / jnp.sum(exps, axis=1, keepdims=True)
            side, gates = lax.optimization_barrier((side, gates))
        if k == cols - 2:
            grad_gates = after(dg_back, gates)[:, :local].reshape(experts, tok).T
            grad_logits = gates * (
                grad_gates - jnp.sum(gates * grad_gates, axis=1, keepdims=True)
            )
            router_term = lax.dot_general(
                grad_logits,
                router,
                (((1,), (1,)), ((), ())),
                precision=HIGHEST,
                preferred_element_type=F32,
            )
            grad_router = lax.dot_general(
                grad_logits,
                normed_wide,
                (((0,), (0,)), ((), ())),
                precision=HIGHEST,
                preferred_element_type=F32,
            )
            small = halve[0](grad_router.reshape(1, 2, 2, experts // 4, feat))
            side, router_term, small = lax.optimization_barrier((side, router_term, small))
        if k == 1:
            side, res = lax.optimization_barrier((side, res))
        total, side, terms = arrived(lax.optimization_barrier((total, side, terms)), sent)
        gn = total + side.astype(F32)
        if k:
            gn = gn.astype(BF16)

    grad_middle, grad_attn, gain_moe_part, grad_heads = mid_back(
        gn, router_term, middle, out_grad, norm_gain_moe, out_all
    )
    sent = exchange(1, 4, gn)
    grads_block = lax.all_to_all(
        grad_heads, "col", split_axis=0, concat_axis=0, tiled=True
    )
    small = halve[1](after(small, grad_heads))
    core = (row % 2).reshape(1)
    w_out_sum = w_out_part(core, after(grad_attn, grad_heads), heads, w_out.shape[0])
    w_out_sum = [v.reshape(-1, 2, 1, w_out.shape[0], feat) for v in w_out_sum]
    w_out_sum = sum_out[1][0](sum_out[0][1](w_out_sum))
    grads_block, small, w_out_sum = arrived(
        lax.optimization_barrier((grads_block, small, w_out_sum)), sent
    )

    sent = exchange(1, 0, grads_block)
    small = sum_all[2](small)
    grad_mixed = attn_backward(
        here, grads_block.reshape(cols * tok, head_cols), q_rows, key_rows, value_rows, lse,
        cos, sin, starts, cols,
    )
    w_out_sum = sum_out[1][1](w_out_sum)
    grad_mixed, small = arrived(lax.optimization_barrier((grad_mixed, small)), sent)

    def na_part(k, *earlier):
        mixed = after(grad_mixed[k * tok : (k + 1) * tok], *earlier)
        return dot_nt(mixed, qkv_own)

    def held(*values):
        return arrived(lax.optimization_barrier(values), sent)

    sent = exchange(1, 1, grad_mixed)
    first_na = na_part(cols - 1).astype(BF16)
    grad_na = shift(first_na, "col", -1)
    small = sum_all[3](small)
    *w_qkv_sum, gain_attn_part = w_qkv_part(
        core, after(block_rows, first_na), grad_mixed, qkv_own, norm_gain_attn, w_qkv.shape[0]
    )
    w_qkv_sum = [v.reshape(-1, 2, 1, *w_qkv.shape) for v in w_qkv_sum]
    w_qkv_sum = sum_out[0][1](w_qkv_sum)
    gains = sum_all[0](jnp.concatenate([gain_moe_part, gain_attn_part], axis=0))
    next_na = na_part(cols - 2, first_na)
    grad_na, small, w_out_sum, w_qkv_sum, gains, next_na = held(
        grad_na, small, w_out_sum, w_qkv_sum, gains, next_na
    )

    grad_na = (grad_na.astype(F32) + next_na).astype(BF16)
    sent = []
    next_na = na_part(cols - 3, grad_na)
    grad_w_in = grad_w_down = next_na
    if paired:
        downs = len(piece_shapes(feat, FFE, True)[0])
        grad_w_in = add_pairs(own[0][downs:], after(far[0][downs:], next_na), 0, local)
        grad_w_down = add_pairs(own[0][:downs], after(far[0][:downs], next_na), 0, local)
    grad_na = shift(grad_na, "col", -1)
    gains = sum_all[1](gains)
    w_qkv_sum = sum_out[1][0](w_qkv_sum)
    for step in sum_out[2:]:
        w_out_sum = step[1](step[0](w_out_sum))
    for step in sum_all[4:]:
        small = step(small)
    gains = sum_all[2](gains)
    grad_na, next_na, gains, small, w_qkv_sum, grad_w_in, grad_w_down, w_out_sum = held(
        grad_na, next_na, gains, small, w_qkv_sum, grad_w_in, grad_w_down, w_out_sum
    )

    grad_na = (grad_na.astype(F32) + next_na).astype(BF16)
    next_na = na_part(cols - 4, grad_na)
    lines = lax.all_to_all(
        jnp.stack([w_out_sum[..., k * head_cols : (k + 1) * head_cols] for k in range(cols)]),
        "col",
        split_axis=0,
        concat_axis=0,
        tiled=True,
    )
    result = middle + after(res, next_na).astype(F32)
    grad_na = shift(grad_na, "col", -1)
    gains = sum_all[3](gains)
    small = spread[0](small)
    w_qkv_sum = sum_out[1][1](w_qkv_sum)
    if paired:
        downs = len(piece_shapes(feat, FFE, False)[0])
        grad_w_in = add_pairs(own[1][downs:], after(far[1][downs:], next_na), 1, local, grad_w_in)
        grad_w_down = add_pairs(own[1][:downs], far[1][:downs], 1, local, grad_w_down)
    else:
        ins, outs = [], []
        for e in range(local):
            downs = len(piece_shapes(feat, FFE, e == 0)[0])
            outs.append(jnp.concatenate(own[e][:downs]))
            ins.append(jnp.concatenate(own[e][downs:]))
        grad_w_in = lax.psum(jnp.stack(ins), "dp").astype(F32)
        grad_w_down = lax.psum(jnp.stack(outs), "dp").astype(F32)
    grad_na, next_na, gains, small, w_qkv_sum, lines, grad_w_in, grad_w_down, result = held(
        grad_na, next_na, gains, small, w_qkv_sum, lines, grad_w_in, grad_w_down, result
    )

    grad_na = grad_na.astype(F32) + next_na
    for step in sum_all[4:]:
        gains = step(gains)
    small = spread[1](small).reshape(experts, feat)
    for step in sum_out[2:]:
        w_qkv_sum = step[1](step[0](w_qkv_sum))
    grad_hidden = grad_middle + norm_back(rows_in, norm_gain_attn, grad_na)
    grad_w_qkv = w_qkv_sum.reshape(w_qkv.shape).astype(F32)
    grad_w_out = jnp.sum(lines.astype(F32), axis=0).reshape(w_out.shape)
    return (
        result,
        grad_hidden,
        gains[1],
        gains[0],
        grad_w_qkv,
        grad_w_out,
        small.T,
        grad_w_in,
        grad_w_down,
    )


def solution(mesh):
    in_specs = (
        P(("dp", "row", "col"), None),
        P(),
        P(),
        P(("dp", "row"), "col"),
        P(("dp", "row"), "col"),
        P(),
        P(("row", "col"), None, None),
        P(("row", "col"), None, None),
        P(("dp", "row"), None),
        P(("dp", "row", "col"), None),
        P(("dp", "row", "col"), None),
    )
    out_specs = (
        P(("dp", "row", "col"), None),
        P(("dp", "row", "col"), None),
        P(),
        P(),
        P(("dp", "row"), "col"),
        P(("dp", "row"), "col"),
        P(),
        P(("row", "col"), None, None),
        P(("row", "col"), None, None),
    )
    return jax.shard_map(shards, mesh=mesh, in_specs=in_specs, out_specs=out_specs, check_vma=False)
```

time: 908 us -> 683 us (0.75)
  waiting for transfers between devices: 565 us -> 279 us
  Pallas kernels: 114 us -> 199 us
  matrix products: 30.1 us -> 15.7 us
    reduce_scatter x2 -> x0, waiting for transfers between devices: 142 us -> none  [the longest x1 103 us: shards(): gn = lax.psum_scatter(gn_part, plane, scatter_dimension=0, tiled=True)]
    all_gather x4 -> x2, waiting for transfers between devices: 124 us -> 12.5 us  [the longest x1 11.1 us: shards(): lax.all_gather(after(out_grad, x_parts[2]), plane, axis=0, tiled=True)]
    pallas_call x3 -> x16, Pallas kernels: 114 us -> 199 us  [the longest x1 45.8 us: moe_front(): pl.pallas_call(functools.partial(front_body, cap, tile, tiles, group, sou...]
    ppermute x21 -> x12, waiting for transfers between devices: 200 us -> 116 us  [shift(): lax.ppermute(values, axis, [(i, (i + by) % size) for i in range(size)])]
    ppermute x12 -> x48, waiting for transfers between devices: 60.6 us -> 116 us  [swap(): return lax.ppermute(values, axis, [(i, i ^ bit) for i in range(size)])]
    ppermute x21 -> x12, starting transfers between devices: 50.3 us -> 13.1 us  [shift(): lax.ppermute(values, axis, [(i, (i + by) % size) for i in range(size)])]
    all_gather x1 -> x0, blocking collectives: 34 us -> none  [shards(): rt_all = lax.all_gather(routes.T, plane, axis=0)]
    all_to_all x0 -> x1, blocking collectives: none -> 32.9 us  [shards(): lax.all_to_all(heads_block.reshape(cols, tok, head_cols), 'col', split_ax...]
  transfers between devices with their start and end apart: 43 -> 67, of which waited for: 22 -> 29; matrix products, arithmetic and copies ran while one was open for 9% -> 8% of each run, Pallas kernels for 3% -> 27%
where the time goes in v3:
time: 683 us; the launch traced here: 675 us
  waiting for transfers between devices  279 us (41%)
  Pallas kernels  199 us (29%)
  starting transfers between devices  75.7 us (11%)
  other arithmetic  43.5 us (6%)
  blocking collectives  32.9 us (5%)
  matrix products  15.7 us (2%)
  between operations  15 us (2%)
  local copies, waits for them, and re-layouts  14.5 us (2%)
    ppermute x48, waiting for transfers between devices, swap(): return lax.ppermute(values, axis, [(i, i ^ bit) for i in range(size)])  116 us
    ppermute x12, waiting for transfers between devices, shift(): lax.ppermute(values, axis, [(i, (i + by) % size) for i in range(size)])  116 us
    pallas_call x1, Pallas kernels, moe_front(): pl.pallas_call(functools.partial(front_body, cap, tile, tiles, group, sou...  45.8 us
    ppermute x48, starting transfers between devices, swap(): return lax.ppermute(values, axis, [(i, i ^ bit) for i in range(size)])  44.6 us
    pallas_call x1, Pallas kernels, moe_back_first(): pl.pallas_call(functools.partial(back_first_body, cap, tile, tiles, group...  34 us
    all_to_all x1, blocking collectives, shards(): lax.all_to_all(heads_block.reshape(cols, tok, head_cols), 'col', split_ax...  32.9 us
    pallas_call x1, Pallas kernels, moe_back_last(): pl.pallas_call(functools.partial(back_last_body, cap, tile, tiles, group)...  31.5 us
    pallas_call x4, Pallas kernels, add_pairs(): pl.pallas_call(functools.partial(add_body, starts), grid=(starts[-1],), i...  18.8 us
  transfers between devices with their start and end apart: 67, of which 29 were waited for; matrix products, arithmetic and copies ran while one was open for 8% of the time, Pallas kernels for 27%

profile of v3, /device:TPU:0, one launch (start us, length us, event | category | flops | bytes accessed | tf_op | source)
XLA Modules:
  0.0 675.2 jit_solution(17241100103919630653)
XLA Ops:
  21.9 12.7 %collective-permute-done.refs_1_ = bf16[256,1536]{1,0:T(8,128)(2,1)} collective-permute-done((bf16[256,1536]{1,0:T(8,128)(2,1)S(1)}, bf16[256,1536]{1,0:T(8,128)(2,1)}, u32[]{:S(2)}, u32[]{:S(2)}) %collective-permute-start) | collective-permute-done | bytes 786464 | tf_op jit(solution)/shard_map/ppermute | solution.py:1010
  35.9 17.8 %collective-permute-done.4 = s32[4,8,256]{2,1,0:T(8,128)S(1)} collective-permute-done((s32[4,8,256]{2,1,0:T(8,128)S(1)}, s32[4,8,256]{2,1,0:T(8,128)S(1)}, u32[]{:S(2)}, u32[]{:S(2)}) %collective-permute-start.4) | collective-permute-done | bytes 32800 | tf_op jit(solution)/shard_map/ppermute | solution.py:1015
  58.6 21.9 %collective-permute-done.6 = s32[8,8,256]{2,1,0:T(8,128)S(1)} collective-permute-done((s32[8,8,256]{2,1,0:T(8,128)S(1)}, s32[8,8,256]{2,1,0:T(8,128)S(1)}, u32[]{:S(2)}, u32[]{:S(2)}) %collective-permute-start.6) | collective-permute-done | bytes 65568 | tf_op jit(solution)/shard_map/ppermute | solution.py:1015
  81.5 12.8 %attn_forward.1 = (bf16[1024,768]{1,0:T(8,128)(2,1)}, bf16[1024,256]{1,0:T(8,128)(2,1)}, bf16[1024,256]{1,0:T(8,128)(2,1)}, f32[6,8,256]{2,1,0:T(8,128)}, bf16[1024,384]{1,0:T(8,128)(2,1)}) custom-call(s32[1]{0:T(128)} %bitcast.here_ref, bf16[256,1536]{1,0:T(8,128)(2,1)} %copy-done.24, bf16[256,1536]{1,0:T(8,128)(2,1)} %collective-permute-done.refs_1_, ...), custom_call_target="tpu_custom_call" | custom-call | flops 8053063680 | bytes 5242880 | tf_op jit(solution)/shard_map/attn_forward/pallas_call | solution.py:139
  94.3 32.9 %all_to_all.20 = bf16[4,256,384]{2,1,0:T(8,128)(2,1)S(1)} all-to-all(bf16[4,256,384]{2,1,0:T(8,128)(2,1)} %bitcast.89), channel_id=1, replica_groups=mesh['dp'=2,'row'=4,'col'=4] {'col'}, dimensions={0} | all-to-all | bytes 1572864 | tf_op jit(solution)/shard_map/all_to_all | solution.py:1178
  135.1 20.2 %collective-permute-done.8.refs_1_ = bf16[256,1536]{1,0:T(8,128)(2,1)S(1)} collective-permute-done((bf16[256,1536]{1,0:T(8,128)(2,1)S(1)}, bf16[256,1536]{1,0:T(8,128)(2,1)S(1)}, u32[]{:S(2)}, u32[]{:S(2)}) %collective-permute-start.8) | collective-permute-done | bytes 786464 | tf_op jit(solution)/shard_map/ppermute | solution.py:1010
  156.6 19.4 %collective-permute-done.10.refs_2_ = bf16[256,1536]{1,0:T(8,128)(2,1)S(1)} collective-permute-done((bf16[256,1536]{1,0:T(8,128)(2,1)S(1)}, bf16[256,1536]{1,0:T(8,128)(2,1)S(1)}, u32[]{:S(2)}, u32[]{:S(2)}) %collective-permute-start.10) | collective-permute-done | bytes 786464 | tf_op jit(solution)/shard_map/ppermute | solution.py:1010
  177.9 25.9 %collective-permute-done.12.refs_3_ = bf16[256,1536]{1,0:T(8,128)(2,1)} collective-permute-done((bf16[256,1536]{1,0:T(8,128)(2,1)S(1)}, bf16[256,1536]{1,0:T(8,128)(2,1)}, u32[]{:S(2)}, u32[]{:S(2)}) %collective-permute-start.12) | collective-permute-done | bytes 786464 | tf_op jit(solution)/shard_map/ppermute | solution.py:1010
  207.5 12.5 %collective-permute-done.13.refs_7_ = bf16[256,1536]{1,0:T(8,128)(2,1)} collective-permute-done((bf16[256,1536]{1,0:T(8,128)(2,1)}, bf16[256,1536]{1,0:T(8,128)(2,1)}, u32[]{:S(2)}, u32[]{:S(2)}) %collective-permute-start.13) | collective-permute-done | bytes 786464 | tf_op jit(solution)/shard_map/ppermute | solution.py:1015
  230.0 45.8 %moe_front.1 = (bf16[4096,1536]{1,0:T(8,128)(2,1)}, bf16[2,2048,1536]{2,1,0:T(8,128)(2,1)}, f32[2,2048,1024]{2,1,0:T(8,128)}, f32[2,2048,128]{2,1,0:T(8,128)}, f32[2,16,256]{2,1,0:T(8,128)}) custom-call(s32[1]{0:T(128)} %bitcast.9.first_ref, s32[4,16]{1,0:T(4,128)} %pad_add_fusion.4.ids_ref, s32[2,17]{1,0:T(2,128)} %bitcast.96, ...), custom_call_target="tpu_custom_call" | custom-call | flops 9663676416 | bytes 31457280 | tf_op jit(solution)/shard_map/moe_front/pallas_call | solution.py:401
  275.9 11.1 %all-gather.8.cloned.1.call-done.refs_0_.refs_1_.refs_2_.refs_3_ = bf16[4096,1536]{1,0:T(8,128)(2,1)} async-done(((bf16[256,1536]{1,0:T(8,128)(2,1)}), bf16[4096,1536]{1,0:T(8,128)(2,1)}) %all-gather.8.cloned.1.call-update) | async-done | bytes 12582928 | tf_op jit(solution)/shard_map/all_gather | solution.py:1191
  287.0 34.0 %moe_back_first.1 = (bf16[2048,1536]{1,0:T(8,128)(2,1)}, f32[2048,128]{1,0:T(8,128)}, bf16[1,2048,1536]{2,1,0:T(8,128)(2,1)}, bf16[512,1536]{1,0:T(8,128)(2,1)},...) custom-call(s32[2,17]{1,0:T(2,128)} %bitcast.97, s32[4,16]{1,0:T(4,128)} %pad_add_fusion.4.ids_ref, ...), custom_call_target="tpu_custom_call" | custom-call | flops 12884901888 | bytes 62914560 | tf_op jit(solution)/shard_map/moe_back_first/pallas_call | solution.py:565
  324.8 31.5 %moe_back_last.1 = (bf16[2048,1536]{1,0:T(8,128)(2,1)}, bf16[2048,1536]{1,0:T(8,128)(2,1)}, f32[16,8,256]{2,1,0:T(8,128)}, bf16[256,1536]{1,0:T(8,128)(2,1)}, bf...) custom-call(s32[2,17]{1,0:T(2,128)} %bitcast.98, ...), custom_call_target="tpu_custom_call" | custom-call | flops 12884901888 | bytes 31457280 | tf_op jit(solution)/shard_map/moe_back_last/pallas_call | solution.py:726
  358.8 9.1 %all-to-all-start.1 = ((f32[16,8,256]{2,1,0:T(8,128)}), f32[16,8,256]{2,1,0:T(8,128)S(1)}, u32[]{:S(2)}, u32[]{:S(2)}) async-start(f32[16,8,256]{2,1,0:T(8,128)} %get-tuple-element.258), calls=%async_computation.1 | async-start | bytes 262144 | tf_op jit(solution)/shard_map/all_to_all | solution.py:1233
  368.0 12.1 %all-to-all-done.1 = f32[16,8,256]{2,1,0:T(8,128)S(1)} async-done(((f32[16,8,256]{2,1,0:T(8,128)}), f32[16,8,256]{2,1,0:T(8,128)S(1)}, u32[]{:S(2)}, u32[]{:S(2)}) %all-to-all-start.1) | async-done | bytes 131104 | tf_op jit(solution)/shard_map/all_to_all | solution.py:1233
  392.1 13.1 %collective-permute-done.25 = bf16[256,1536]{1,0:T(8,128)(2,1)} collective-permute-done((bf16[256,1536]{1,0:T(8,128)(2,1)}, bf16[256,1536]{1,0:T(8,128)(2,1)}, u32[]{:S(2)}, u32[]{:S(2)}) %collective-permute-start.25) | collective-permute-done | bytes 786464 | tf_op jit(solution)/shard_map/ppermute | solution.py:1015
  421.0 10.7 %collective-permute-done.28 = bf16[256,1536]{1,0:T(8,128)(2,1)} collective-permute-done((bf16[256,1536]{1,0:T(8,128)(2,1)}, bf16[256,1536]{1,0:T(8,128)(2,1)}, u32[]{:S(2)}, u32[]{:S(2)}) %collective-permute-start.28) | collective-permute-done | bytes 786464 | tf_op jit(solution)/shard_map/ppermute | solution.py:1015
  431.7 16.9 %collective-permute-done.27 = bf16[256,1536]{1,0:T(8,128)(2,1)} collective-permute-done((bf16[256,1536]{1,0:T(8,128)(2,1)}, bf16[256,1536]{1,0:T(8,128)(2,1)}, u32[]{:S(2)}, u32[]{:S(2)}) %collective-permute-start.27) | collective-permute-done | bytes 786464 | tf_op jit(solution)/shard_map/ppermute | solution.py:1010
  461.0 8.6 %collective-permute-done.32 = bf16[256,1536]{1,0:T(8,128)(2,1)} collective-permute-done((bf16[256,1536]{1,0:T(8,128)(2,1)}, bf16[256,1536]{1,0:T(8,128)(2,1)}, u32[]{:S(2)}, u32[]{:S(2)}) %collective-permute-start.32) | collective-permute-done | bytes 786464 | tf_op jit(solution)/shard_map/ppermute | solution.py:1015
  474.8 6.2 collective-permute-done.33.refs_3_
  486.1 14.2 %collective-permute-done.34 = bf16[256,1536]{1,0:T(8,128)(2,1)S(1)} collective-permute-done((bf16[256,1536]{1,0:T(8,128)(2,1)S(1)}, bf16[256,1536]{1,0:T(8,128)(2,1)S(1)}, u32[]{:S(2)}, u32[]{:S(2)}) %collective-permute-start.34) | collective-permute-done | bytes 786464 | tf_op jit(solution)/shard_map/ppermute | solution.py:1010
  501.6 4.4 collective-permute-done.36.refs_4_
  508.3 8.0 %mid_back.1 = (f32[256,1536]{1,0:T(8,128)}, bf16[256,1536]{1,0:T(8,128)(2,1)}, f32[1,1536]{1,0:T(1,128)}, bf16[4,256,384]{2,1,0:T(8,128)(2,1)}) custom-call(f32[256,1536]{1,0:T(8,128)} %convert_add_fusion.4.gn_ref, f32[256,1536]{1,0:T(8,128)} %fusion.18.term_ref, f32[256,1536]{1,0:T(8,128)} %copy-done.16, bf16[256,1536]{1,0:T(8,128)(2,1)} %dy_ref.1, ...), custom_call_target="tpu_custom_call" | custom-call | flops 1207959552 | bytes 9437184 | tf_op jit(solution)/shard_map/mid_back/pallas_call | solution.py:846
  516.3 6.0 w_out_part.1
  523.5 4.6 all-to-all-start.2
  534.4 14.2 %all-to-all-done.2 = bf16[4,256,384]{2,1,0:T(8,128)(2,1)} async-done(((bf16[4,256,384]{2,1,0:T(8,128)(2,1)}), bf16[4,256,384]{2,1,0:T(8,128)(2,1)}, u32[]{:S(2)}, u32[]{:S(2)}) %all-to-all-start.2) | async-done | bytes 786464 | tf_op jit(solution)/shard_map/all_to_all | solution.py:1290
  548.5 5.2 collective-permute-done.39.refs_5_
  558.4 17.5 %attn_backward.1.mixed_ref = bf16[1024,640]{1,0:T(8,128)(2,1)} custom-call(s32[1]{0:T(128)} %bitcast.here_ref, bf16[1024,384]{1,0:T(8,128)(2,1)} %bitcast.22.grads_ref, bf16[1024,768]{1,0:T(8,128)(2,1)} %get-tuple-element.334.q_ref, bf16[1024,256]{1,0:T(8,128)(2,1)} %get-tuple-element.335.kk_ref, bf16[1024,256]{1,0:T(8,128)(2,1)} %get-tuple-element.336.vv_ref, ...), custom_call_target="tpu_custom_call" | custom-call | flops 12000000000 | bytes 1048576 | tf_op jit(solution)/shard_map/attn_backward/pallas_call | solution.py:230
  582.5 11.8 %w_qkv_part.1 = (bf16[4,192,640]{2,1,0:T(8,128)(2,1)}, bf16[4,192,640]{2,1,0:T(8,128)(2,1)}, f32[1,1536]{1,0:T(1,128)}) custom-call(s32[1]{0:T(128)} %bitcast.19.core_ref, bf16[1024,1536]{1,0:T(8,128)(2,1)} %pad_maximum_fusion.rows_ref, bf16[1024,640]{1,0:T(8,128)(2,1)} %attn_backward.1.mixed_ref, ...), custom_call_target="tpu_custom_call" | custom-call | flops 12000000000 | bytes 1048576 | tf_op jit(solution)/shard_map/w_qkv_part/pallas_call | solution.py:952
  610.6 8.4 %add_pairs.4.refs_6_ = f32[2,1536,1024]{2,1,0:T(8,128)} custom-call(bf16[384,1024]{1,0:T(8,128)(2,1)S(1)} %copy-done.11, bf16[512,1024]{1,0:T(8,128)(2,1)S(1)} %copy-done.6, bf16[640,1024]{1,0:T(8,128)(2,1)S(1)} %copy-done.1, bf16[384,1024]{1,0:T(8,128)(2,1)S(1)} %copy-done.13, bf16[512,1024]{1,0:T(8,128)(2,1)} %collective-permute-done.26.refs_4_, ...), custom_call_target="tpu_custom_call" | custom-call | flops 12000000000 | bytes 1048576 | tf_op jit(solution)/shard_map/add_pairs/pallas_call | solution.py:803
  638.8 5.1 add_pairs.6
  650.1 6.7 all-to-all-done.3
  (345 shorter events, 178.9 us)
Async XLA Ops:
  7.2 73.3 %all-gather.4.cloned.1.call-start = ((), (), s32[]{:S(2)}) async-start(), calls=%async_computation.5 | async-start | bytes 2211840 | tf_op jit(solution)/shard_map/all_gather | solution.py:1161
  7.9 120.6 %all-gather.6.cloned.1.call-start = ((), (), s32[]{:S(2)}) async-start(), calls=%async_computation.6 | async-start | bytes 4866048 | tf_op jit(solution)/shard_map/all_gather | solution.py:1162
  8.7 278.3 %all-gather.8.cloned.1.call-start = ((), (), s32[]{:S(2)}) async-start(), calls=%async_computation.7 | async-start | bytes 13369344 | tf_op jit(solution)/shard_map/all_gather | solution.py:1191
  11.6 23.0 %collective-permute-start = (bf16[256,1536]{1,0:T(8,128)(2,1)S(1)}, bf16[256,1536]{1,0:T(8,128)(2,1)}, u32[]{:S(2)}, u32[]{:S(2)}) collective-permute-start(bf16[256,1536]{1,0:T(8,128)(2,1)S(1)} %fusion.4.refs_0_), channel_id=1, source_target_pairs={{0,1},{1,2},{2,3},{3,0},{4,5},{5,6},{6,7},{7,4},{8,9},{9,10},{10,1... | collective-permute-start | bytes 2359304 | tf_op jit(solution)/shard_map/ppermute | solution.py:1010
  34.6 21.9 %collective-permute-start.3 = (bf16[256,1536]{1,0:T(8,128)(2,1)}, bf16[256,1536]{1,0:T(8,128)(2,1)S(1)}, u32[]{:S(2)}, u32[]{:S(2)}) collective-permute-start(bf16[256,1536]{1,0:T(8,128)(2,1)} %collective-permute-done.refs_1_), channel_id=1, source_target_pairs={{0,1},{1,2},{2,3},{3,0},{4,5},{5,6},{6,7},{7,4},{8,9},{9,10},{10,1... | collective-permute-start | bytes 2359304 | tf_op jit(solution)/shard_map/ppermute | solution.py:1010
  56.5 24.0 %collective-permute-start.5 = (bf16[256,1536]{1,0:T(8,128)(2,1)S(1)}, bf16[256,1536]{1,0:T(8,128)(2,1)S(1)}, u32[]{:S(2)}, u32[]{:S(2)}) collective-permute-start(bf16[256,1536]{1,0:T(8,128)(2,1)S(1)} %collective-permute-done.3.refs_2_), channel_id=1, source_target_pairs={{0,1},{1,2},{2,3},{3,0},{4,5},{5,6},{6,7},{7,4},{8,9},{9,10},{10,1... | collective-permute-start | bytes 2359304 | tf_op jit(solution)/shard_map/ppermute | solution.py:1010
  56.7 23.8 %collective-permute-start.6 = (s32[8,8,256]{2,1,0:T(8,128)S(1)}, s32[8,8,256]{2,1,0:T(8,128)S(1)}, u32[]{:S(2)}, u32[]{:S(2)}) collective-permute-start(s32[8,8,256]{2,1,0:T(8,128)S(1)} %pad_add_fusion.1), channel_id=1, source_target_pairs={{0,2},{1,3},{2,0},{3,1},{4,6},{5,7},{6,4},{7,5},{8,10},{9,11},{10,... | collective-permute-start | bytes 196616 | tf_op jit(solution)/shard_map/ppermute | solution.py:1015
  133.8 21.6 %collective-permute-start.8 = (bf16[256,1536]{1,0:T(8,128)(2,1)S(1)}, bf16[256,1536]{1,0:T(8,128)(2,1)S(1)}, u32[]{:S(2)}, u32[]{:S(2)}) collective-permute-start(bf16[256,1536]{1,0:T(8,128)(2,1)S(1)} %multiply_convert_fusion.refs_0_), channel_id=1, source_target_pairs={{0,1},{1,2},{2,3},{3,0},{4,5},{5,6},{6,7},{7,4},{8,9},{9,10},{10,1... | collective-permute-start | bytes 2359304 | tf_op jit(solution)/shard_map/ppermute | solution.py:1010
  133.8 21.5 %collective-permute-start.7 = (bf16[256,1536]{1,0:T(8,128)(2,1)S(1)}, bf16[256,1536]{1,0:T(8,128)(2,1)}, u32[]{:S(2)}, u32[]{:S(2)}) collective-permute-start(bf16[256,1536]{1,0:T(8,128)(2,1)S(1)} %multiply_convert_fusion.refs_0_), channel_id=1, source_target_pairs={{0,8},{4,12},{8,0},{12,4},{1,9},{5,13},{9,1},{13,5},{2,10},{6,14},... | collective-permute-start | bytes 2359304 | tf_op jit(solution)/shard_map/ppermute | solution.py:1015
  176.1 285.0 %reduce-scatter.2.cloned.1.call-start = ((), (), s32[]{:S(2)}) async-start(), calls=%async_computation.8 | async-start | bytes 13369344 | tf_op jit(solution)/shard_map/reduce_scatter | solution.py:1202
  176.1 27.7 %collective-permute-start.12 = (bf16[256,1536]{1,0:T(8,128)(2,1)S(1)}, bf16[256,1536]{1,0:T(8,128)(2,1)}, u32[]{:S(2)}, u32[]{:S(2)}) collective-permute-start(bf16[256,1536]{1,0:T(8,128)(2,1)S(1)} %collective-permute-done.10.refs_2_), channel_id=1, source_target_pairs={{0,1},{1,2},{2,3},{3,0},{4,5},{5,6},{6,7},{7,4},{8,9},{9,10},{10,1... | collective-permute-start | bytes 2359304 | tf_op jit(solution)/shard_map/ppermute | solution.py:1010
  176.6 27.2 %collective-permute-start.11 = (bf16[256,1536]{1,0:T(8,128)(2,1)S(1)}, bf16[256,1536]{1,0:T(8,128)(2,1)S(1)}, u32[]{:S(2)}, u32[]{:S(2)}) collective-permute-start(bf16[256,1536]{1,0:T(8,128)(2,1)S(1)} %collective-permute-done.10.refs_2_), channel_id=1, source_target_pairs={{0,8},{4,12},{8,0},{12,4},{1,9},{5,13},{9,1},{13,5},{2,10},{6,14},... | collective-permute-start | bytes 2359304 | tf_op jit(solution)/shard_map/ppermute | solution.py:1015
  321.0 35.3 %collective-permute-start.22 = (bf16[512,1536]{1,0:T(8,128)(2,1)}, bf16[512,1536]{1,0:T(8,128)(2,1)S(1)}, u32[]{:S(2)}, u32[]{:S(2)}) collective-permute-start(bf16[512,1536]{1,0:T(8,128)(2,1)} %get-tuple-element.256.refs_0_), channel_id=1, source_target_pairs={{0,16},{16,0},{1,17},{17,1},{2,18},{18,2},{3,19},{19,3},{4,20},{20... | collective-permute-start | bytes 4718600 | tf_op jit(solution)/shard_map/ppermute | solution.py:1015
  356.3 23.8 %collective-permute-start.23 = (bf16[2048,1536]{1,0:T(8,128)(2,1)}, bf16[2048,1536]{1,0:T(8,128)(2,1)}, u32[]{:S(2)}, u32[]{:S(2)}) collective-permute-start(bf16[2048,1536]{1,0:T(8,128)(2,1)} %get-tuple-element.257), channel_id=1, source_target_pairs={{0,4},{4,0},{8,12},{12,8},{1,5},{5,1},{9,13},{13,9},{2,6},{6,2},{1... | collective-permute-start | bytes 18874376 | tf_op jit(solution)/shard_map/ppermute | solution.py:1015
  356.4 23.7 %collective-permute-start.24 = (bf16[384,1024]{1,0:T(8,128)(2,1)S(1)}, bf16[384,1024]{1,0:T(8,128)(2,1)S(1)}, u32[]{:S(2)}, u32[]{:S(2)}) collective-permute-start(bf16[384,1024]{1,0:T(8,128)(2,1)S(1)} %copy-done.10), channel_id=1, source_target_pairs={{0,16},{16,0},{1,17},{17,1},{2,18},{18,2},{3,19},{19,3},{4,20},{20... | collective-permute-start | bytes 2359304 | tf_op jit(solution)/shard_map/ppermute | solution.py:1015
  358.8 21.3 %all-to-all-start.1 = ((f32[16,8,256]{2,1,0:T(8,128)}), f32[16,8,256]{2,1,0:T(8,128)S(1)}, u32[]{:S(2)}, u32[]{:S(2)}) async-start(f32[16,8,256]{2,1,0:T(8,128)} %get-tuple-element.258), calls=%async_computation.1 | async-start | bytes 262144 | tf_op jit(solution)/shard_map/all_to_all | solution.py:1233
  384.5 20.7 %collective-permute-start.25 = (bf16[256,1536]{1,0:T(8,128)(2,1)}, bf16[256,1536]{1,0:T(8,128)(2,1)}, u32[]{:S(2)}, u32[]{:S(2)}) collective-permute-start(bf16[256,1536]{1,0:T(8,128)(2,1)} %get-tuple-element.265), channel_id=1, source_target_pairs={{0,8},{4,12},{8,0},{12,4},{1,9},{5,13},{9,1},{13,5},{2,10},{6,14},... | collective-permute-start | bytes 2359304 | tf_op jit(solution)/shard_map/ppermute | solution.py:1015
  387.4 25.1 %collective-permute-start.26 = (bf16[512,1024]{1,0:T(8,128)(2,1)S(1)}, bf16[512,1024]{1,0:T(8,128)(2,1)}, u32[]{:S(2)}, u32[]{:S(2)}) collective-permute-start(bf16[512,1024]{1,0:T(8,128)(2,1)S(1)} %copy-done.5), channel_id=1, source_target_pairs={{0,16},{16,0},{1,17},{17,1},{2,18},{18,2},{3,19},{19,3},{4,20},{20... | collective-permute-start | bytes 3145736 | tf_op jit(solution)/shard_map/ppermute | solution.py:1015
  415.4 33.2 %collective-permute-start.27 = (bf16[256,1536]{1,0:T(8,128)(2,1)}, bf16[256,1536]{1,0:T(8,128)(2,1)}, u32[]{:S(2)}, u32[]{:S(2)}) collective-permute-start(bf16[256,1536]{1,0:T(8,128)(2,1)} %add_convert_fusion.5), channel_id=1, source_target_pairs={{0,3},{1,0},{2,1},{3,2},{4,7},{5,4},{6,5},{7,6},{8,11},{9,8},{10,9... | collective-permute-start | bytes 2359304 | tf_op jit(solution)/shard_map/ppermute | solution.py:1010
  416.2 34.0 %collective-permute-start.30 = (bf16[640,1024]{1,0:T(8,128)(2,1)S(1)}, bf16[640,1024]{1,0:T(8,128)(2,1)}, u32[]{:S(2)}, u32[]{:S(2)}) collective-permute-start(bf16[640,1024]{1,0:T(8,128)(2,1)S(1)} %copy-done.1), channel_id=1, source_target_pairs={{0,16},{16,0},{1,17},{17,1},{2,18},{18,2},{3,19},{19,3},{4,20},{20... | collective-permute-start | bytes 3932168 | tf_op jit(solution)/shard_map/ppermute | solution.py:1015
  456.4 24.7 %collective-permute-start.33 = (bf16[512,1024]{1,0:T(8,128)(2,1)}, bf16[512,1024]{1,0:T(8,128)(2,1)}, u32[]{:S(2)}, u32[]{:S(2)}) collective-permute-start(bf16[512,1024]{1,0:T(8,128)(2,1)} %get-tuple-element.307.refs_0_), channel_id=1, source_target_pairs={{0,16},{16,0},{1,17},{17,1},{2,18},{18,2},{3,19},{19,3},{4,20},{20... | collective-permute-start | bytes 3145736 | tf_op jit(solution)/shard_map/ppermute | solution.py:1015
  483.3 22.7 %collective-permute-start.36 = (bf16[512,1024]{1,0:T(8,128)(2,1)S(1)}, bf16[512,1024]{1,0:T(8,128)(2,1)S(1)}, u32[]{:S(2)}, u32[]{:S(2)}) collective-permute-start(bf16[512,1024]{1,0:T(8,128)(2,1)S(1)} %copy-done.2), channel_id=1, source_target_pairs={{0,16},{16,0},{1,17},{17,1},{2,18},{18,2},{3,19},{19,3},{4,20},{20... | collective-permute-start | bytes 3145736 | tf_op jit(solution)/shard_map/ppermute | solution.py:1015
  523.5 25.0 %all-to-all-start.2 = ((bf16[4,256,384]{2,1,0:T(8,128)(2,1)}), bf16[4,256,384]{2,1,0:T(8,128)(2,1)}, u32[]{:S(2)}, u32[]{:S(2)}) async-start(bf16[4,256,384]{2,1,0:T(8,128)(2,1)} %get-tuple-element.319), calls=%async_computation.3 | async-start | bytes 1572864 | tf_op jit(solution)/shard_map/all_to_all | solution.py:1290
  528.2 25.6 %collective-permute-start.39 = (bf16[512,1024]{1,0:T(8,128)(2,1)}, bf16[512,1024]{1,0:T(8,128)(2,1)}, u32[]{:S(2)}, u32[]{:S(2)}) collective-permute-start(bf16[512,1024]{1,0:T(8,128)(2,1)} %get-tuple-element.332.refs_2_), channel_id=1, source_target_pairs={{0,16},{16,0},{1,17},{17,1},{2,18},{18,2},{3,19},{19,3},{4,20},{20... | collective-permute-start | bytes 3145736 | tf_op jit(solution)/shard_map/ppermute | solution.py:1015
  553.8 22.1 %collective-permute-start.40 = (f32[1,1,1,8,1536]{4,3,2,1,0:T(8,128)S(1)}, f32[1,1,1,8,1536]{4,3,2,1,0:T(8,128)S(1)}, u32[]{:S(2)}, u32[]{:S(2)}) collective-permute-start(f32[1,1,1,8,1536]{4,3,2,1,0:T(8,128)S(1)} %dynamic-slice_add_fusion.1), channel_id=1, source_target_pairs={{0,1},{1,0},{2,3},{3,2},{4,5},{5,4},{6,7},{7,6},{8,9},{9,8},{10,11... | collective-permute-start | bytes 147464 | tf_op jit(solution)/shard_map/ppermute | solution.py:1015
  557.0 41.1 %collective-permute-start.44 = (bf16[2,1,1,192,1536]{4,3,1,0,2:T(8,128)(2,1)}, bf16[2,1,1,192,1536]{4,3,1,0,2:T(8,128)(2,1)}, u32[]{:S(2)}, u32[]{:S(2)}) collective-permute-start(bf16[2,1,1,192,1536]{4,3,1,0,2:T(8,128)(2,1)} %get-tuple-element.346), channel_id=1, source_target_pairs={{0,8},{4,12},{8,0},{12,4},{1,9},{5,13},{9,1},{13,5},{2,10},{6,14},... | collective-permute-start | bytes 3538952 | tf_op jit(solution)/shard_map/ppermute | solution.py:1015
  579.8 20.7 %collective-permute-start.47 = (bf16[256,1536]{1,0:T(8,128)(2,1)}, bf16[256,1536]{1,0:T(8,128)(2,1)}, u32[]{:S(2)}, u32[]{:S(2)}) collective-permute-start(bf16[256,1536]{1,0:T(8,128)(2,1)} %get-tuple-element.361.refs_1_), channel_id=1, source_target_pairs={{0,16},{16,0},{1,17},{17,1},{2,18},{18,2},{3,19},{19,3},{4,20},{20... | collective-permute-start | bytes 2359304 | tf_op jit(solution)/shard_map/ppermute | solution.py:1015
  602.0 21.0 %collective-permute-start.48 = (bf16[256,1536]{1,0:T(8,128)(2,1)S(1)}, bf16[256,1536]{1,0:T(8,128)(2,1)S(1)}, u32[]{:S(2)}, u32[]{:S(2)}) collective-permute-start(bf16[256,1536]{1,0:T(8,128)(2,1)S(1)} %add_convert_fusion.2), channel_id=1, source_target_pairs={{0,3},{1,0},{2,1},{3,2},{4,7},{5,4},{6,5},{7,6},{8,11},{9,8},{10,9... | collective-permute-start | bytes 2359304 | tf_op jit(solution)/shard_map/ppermute | solution.py:1010
  624.0 26.0 %collective-permute-start.53 = (bf16[256,1536]{1,0:T(8,128)(2,1)}, bf16[256,1536]{1,0:T(8,128)(2,1)S(1)}, u32[]{:S(2)}, u32[]{:S(2)}) collective-permute-start(bf16[256,1536]{1,0:T(8,128)(2,1)} %add_convert_fusion.1), channel_id=1, source_target_pairs={{0,3},{1,0},{2,1},{3,2},{4,7},{5,4},{6,5},{7,6},{8,11},{9,8},{10,9... | collective-permute-start | bytes 2359304 | tf_op jit(solution)/shard_map/ppermute | solution.py:1010
  627.9 21.2 %collective-permute-start.54 = (f32[2,1536]{1,0:T(2,128)S(1)}, f32[2,1536]{1,0:T(2,128)S(1)}, u32[]{:S(2)}, u32[]{:S(2)}) collective-permute-start(f32[2,1536]{1,0:T(2,128)S(1)} %add.453), channel_id=1, source_target_pairs={{0,2},{1,3},{2,0},{3,1},{4,6},{5,7},{6,4},{7,5},{8,10},{9,11},{10,... | collective-permute-start | bytes 36872 | tf_op jit(solution)/shard_map/ppermute | solution.py:1015
  628.0 21.1 %collective-permute-start.55 = (f32[1,1,1,8,1536]{4,3,2,1,0:T(8,128)S(1)}, f32[1,1,1,8,1536]{4,3,2,1,0:T(8,128)S(1)}, u32[]{:S(2)}, u32[]{:S(2)}) collective-permute-start(f32[1,1,1,8,1536]{4,3,2,1,0:T(8,128)S(1)} %add.454), channel_id=1, source_target_pairs={{0,8},{4,12},{8,0},{12,4},{1,9},{5,13},{9,1},{13,5},{2,10},{6,14},... | collective-permute-start | bytes 147464 | tf_op jit(solution)/shard_map/ppermute | solution.py:1015
  629.6 27.2 %all-to-all-start.3 = ((bf16[4,1,1,1,192,384]{5,4,3,2,1,0:T(8,128)(2,1)}), bf16[4,1,1,1,192,384]{5,4,3,2,1,0:T(8,128)(2,1)}, u32[]{:S(2)}, u32[]{:S(2)}) async-start(bf16[4,1,1,1,192,384]{5,4,3,2,1,0:T(8,128)(2,1)} %pad_maximum_fusion.2), calls=%async_computation.4 | async-start | bytes 1179648 | tf_op jit(solution)/shard_map/all_to_all | solution.py:1355
  (95 other events, 1066.1 us)
Sparse Core Ops, SparseCore 0:
  9.9 30.0 all-gather.3
  42.9 85.6 all-gather.5
  176.2 110.7 all-gather.7
  291.5 151.9 reduce-scatter.1

commit v4 on v3

--- a/solution.py
+++ b/solution.py
@@ -165,7 +165,7 @@
 
 def attn_backward_body(
     chunks, here_ref, grads_ref, q_ref, kk_ref, vv_ref, lse_ref, cos_ref, sin_ref, start_ref,
-    turned_ref, dk, dv, dq,
+    turned_ref, first_ref, dk, dv, dq,
 ):
     tok = q_ref.shape[0] // chunks
     here = here_ref[0]
@@ -223,6 +223,11 @@
         for i, vals_of in enumerate(tiles):
             turned_ref[to, 128 * i : 128 * (i + 1)] = vals_of.astype(BF16)
 
+        @pl.when(lax.rem(here + (chunks - a), chunks) == chunks - 1)
+        def _(tiles=tiles):
+            for i, vals_of in enumerate(tiles):
+                first_ref[:, 128 * i : 128 * (i + 1)] = vals_of.astype(BF16)
+
 
 def attn_backward(here, grads, q_rows, key_rows, value_rows, lse, cos, sin, starts, chunks):
     total = q_rows.shape[0]
@@ -235,8 +240,14 @@
             whole_block(v)
             for v in (grads, q_rows, key_rows, value_rows, lse, cos, sin, starts)
         ],
-        out_specs=whole_block(jax.ShapeDtypeStruct((total, cols), BF16)),
-        out_shape=jax.ShapeDtypeStruct((total, cols), BF16),
+        out_specs=[
+            whole_block(jax.ShapeDtypeStruct((total, cols), BF16)),
+            whole_block(jax.ShapeDtypeStruct((total // chunks, cols), BF16)),
+        ],
+        out_shape=[
+            jax.ShapeDtypeStruct((total, cols), BF16),
+            jax.ShapeDtypeStruct((total // chunks, cols), BF16),
+        ],
         scratch_shapes=[
             pltpu.VMEM((total, 256), F32),
             pltpu.VMEM((total, 256), F32),
@@ -815,14 +826,15 @@
 
 
 def mid_back_body(
-    gn_ref, term_ref, mid_ref, dy_ref, gain_ref, out_ref,
+    own_ref, moved_ref, side_ref, term_ref, mid_ref, dy_ref, gain_ref, out_ref,
     grad_ref, low_ref, gain_grad_ref, block_ref,
 ):
     @pl.when(pl.program_id(0) == 0)
     def _():
         mid = mid_ref[...]
         scale = lax.rsqrt(jnp.mean(mid * mid, axis=1, keepdims=True) + EPSILON)
-        grad = gn_ref[...] + term_ref[...]
+        grad = own_ref[...].astype(F32) + moved_ref[...].astype(F32)
+        grad = grad + side_ref[...].astype(F32) + term_ref[...]
         gain_grad_ref[...] = jnp.sum(grad * mid * scale, axis=0, keepdims=True)
         weighted = grad * gain_ref[...]
         inner = jnp.mean(weighted * mid, axis=1, keepdims=True)
@@ -833,10 +845,10 @@
     block_ref[0] = dot_nn(low_ref[...], out_ref[0]).astype(BF16)
 
 
-def mid_back(gn, router_term, middle, out_grad, gain, out_all):
+def mid_back(sums, router_term, middle, out_grad, gain, out_all):
     tok, feat = middle.shape
     groups, _, width = out_all.shape
-    args = (gn, router_term, middle, out_grad, gain[None])
+    args = (*sums, router_term, middle, out_grad, gain[None])
     outs = [
         jax.ShapeDtypeStruct((tok, feat), F32),
         jax.ShapeDtypeStruct((tok, feat), BF16),
@@ -1239,9 +1251,9 @@
     for k in range(cols - 1, -1, -1):
         side = swap(terms[0], "row", 2)
         sent = exchange(*((0, 2), (0, 3), (1, 2), (1, 3))[cols - 1 - k], terms[0])
-        total = terms[1].astype(F32)
+        own_term, moved = terms[1], None
         if gn is not None:
-            total = total + shift(gn, "col", -1).astype(F32)
+            moved = shift(gn, "col", -1)
         if k:
             terms = near_terms(gn_near, after(from_far, terms[0]), cols + k - 1, k - 1, tok)
         if k == cols - 1:
@@ -1278,15 +1290,19 @@
             side, router_term, small = lax.optimization_barrier((side, router_term, small))
         if k == 1:
             side, res = lax.optimization_barrier((side, res))
-        total, side, terms = arrived(lax.optimization_barrier((total, side, terms)), sent)
-        gn = total + side.astype(F32)
+        own_term, moved, side, terms = arrived(
+            lax.optimization_barrier((own_term, moved, side, terms)), sent
+        )
         if k:
+            gn = own_term.astype(F32) + side.astype(F32)
+            if moved is not None:
+                gn = gn + moved.astype(F32)
             gn = gn.astype(BF16)
 
     grad_middle, grad_attn, gain_moe_part, grad_heads = mid_back(
-        gn, router_term, middle, out_grad, norm_gain_moe, out_all
-    )
-    sent = exchange(1, 4, gn)
+        (own_term, moved, side), router_term, middle, out_grad, norm_gain_moe, out_all
+    )
+    sent = exchange(1, 4, side)
     grads_block = lax.all_to_all(
         grad_heads, "col", split_axis=0, concat_axis=0, tiled=True
     )
@@ -1301,12 +1317,14 @@
 
     sent = exchange(1, 0, grads_block)
     small = sum_all[2](small)
-    grad_mixed = attn_backward(
+    grad_mixed, first_mixed = attn_backward(
         here, grads_block.reshape(cols * tok, head_cols), q_rows, key_rows, value_rows, lse,
         cos, sin, starts, cols,
     )
     w_out_sum = sum_out[1][1](w_out_sum)
-    grad_mixed, small = arrived(lax.optimization_barrier((grad_mixed, small)), sent)
+    grad_mixed, first_mixed, small = arrived(
+        lax.optimization_barrier((grad_mixed, first_mixed, small)), sent
+    )
 
     def na_part(k, *earlier):
         mixed = after(grad_mixed[k * tok : (k + 1) * tok], *earlier)
@@ -1316,7 +1334,7 @@
         return arrived(lax.optimization_barrier(values), sent)
 
     sent = exchange(1, 1, grad_mixed)
-    first_na = na_part(cols - 1).astype(BF16)
+    first_na = dot_nt(first_mixed, qkv_own).astype(BF16)
     grad_na = shift(first_na, "col", -1)
     small = sum_all[3](small)
     *w_qkv_sum, gain_attn_part = w_qkv_part(

time: 683 us -> 691 us (1.012)
  waiting for transfers between devices: 279 us -> 298 us
  Pallas kernels: 199 us -> 190 us
  other arithmetic: 43.5 us -> 36.2 us
    ppermute x48, waiting for transfers between devices: 116 us -> 134 us  [swap(): return lax.ppermute(values, axis, [(i, i ^ bit) for i in range(size)])]
  transfers between devices with their start and end apart: 67 -> 67, of which waited for: 29 -> 29; matrix products, arithmetic and copies ran while one was open for 8% -> 8% of each run, Pallas kernels for 27% -> 26%
where the time goes in v4:
time: 691 us; the launch traced here: 687 us
  waiting for transfers between devices  298 us (43%)
  Pallas kernels  190 us (27%)
  starting transfers between devices  79.8 us (12%)
  other arithmetic  36.2 us (5%)
  blocking collectives  33 us (5%)
  matrix products  18.7 us (3%)
  local copies, waits for them, and re-layouts  15.5 us (2%)
  between operations  15 us (2%)
    ppermute x48, waiting for transfers between devices, swap(): return lax.ppermute(values, axis, [(i, i ^ bit) for i in range(size)])  134 us
    ppermute x12, waiting for transfers between devices, shift(): lax.ppermute(values, axis, [(i, (i + by) % size) for i in range(size)])  117 us
    ppermute x48, starting transfers between devices, swap(): return lax.ppermute(values, axis, [(i, i ^ bit) for i in range(size)])  43 us
    pallas_call x1, Pallas kernels, moe_front(): pl.pallas_call(functools.partial(front_body, cap, tile, tiles, group, sou...  42.8 us
    all_to_all x1, blocking collectives, shards(): lax.all_to_all(heads_block.reshape(cols, tok, head_cols), 'col', split_ax...  33 us
    pallas_call x1, Pallas kernels, moe_back_first(): pl.pallas_call(functools.partial(back_first_body, cap, tile, tiles, group...  28.8 us
    pallas_call x1, Pallas kernels, moe_back_last(): pl.pallas_call(functools.partial(back_last_body, cap, tile, tiles, group)...  28.8 us
    pallas_call x1, Pallas kernels, attn_backward(): pl.pallas_call(functools.partial(attn_backward_body, chunks), grid=(1,),...  18.8 us
  transfers between devices with their start and end apart: 67, of which 29 were waited for; matrix products, arithmetic and copies ran while one was open for 8% of the time, Pallas kernels for 26%

profile of v4, /device:TPU:0, one launch (start us, length us, event | category | flops | bytes accessed | tf_op | source)
XLA Modules:
  0.0 686.9 jit_solution(8440451641358453203)
XLA Ops:
  21.9 12.7 %collective-permute-done.refs_1_ = bf16[256,1536]{1,0:T(8,128)(2,1)} collective-permute-done((bf16[256,1536]{1,0:T(8,128)(2,1)S(1)}, bf16[256,1536]{1,0:T(8,128)(2,1)}, u32[]{:S(2)}, u32[]{:S(2)}) %collective-permute-start) | collective-permute-done | bytes 786464 | tf_op jit(solution)/shard_map/ppermute | solution.py:1022
  35.9 17.8 %collective-permute-done.4 = s32[4,8,256]{2,1,0:T(8,128)S(1)} collective-permute-done((s32[4,8,256]{2,1,0:T(8,128)S(1)}, s32[4,8,256]{2,1,0:T(8,128)S(1)}, u32[]{:S(2)}, u32[]{:S(2)}) %collective-permute-start.4) | collective-permute-done | bytes 32800 | tf_op jit(solution)/shard_map/ppermute | solution.py:1027
  58.6 21.9 %collective-permute-done.6 = s32[8,8,256]{2,1,0:T(8,128)S(1)} collective-permute-done((s32[8,8,256]{2,1,0:T(8,128)S(1)}, s32[8,8,256]{2,1,0:T(8,128)S(1)}, u32[]{:S(2)}, u32[]{:S(2)}) %collective-permute-start.6) | collective-permute-done | bytes 65568 | tf_op jit(solution)/shard_map/ppermute | solution.py:1027
  81.4 12.8 %attn_forward.1 = (bf16[1024,768]{1,0:T(8,128)(2,1)}, bf16[1024,256]{1,0:T(8,128)(2,1)}, bf16[1024,256]{1,0:T(8,128)(2,1)}, f32[6,8,256]{2,1,0:T(8,128)}, bf16[1024,384]{1,0:T(8,128)(2,1)}) custom-call(s32[1]{0:T(128)} %bitcast.here_ref, bf16[256,1536]{1,0:T(8,128)(2,1)} %copy-done.23, bf16[256,1536]{1,0:T(8,128)(2,1)} %collective-permute-done.refs_1_, ...), custom_call_target="tpu_custom_call" | custom-call | flops 8053063680 | bytes 5242880 | tf_op jit(solution)/shard_map/attn_forward/pallas_call | solution.py:139
  94.2 33.0 %all_to_all.20 = bf16[4,256,384]{2,1,0:T(8,128)(2,1)S(1)} all-to-all(bf16[4,256,384]{2,1,0:T(8,128)(2,1)} %bitcast.89), channel_id=1, replica_groups=mesh['dp'=2,'row'=4,'col'=4] {'col'}, dimensions={0} | all-to-all | bytes 1572864 | tf_op jit(solution)/shard_map/all_to_all | solution.py:1190
  135.1 20.2 %collective-permute-done.8.refs_1_ = bf16[256,1536]{1,0:T(8,128)(2,1)S(1)} collective-permute-done((bf16[256,1536]{1,0:T(8,128)(2,1)S(1)}, bf16[256,1536]{1,0:T(8,128)(2,1)S(1)}, u32[]{:S(2)}, u32[]{:S(2)}) %collective-permute-start.8) | collective-permute-done | bytes 786464 | tf_op jit(solution)/shard_map/ppermute | solution.py:1022
  156.6 19.4 %collective-permute-done.10.refs_2_ = bf16[256,1536]{1,0:T(8,128)(2,1)S(1)} collective-permute-done((bf16[256,1536]{1,0:T(8,128)(2,1)S(1)}, bf16[256,1536]{1,0:T(8,128)(2,1)S(1)}, u32[]{:S(2)}, u32[]{:S(2)}) %collective-permute-start.10) | collective-permute-done | bytes 786464 | tf_op jit(solution)/shard_map/ppermute | solution.py:1022
  177.9 25.9 %collective-permute-done.12.refs_3_ = bf16[256,1536]{1,0:T(8,128)(2,1)} collective-permute-done((bf16[256,1536]{1,0:T(8,128)(2,1)S(1)}, bf16[256,1536]{1,0:T(8,128)(2,1)}, u32[]{:S(2)}, u32[]{:S(2)}) %collective-permute-start.12) | collective-permute-done | bytes 786464 | tf_op jit(solution)/shard_map/ppermute | solution.py:1022
  207.6 12.5 %collective-permute-done.13.refs_7_ = bf16[256,1536]{1,0:T(8,128)(2,1)} collective-permute-done((bf16[256,1536]{1,0:T(8,128)(2,1)}, bf16[256,1536]{1,0:T(8,128)(2,1)}, u32[]{:S(2)}, u32[]{:S(2)}) %collective-permute-start.13) | collective-permute-done | bytes 786464 | tf_op jit(solution)/shard_map/ppermute | solution.py:1027
  230.0 42.8 %moe_front.1 = (bf16[4096,1536]{1,0:T(8,128)(2,1)}, bf16[2,2048,1536]{2,1,0:T(8,128)(2,1)}, f32[2,2048,1024]{2,1,0:T(8,128)}, f32[2,2048,128]{2,1,0:T(8,128)}, f32[2,16,256]{2,1,0:T(8,128)}) custom-call(s32[1]{0:T(128)} %bitcast.9.first_ref, s32[4,16]{1,0:T(4,128)} %pad_add_fusion.4.ids_ref, s32[2,17]{1,0:T(2,128)} %bitcast.96, ...), custom_call_target="tpu_custom_call" | custom-call | flops 9663676416 | bytes 31457280 | tf_op jit(solution)/shard_map/moe_front/pallas_call | solution.py:412
  272.8 14.2 %all-gather.8.cloned.1.call-done.refs_0_.refs_1_.refs_2_.refs_3_ = bf16[4096,1536]{1,0:T(8,128)(2,1)} async-done(((bf16[256,1536]{1,0:T(8,128)(2,1)}), bf16[4096,1536]{1,0:T(8,128)(2,1)}) %all-gather.8.cloned.1.call-update) | async-done | bytes 12582928 | tf_op jit(solution)/shard_map/all_gather | solution.py:1203
  287.0 28.8 %moe_back_first.1 = (bf16[2048,1536]{1,0:T(8,128)(2,1)}, f32[2048,128]{1,0:T(8,128)}, bf16[1,2048,1536]{2,1,0:T(8,128)(2,1)}, bf16[512,1536]{1,0:T(8,128)(2,1)},...) custom-call(s32[2,17]{1,0:T(2,128)} %bitcast.97, s32[4,16]{1,0:T(4,128)} %pad_add_fusion.4.ids_ref, ...), custom_call_target="tpu_custom_call" | custom-call | flops 12884901888 | bytes 62914560 | tf_op jit(solution)/shard_map/moe_back_first/pallas_call | solution.py:576
  317.5 28.8 %moe_back_last.1 = (bf16[2048,1536]{1,0:T(8,128)(2,1)}, bf16[2048,1536]{1,0:T(8,128)(2,1)}, f32[16,8,256]{2,1,0:T(8,128)}, bf16[256,1536]{1,0:T(8,128)(2,1)}, bf...) custom-call(s32[2,17]{1,0:T(2,128)} %bitcast.98, ...), custom_call_target="tpu_custom_call" | custom-call | flops 12884901888 | bytes 31457280 | tf_op jit(solution)/shard_map/moe_back_last/pallas_call | solution.py:737
  346.2 7.1 %collective-permute-done.22.refs_1_ = bf16[512,1536]{1,0:T(8,128)(2,1)S(1)} collective-permute-done((bf16[512,1536]{1,0:T(8,128)(2,1)}, bf16[512,1536]{1,0:T(8,128)(2,1)S(1)}, u32[]{:S(2)}, u32[]{:S(2)}) %collective-permute-start.22) | collective-permute-done | bytes 1572896 | tf_op jit(solution)/shard_map/ppermute | solution.py:1027
  357.5 11.7 %all-to-all-start.1 = ((f32[16,8,256]{2,1,0:T(8,128)}), f32[16,8,256]{2,1,0:T(8,128)S(1)}, u32[]{:S(2)}, u32[]{:S(2)}) async-start(f32[16,8,256]{2,1,0:T(8,128)} %get-tuple-element.268), calls=%async_computation.1 | async-start | bytes 262144 | tf_op jit(solution)/shard_map/all_to_all | solution.py:1245
  369.9 10.6 %all-to-all-done.1 = f32[16,8,256]{2,1,0:T(8,128)S(1)} async-done(((f32[16,8,256]{2,1,0:T(8,128)}), f32[16,8,256]{2,1,0:T(8,128)S(1)}, u32[]{:S(2)}, u32[]{:S(2)}) %all-to-all-start.1) | async-done | bytes 131104 | tf_op jit(solution)/shard_map/all_to_all | solution.py:1245
  388.8 16.3 %collective-permute-done.25 = bf16[256,1536]{1,0:T(8,128)(2,1)S(1)} collective-permute-done((bf16[256,1536]{1,0:T(8,128)(2,1)}, bf16[256,1536]{1,0:T(8,128)(2,1)S(1)}, u32[]{:S(2)}, u32[]{:S(2)}) %collective-permute-start.25) | collective-permute-done | bytes 786464 | tf_op jit(solution)/shard_map/ppermute | solution.py:1027
  420.7 11.9 %collective-permute-done.28 = bf16[256,1536]{1,0:T(8,128)(2,1)} collective-permute-done((bf16[256,1536]{1,0:T(8,128)(2,1)}, bf16[256,1536]{1,0:T(8,128)(2,1)}, u32[]{:S(2)}, u32[]{:S(2)}) %collective-permute-start.28) | collective-permute-done | bytes 786464 | tf_op jit(solution)/shard_map/ppermute | solution.py:1027
  432.6 16.9 %collective-permute-done.27 = bf16[256,1536]{1,0:T(8,128)(2,1)} collective-permute-done((bf16[256,1536]{1,0:T(8,128)(2,1)}, bf16[256,1536]{1,0:T(8,128)(2,1)}, u32[]{:S(2)}, u32[]{:S(2)}) %collective-permute-start.27) | collective-permute-done | bytes 786464 | tf_op jit(solution)/shard_map/ppermute | solution.py:1022
  460.8 8.5 %collective-permute-done.32 = bf16[256,1536]{1,0:T(8,128)(2,1)} collective-permute-done((bf16[256,1536]{1,0:T(8,128)(2,1)}, bf16[256,1536]{1,0:T(8,128)(2,1)}, u32[]{:S(2)}, u32[]{:S(2)}) %collective-permute-start.32) | collective-permute-done | bytes 786464 | tf_op jit(solution)/shard_map/ppermute | solution.py:1027
  473.3 7.5 %collective-permute-done.33.refs_3_ = bf16[512,1024]{1,0:T(8,128)(2,1)} collective-permute-done((bf16[512,1024]{1,0:T(8,128)(2,1)}, bf16[512,1024]{1,0:T(8,128)(2,1)}, u32[]{:S(2)}, u32[]{:S(2)}) %collective-permute-start.33) | collective-permute-done | bytes 1048608 | tf_op jit(solution)/shard_map/ppermute | solution.py:1027
  486.8 15.0 %collective-permute-done.34.moved_ref = bf16[256,1536]{1,0:T(8,128)(2,1)S(1)} collective-permute-done((bf16[256,1536]{1,0:T(8,128)(2,1)S(1)}, bf16[256,1536]{1,0:T(8,128)(2,1)S(1)}, u32[]{:S(2)}, u32[]{:S(2)}) %collective-permute-start.34) | collective-permute-done | bytes 786464 | tf_op jit(solution)/shard_map/ppermute | solution.py:1022
  505.3 8.8 %mid_back.1 = (f32[256,1536]{1,0:T(8,128)}, bf16[256,1536]{1,0:T(8,128)(2,1)}, f32[1,1536]{1,0:T(1,128)}, bf16[4,256,384]{2,1,0:T(8,128)(2,1)}) custom-call(bf16[256,1536]{1,0:T(8,128)(2,1)} %get-tuple-element.331.own_ref, bf16[256,1536]{1,0:T(8,128)(2,1)} %copy-done.34, bf16[256,1536]{1,0:T(8,128)(2,1)} %copy-done.35, f32[256,1536]{1,0:T(8,128)} %fusion.18.term_ref, ...), custom_call_target="tpu_custom_call" | custom-call | flops 1207959552 | bytes 9437184 | tf_op jit(solution)/shard_map/mid_back/pallas_call | solution.py:858
  514.1 6.0 w_out_part.1
  532.3 14.0 %all-to-all-done.2 = bf16[4,256,384]{2,1,0:T(8,128)(2,1)} async-done(((bf16[4,256,384]{2,1,0:T(8,128)(2,1)}), bf16[4,256,384]{2,1,0:T(8,128)(2,1)}, u32[]{:S(2)}, u32[]{:S(2)}) %all-to-all-start.2) | async-done | bytes 786464 | tf_op jit(solution)/shard_map/all_to_all | solution.py:1306
  546.2 5.2 collective-permute-done.39.refs_5_
  556.4 18.8 %attn_backward.1 = (bf16[1024,640]{1,0:T(8,128)(2,1)}, bf16[256,640]{1,0:T(8,128)(2,1)}) custom-call(s32[1]{0:T(128)} %bitcast.here_ref, bf16[1024,384]{1,0:T(8,128)(2,1)} %bitcast.22.grads_ref, bf16[1024,768]{1,0:T(8,128)(2,1)} %get-tuple-element.350.q_ref, bf16[1024,256]{1,0:T(8,128)(2,1)} %get-tuple-element.351.kk_ref, ...), custom_call_target="tpu_custom_call" | custom-call | flops 12000000000 | bytes 1048576 | tf_op jit(solution)/shard_map/attn_backward/pallas_call | solution.py:235
  581.4 11.8 %w_qkv_part.1 = (bf16[4,192,640]{2,1,0:T(8,128)(2,1)}, bf16[4,192,640]{2,1,0:T(8,128)(2,1)}, f32[1,1536]{1,0:T(1,128)}) custom-call(s32[1]{0:T(128)} %bitcast.19.core_ref, bf16[1024,1536]{1,0:T(8,128)(2,1)} %pad_maximum_fusion.rows_ref, bf16[1024,640]{1,0:T(8,128)(2,1)} %get-tuple-element.368.mixed_ref, ...), custom_call_target="tpu_custom_call" | custom-call | flops 12000000000 | bytes 1048576 | tf_op jit(solution)/shard_map/w_qkv_part/pallas_call | solution.py:964
  600.5 14.1 %collective-permute-done.47.refs_3_ = bf16[256,1536]{1,0:T(8,128)(2,1)S(1)} collective-permute-done((bf16[256,1536]{1,0:T(8,128)(2,1)S(1)}, bf16[256,1536]{1,0:T(8,128)(2,1)S(1)}, u32[]{:S(2)}, u32[]{:S(2)}) %collective-permute-start.47) | collective-permute-done | bytes 786464 | tf_op jit(solution)/shard_map/ppermute | solution.py:1027
  623.7 8.7 %add_pairs.4.refs_6_ = f32[2,1536,1024]{2,1,0:T(8,128)} custom-call(bf16[384,1024]{1,0:T(8,128)(2,1)S(1)} %copy-done.10, bf16[512,1024]{1,0:T(8,128)(2,1)} %get-tuple-element.285.refs_1_, bf16[640,1024]{1,0:T(8,128)(2,1)S(1)} %copy-done.1, bf16[384,1024]{1,0:T(8,128)(2,1)S(1)} %copy-done.12, bf16[512,1024]{1,0:T(8,128)(2,1)} %collective-permute-done.26.refs_4_, ...), custom_call_target="tpu_custom_call" | custom-call | flops 12000000000 | bytes 1048576 | tf_op jit(solution)/shard_map/add_pairs/pallas_call | solution.py:814
  652.9 5.1 add_pairs.6
  663.7 6.2 all-to-all-done.3
  (345 shorter events, 177.0 us)
Async XLA Ops:
  7.2 73.3 %all-gather.4.cloned.1.call-start = ((), (), s32[]{:S(2)}) async-start(), calls=%async_computation.5 | async-start | bytes 2211840 | tf_op jit(solution)/shard_map/all_gather | solution.py:1173
  7.9 120.6 %all-gather.6.cloned.1.call-start = ((), (), s32[]{:S(2)}) async-start(), calls=%async_computation.6 | async-start | bytes 4866048 | tf_op jit(solution)/shard_map/all_gather | solution.py:1174
  8.7 278.3 %all-gather.8.cloned.1.call-start = ((), (), s32[]{:S(2)}) async-start(), calls=%async_computation.7 | async-start | bytes 13369344 | tf_op jit(solution)/shard_map/all_gather | solution.py:1203
  11.6 23.0 %collective-permute-start = (bf16[256,1536]{1,0:T(8,128)(2,1)S(1)}, bf16[256,1536]{1,0:T(8,128)(2,1)}, u32[]{:S(2)}, u32[]{:S(2)}) collective-permute-start(bf16[256,1536]{1,0:T(8,128)(2,1)S(1)} %fusion.4.refs_0_), channel_id=1, source_target_pairs={{0,1},{1,2},{2,3},{3,0},{4,5},{5,6},{6,7},{7,4},{8,9},{9,10},{10,1... | collective-permute-start | bytes 2359304 | tf_op jit(solution)/shard_map/ppermute | solution.py:1022
  34.6 21.9 %collective-permute-start.3 = (bf16[256,1536]{1,0:T(8,128)(2,1)}, bf16[256,1536]{1,0:T(8,128)(2,1)S(1)}, u32[]{:S(2)}, u32[]{:S(2)}) collective-permute-start(bf16[256,1536]{1,0:T(8,128)(2,1)} %collective-permute-done.refs_1_), channel_id=1, source_target_pairs={{0,1},{1,2},{2,3},{3,0},{4,5},{5,6},{6,7},{7,4},{8,9},{9,10},{10,1... | collective-permute-start | bytes 2359304 | tf_op jit(solution)/shard_map/ppermute | solution.py:1022
  56.5 24.0 %collective-permute-start.5 = (bf16[256,1536]{1,0:T(8,128)(2,1)S(1)}, bf16[256,1536]{1,0:T(8,128)(2,1)S(1)}, u32[]{:S(2)}, u32[]{:S(2)}) collective-permute-start(bf16[256,1536]{1,0:T(8,128)(2,1)S(1)} %collective-permute-done.3.refs_2_), channel_id=1, source_target_pairs={{0,1},{1,2},{2,3},{3,0},{4,5},{5,6},{6,7},{7,4},{8,9},{9,10},{10,1... | collective-permute-start | bytes 2359304 | tf_op jit(solution)/shard_map/ppermute | solution.py:1022
  56.7 23.8 %collective-permute-start.6 = (s32[8,8,256]{2,1,0:T(8,128)S(1)}, s32[8,8,256]{2,1,0:T(8,128)S(1)}, u32[]{:S(2)}, u32[]{:S(2)}) collective-permute-start(s32[8,8,256]{2,1,0:T(8,128)S(1)} %pad_add_fusion.1), channel_id=1, source_target_pairs={{0,2},{1,3},{2,0},{3,1},{4,6},{5,7},{6,4},{7,5},{8,10},{9,11},{10,... | collective-permute-start | bytes 196616 | tf_op jit(solution)/shard_map/ppermute | solution.py:1027
  133.8 21.6 %collective-permute-start.8 = (bf16[256,1536]{1,0:T(8,128)(2,1)S(1)}, bf16[256,1536]{1,0:T(8,128)(2,1)S(1)}, u32[]{:S(2)}, u32[]{:S(2)}) collective-permute-start(bf16[256,1536]{1,0:T(8,128)(2,1)S(1)} %multiply_convert_fusion.refs_0_), channel_id=1, source_target_pairs={{0,1},{1,2},{2,3},{3,0},{4,5},{5,6},{6,7},{7,4},{8,9},{9,10},{10,1... | collective-permute-start | bytes 2359304 | tf_op jit(solution)/shard_map/ppermute | solution.py:1022
  133.8 21.5 %collective-permute-start.7 = (bf16[256,1536]{1,0:T(8,128)(2,1)S(1)}, bf16[256,1536]{1,0:T(8,128)(2,1)}, u32[]{:S(2)}, u32[]{:S(2)}) collective-permute-start(bf16[256,1536]{1,0:T(8,128)(2,1)S(1)} %multiply_convert_fusion.refs_0_), channel_id=1, source_target_pairs={{0,8},{4,12},{8,0},{12,4},{1,9},{5,13},{9,1},{13,5},{2,10},{6,14},... | collective-permute-start | bytes 2359304 | tf_op jit(solution)/shard_map/ppermute | solution.py:1027
  155.3 20.7 %collective-permute-start.10 = (bf16[256,1536]{1,0:T(8,128)(2,1)S(1)}, bf16[256,1536]{1,0:T(8,128)(2,1)S(1)}, u32[]{:S(2)}, u32[]{:S(2)}) collective-permute-start(bf16[256,1536]{1,0:T(8,128)(2,1)S(1)} %collective-permute-done.8.refs_1_), channel_id=1, source_target_pairs={{0,1},{1,2},{2,3},{3,0},{4,5},{5,6},{6,7},{7,4},{8,9},{9,10},{10,1... | collective-permute-start | bytes 2359304 | tf_op jit(solution)/shard_map/ppermute | solution.py:1022
  176.1 284.7 %reduce-scatter.2.cloned.1.call-start = ((), (), s32[]{:S(2)}) async-start(), calls=%async_computation.8 | async-start | bytes 13369344 | tf_op jit(solution)/shard_map/reduce_scatter | solution.py:1214
  176.1 27.7 %collective-permute-start.12 = (bf16[256,1536]{1,0:T(8,128)(2,1)S(1)}, bf16[256,1536]{1,0:T(8,128)(2,1)}, u32[]{:S(2)}, u32[]{:S(2)}) collective-permute-start(bf16[256,1536]{1,0:T(8,128)(2,1)S(1)} %collective-permute-done.10.refs_2_), channel_id=1, source_target_pairs={{0,1},{1,2},{2,3},{3,0},{4,5},{5,6},{6,7},{7,4},{8,9},{9,10},{10,1... | collective-permute-start | bytes 2359304 | tf_op jit(solution)/shard_map/ppermute | solution.py:1022
  176.6 27.2 %collective-permute-start.11 = (bf16[256,1536]{1,0:T(8,128)(2,1)S(1)}, bf16[256,1536]{1,0:T(8,128)(2,1)S(1)}, u32[]{:S(2)}, u32[]{:S(2)}) collective-permute-start(bf16[256,1536]{1,0:T(8,128)(2,1)S(1)} %collective-permute-done.10.refs_2_), channel_id=1, source_target_pairs={{0,8},{4,12},{8,0},{12,4},{1,9},{5,13},{9,1},{13,5},{2,10},{6,14},... | collective-permute-start | bytes 2359304 | tf_op jit(solution)/shard_map/ppermute | solution.py:1027
  315.8 37.5 %collective-permute-start.22 = (bf16[512,1536]{1,0:T(8,128)(2,1)}, bf16[512,1536]{1,0:T(8,128)(2,1)S(1)}, u32[]{:S(2)}, u32[]{:S(2)}) collective-permute-start(bf16[512,1536]{1,0:T(8,128)(2,1)} %get-tuple-element.266.refs_0_), channel_id=1, source_target_pairs={{0,16},{16,0},{1,17},{17,1},{2,18},{18,2},{3,19},{19,3},{4,20},{20... | collective-permute-start | bytes 4718600 | tf_op jit(solution)/shard_map/ppermute | solution.py:1027
  353.3 27.2 %collective-permute-start.23 = (bf16[2048,1536]{1,0:T(8,128)(2,1)}, bf16[2048,1536]{1,0:T(8,128)(2,1)}, u32[]{:S(2)}, u32[]{:S(2)}) collective-permute-start(bf16[2048,1536]{1,0:T(8,128)(2,1)} %get-tuple-element.267), channel_id=1, source_target_pairs={{0,4},{4,0},{8,12},{12,8},{1,5},{5,1},{9,13},{13,9},{2,6},{6,2},{1... | collective-permute-start | bytes 18874376 | tf_op jit(solution)/shard_map/ppermute | solution.py:1027
  355.0 25.5 %collective-permute-start.24 = (bf16[384,1024]{1,0:T(8,128)(2,1)S(1)}, bf16[384,1024]{1,0:T(8,128)(2,1)S(1)}, u32[]{:S(2)}, u32[]{:S(2)}) collective-permute-start(bf16[384,1024]{1,0:T(8,128)(2,1)S(1)} %copy-done.9), channel_id=1, source_target_pairs={{0,16},{16,0},{1,17},{17,1},{2,18},{18,2},{3,19},{19,3},{4,20},{20... | collective-permute-start | bytes 2359304 | tf_op jit(solution)/shard_map/ppermute | solution.py:1027
  357.5 23.1 %all-to-all-start.1 = ((f32[16,8,256]{2,1,0:T(8,128)}), f32[16,8,256]{2,1,0:T(8,128)S(1)}, u32[]{:S(2)}, u32[]{:S(2)}) async-start(f32[16,8,256]{2,1,0:T(8,128)} %get-tuple-element.268), calls=%async_computation.1 | async-start | bytes 262144 | tf_op jit(solution)/shard_map/all_to_all | solution.py:1245
  384.0 21.0 %collective-permute-start.25 = (bf16[256,1536]{1,0:T(8,128)(2,1)}, bf16[256,1536]{1,0:T(8,128)(2,1)S(1)}, u32[]{:S(2)}, u32[]{:S(2)}) collective-permute-start(bf16[256,1536]{1,0:T(8,128)(2,1)} %get-tuple-element.275), channel_id=1, source_target_pairs={{0,8},{4,12},{8,0},{12,4},{1,9},{5,13},{9,1},{13,5},{2,10},{6,14},... | collective-permute-start | bytes 2359304 | tf_op jit(solution)/shard_map/ppermute | solution.py:1027
  384.5 25.9 %collective-permute-start.26 = (bf16[512,1024]{1,0:T(8,128)(2,1)}, bf16[512,1024]{1,0:T(8,128)(2,1)}, u32[]{:S(2)}, u32[]{:S(2)}) collective-permute-start(bf16[512,1024]{1,0:T(8,128)(2,1)} %get-tuple-element.285.refs_1_), channel_id=1, source_target_pairs={{0,16},{16,0},{1,17},{17,1},{2,18},{18,2},{3,19},{19,3},{4,20},{20... | collective-permute-start | bytes 3145736 | tf_op jit(solution)/shard_map/ppermute | solution.py:1027
  410.5 22.1 %collective-permute-start.28 = (bf16[256,1536]{1,0:T(8,128)(2,1)}, bf16[256,1536]{1,0:T(8,128)(2,1)}, u32[]{:S(2)}, u32[]{:S(2)}) collective-permute-start(bf16[256,1536]{1,0:T(8,128)(2,1)} %get-tuple-element.289), channel_id=1, source_target_pairs={{0,8},{4,12},{8,0},{12,4},{1,9},{5,13},{9,1},{13,5},{2,10},{6,14},... | collective-permute-start | bytes 2359304 | tf_op jit(solution)/shard_map/ppermute | solution.py:1027
  411.4 38.1 %collective-permute-start.30 = (bf16[640,1024]{1,0:T(8,128)(2,1)S(1)}, bf16[640,1024]{1,0:T(8,128)(2,1)}, u32[]{:S(2)}, u32[]{:S(2)}) collective-permute-start(bf16[640,1024]{1,0:T(8,128)(2,1)S(1)} %copy-done.1), channel_id=1, source_target_pairs={{0,16},{16,0},{1,17},{17,1},{2,18},{18,2},{3,19},{19,3},{4,20},{20... | collective-permute-start | bytes 3932168 | tf_op jit(solution)/shard_map/ppermute | solution.py:1027
  413.9 35.6 %collective-permute-start.27 = (bf16[256,1536]{1,0:T(8,128)(2,1)}, bf16[256,1536]{1,0:T(8,128)(2,1)}, u32[]{:S(2)}, u32[]{:S(2)}) collective-permute-start(bf16[256,1536]{1,0:T(8,128)(2,1)} %add_convert_fusion.5), channel_id=1, source_target_pairs={{0,3},{1,0},{2,1},{3,2},{4,7},{5,4},{6,5},{7,6},{8,11},{9,8},{10,9... | collective-permute-start | bytes 2359304 | tf_op jit(solution)/shard_map/ppermute | solution.py:1022
  456.1 24.6 %collective-permute-start.33 = (bf16[512,1024]{1,0:T(8,128)(2,1)}, bf16[512,1024]{1,0:T(8,128)(2,1)}, u32[]{:S(2)}, u32[]{:S(2)}) collective-permute-start(bf16[512,1024]{1,0:T(8,128)(2,1)} %get-tuple-element.320.refs_0_), channel_id=1, source_target_pairs={{0,16},{16,0},{1,17},{17,1},{2,18},{18,2},{3,19},{19,3},{4,20},{20... | collective-permute-start | bytes 3145736 | tf_op jit(solution)/shard_map/ppermute | solution.py:1027
  480.7 23.6 %collective-permute-start.36 = (bf16[512,1024]{1,0:T(8,128)(2,1)}, bf16[512,1024]{1,0:T(8,128)(2,1)S(1)}, u32[]{:S(2)}, u32[]{:S(2)}) collective-permute-start(bf16[512,1024]{1,0:T(8,128)(2,1)} %get-tuple-element.330.refs_1_), channel_id=1, source_target_pairs={{0,16},{16,0},{1,17},{17,1},{2,18},{18,2},{3,19},{19,3},{4,20},{20... | collective-permute-start | bytes 3145736 | tf_op jit(solution)/shard_map/ppermute | solution.py:1027
  521.3 25.0 %all-to-all-start.2 = ((bf16[4,256,384]{2,1,0:T(8,128)(2,1)}), bf16[4,256,384]{2,1,0:T(8,128)(2,1)}, u32[]{:S(2)}, u32[]{:S(2)}) async-start(bf16[4,256,384]{2,1,0:T(8,128)(2,1)} %get-tuple-element.335), calls=%async_computation.3 | async-start | bytes 1572864 | tf_op jit(solution)/shard_map/all_to_all | solution.py:1306
  525.9 25.6 %collective-permute-start.39 = (bf16[512,1024]{1,0:T(8,128)(2,1)}, bf16[512,1024]{1,0:T(8,128)(2,1)}, u32[]{:S(2)}, u32[]{:S(2)}) collective-permute-start(bf16[512,1024]{1,0:T(8,128)(2,1)} %get-tuple-element.348.refs_2_), channel_id=1, source_target_pairs={{0,16},{16,0},{1,17},{17,1},{2,18},{18,2},{3,19},{19,3},{4,20},{20... | collective-permute-start | bytes 3145736 | tf_op jit(solution)/shard_map/ppermute | solution.py:1027
  551.5 23.7 %collective-permute-start.40 = (f32[1,1,1,8,1536]{4,3,2,1,0:T(8,128)S(1)}, f32[1,1,1,8,1536]{4,3,2,1,0:T(8,128)S(1)}, u32[]{:S(2)}, u32[]{:S(2)}) collective-permute-start(f32[1,1,1,8,1536]{4,3,2,1,0:T(8,128)S(1)} %dynamic-slice_add_fusion.1), channel_id=1, source_target_pairs={{0,1},{1,0},{2,3},{3,2},{4,5},{5,4},{6,7},{7,6},{8,9},{9,8},{10,11... | collective-permute-start | bytes 147464 | tf_op jit(solution)/shard_map/ppermute | solution.py:1027
  553.2 22.1 %collective-permute-start.41 = (bf16[256,1536]{1,0:T(8,128)(2,1)}, bf16[256,1536]{1,0:T(8,128)(2,1)}, u32[]{:S(2)}, u32[]{:S(2)}) collective-permute-start(bf16[256,1536]{1,0:T(8,128)(2,1)} %get-tuple-element.361.refs_0_), channel_id=1, source_target_pairs={{0,16},{16,0},{1,17},{17,1},{2,18},{18,2},{3,19},{19,3},{4,20},{20... | collective-permute-start | bytes 2359304 | tf_op jit(solution)/shard_map/ppermute | solution.py:1027
  554.9 42.8 %collective-permute-start.44 = (bf16[2,1,1,192,1536]{4,3,1,0,2:T(8,128)(2,1)}, bf16[2,1,1,192,1536]{4,3,1,0,2:T(8,128)(2,1)}, u32[]{:S(2)}, u32[]{:S(2)}) collective-permute-start(bf16[2,1,1,192,1536]{4,3,1,0,2:T(8,128)(2,1)} %get-tuple-element.365), channel_id=1, source_target_pairs={{0,8},{4,12},{8,0},{12,4},{1,9},{5,13},{9,1},{13,5},{2,10},{6,14},... | collective-permute-start | bytes 3538952 | tf_op jit(solution)/shard_map/ppermute | solution.py:1027
  575.2 22.5 %collective-permute-start.43 = (f32[1,1,1,8,1536]{4,3,2,1,0:T(8,128)S(1)}, f32[1,1,1,8,1536]{4,3,2,1,0:T(8,128)S(1)}, u32[]{:S(2)}, u32[]{:S(2)}) collective-permute-start(f32[1,1,1,8,1536]{4,3,2,1,0:T(8,128)S(1)} %add.438), channel_id=1, source_target_pairs={{0,2},{1,3},{2,0},{3,1},{4,6},{5,7},{6,4},{7,5},{8,10},{9,11},{10,... | collective-permute-start | bytes 147464 | tf_op jit(solution)/shard_map/ppermute | solution.py:1027
  637.4 26.3 %collective-permute-start.53 = (bf16[256,1536]{1,0:T(8,128)(2,1)}, bf16[256,1536]{1,0:T(8,128)(2,1)S(1)}, u32[]{:S(2)}, u32[]{:S(2)}) collective-permute-start(bf16[256,1536]{1,0:T(8,128)(2,1)} %add_convert_fusion.1), channel_id=1, source_target_pairs={{0,3},{1,0},{2,1},{3,2},{4,7},{5,4},{6,5},{7,6},{8,11},{9,8},{10,9... | collective-permute-start | bytes 2359304 | tf_op jit(solution)/shard_map/ppermute | solution.py:1022
  644.1 25.8 %all-to-all-start.3 = ((bf16[4,1,1,1,192,384]{5,4,3,2,1,0:T(8,128)(2,1)}), bf16[4,1,1,1,192,384]{5,4,3,2,1,0:T(8,128)(2,1)}, u32[]{:S(2)}, u32[]{:S(2)}) async-start(bf16[4,1,1,1,192,384]{5,4,3,2,1,0:T(8,128)(2,1)} %pad_maximum_fusion.2), calls=%async_computation.4 | async-start | bytes 1179648 | tf_op jit(solution)/shard_map/all_to_all | solution.py:1373
  (97 other events, 1047.9 us)
Sparse Core Ops, SparseCore 0:
  9.9 30.0 all-gather.3
  42.9 85.5 all-gather.5
  176.2 110.7 all-gather.7
  291.4 152.4 reduce-scatter.1
